TPU v7x, 32 devices: a whole 2x2x4 slice. The times are simulated.
32 devices in a mesh: groups: 2 (over x), replica: 8 (over z, y), tensor: 2 (over core).
Axes of the slice: x: 2, y: 2, z: 4, core: 2. Of those that a mesh axis runs over, the one named last changes fastest.
Arguments:
- tokens: bfloat16 [12288, 4096], P(('groups', 'replica'), 'tensor'), parts along dimension 0, may hold values from -6 to 6
- query_matrix: bfloat16 [4096, 4096], P('replica', 'tensor'), may hold values from -0.09375 to 0.09375
- adapter_down_weight: bfloat16 [128, 4096, 64], P(('groups', 'replica'), 'tensor'), parts along dimension 0, may hold values from -0.09375 to 0.09375
- adapter_up_weight: bfloat16 [128, 64, 4096], P(('groups', 'replica'), None, 'tensor'), parts along dimension 0, may hold values from -0.75 to 0.75
- block_adapter_ids: int32 [96], P(('groups', 'replica')), parts along dimension 0, may hold values from 0 to 63, as said below
- block_live_rows: int32 [96], P(('groups', 'replica')), parts along dimension 0, may hold values from 1 to 128, as said below
Outputs:
- queries: bfloat16 [12288, 4096], P(('groups', 'replica'), 'tensor'), parts along dimension 0
There are 2 independent parts, one for each index of `groups`. A program takes and returns all parts, laid end to end along the dimension named above; an argument that names none is the same for every part. Nothing has to cross between parts.
Inputs may be any that keep to these rules, and one draw needn't show every extreme that they name: `block_adapter_ids`: adapter a is owned by replica index a // 8. A block on replica index r uses an adapter owned by index r - 1, r or r + 1 (modulo the replica axis), and every replica index has at least one block of each neighbour's adapters. `block_live_rows`: every replica index has at least one full block.
All inputs are finite; a program needn't handle non-finite values.
Results may differ from a plain program's by a relative error of at most 0.0047.
Values may be sent and summed in bfloat16 or wider, within the bound.
No kernel may reach another device: no remote copies, remote signals or barrier semaphores. Data moves between devices by JAX's collectives and lax.ppermute only.
A program may use at most 128 MiB of HBM per device.

v0:
```python
import jax
import jax.numpy as jnp
from jax import lax
from jax.sharding import PartitionSpec as P

adapter_scale = 2.0


def with_halo(block, sides, width):
    for axis, dim in sides:
        count = lax.axis_size(axis)
        forward = [(i, i + 1) for i in range(count - 1)]
        forward.append((count - 1, 0))
        backward = [(target, source) for source, target in forward]
        low = lax.ppermute(
            lax.slice_in_dim(block, block.shape[dim] - width, None, axis=dim), axis, forward
        )
        high = lax.ppermute(lax.slice_in_dim(block, 0, width, axis=dim), axis, backward)
        block = jnp.concatenate([low, block, high], axis=dim)
    return block


def local(
    tokens, query_matrix, adapter_down_weight, adapter_up_weight, block_adapter_ids, block_live_rows
):
    token_rows = tokens.shape[0]
    feat_half = tokens.shape[1]
    block_count = block_adapter_ids.shape[0]
    block_len = token_rows // block_count
    local_adapters = adapter_down_weight.shape[0]
    rank_columns = adapter_down_weight.shape[2]
    all_feats = lax.all_gather(tokens, "tensor", axis=1, tiled=True)
    base_output = jnp.dot(
        all_feats,
        lax.all_gather(query_matrix, "replica", axis=0, tiled=True),
        preferred_element_type=jnp.float32,
    )
    position = lax.axis_index("replica")
    cycle_size = lax.axis_size("replica")
    owner_dev = block_adapter_ids // local_adapters
    distance = (owner_dev - position) % cycle_size
    which_side = jnp.where(distance == cycle_size - 1, 0, jnp.where(distance == 0, 1, 2))
    slot_local = block_adapter_ids % local_adapters
    stacked_blocks = jnp.stack(
        [
            adapter_down_weight.reshape(local_adapters, -1),
            adapter_up_weight.reshape(local_adapters, -1),
        ]
    )
    widened = with_halo(stacked_blocks, (("replica", 1),), local_adapters)
    picked = jnp.take(widened, which_side * local_adapters + slot_local, axis=1)
    down_blocks = picked[0].reshape(block_count, feat_half, rank_columns)
    up_weight_blocks = picked[1].reshape(block_count, rank_columns, -1)
    token_block_list = tokens.reshape(block_count, block_len, feat_half)
    partial_low = jnp.einsum(
        "bnd,bdr->bnr", token_block_list, down_blocks, preferred_element_type=jnp.float32
    )
    low_rank_state = lax.psum(partial_low, "tensor").astype(jnp.bfloat16)
    adapter_delta = jnp.einsum(
        "uzp,upy->uzy", low_rank_state, up_weight_blocks, preferred_element_type=jnp.float32
    )
    adapter_delta = adapter_delta.reshape(token_rows, -1)
    live_row_count = (jnp.arange(block_len)[None, :] < block_live_rows[:, None]).reshape(
        token_rows, 1
    )
    return jnp.where(live_row_count, base_output + adapter_scale * adapter_delta, 0.0).astype(
        jnp.bfloat16
    )


def solution(mesh):
    in_specs = (
        P(("groups", "replica"), "tensor"),
        P("replica", "tensor"),
        P(("groups", "replica"), "tensor", None),
        P(("groups", "replica"), None, "tensor"),
        P(("groups", "replica")),
        P(("groups", "replica")),
    )
    out_specs = P(("groups", "replica"), "tensor")
    return jax.shard_map(local, mesh=mesh, in_specs=in_specs, out_specs=out_specs, check_vma=False)
```

profile of v0, /device:TPU:0, one launch (start us, length us, event | category | flops | bytes accessed | tf_op | source)
XLA Modules:
  0.0 409.2 jit_solution(13642499741222154211)
XLA Ops:
  6.5 0.0 all-gather.3.cloned.1.call-start
  6.5 0.7 all-gather.3.cloned.1.call-update
  7.3 0.0 all-gather.5.cloned.1.call-start
  7.3 0.8 copy-done.1
  8.1 3.2 copy.9
  11.3 0.0 copy-start.2
  11.3 7.7 %stack_reshape.8 = bf16[1,8,131072]{2,0,1:T(2,128)(2,1)} reshape(bf16[8,2048,64]{2,1,0:T(8,128)(2,1)} %copy.9) | data formatting | bytes 4194304 | tf_op jit(solution)/shard_map/stack;reshape | solution.py:44
  19.0 0.0 copy-done.2
  19.0 5.2 %stack_reshape.9 = bf16[1,8,131072]{2,0,1:T(2,128)(2,1)} reshape(bf16[8,64,2048]{2,1,0:T(8,128)(2,1)S(1)} %copy-done.2) | data formatting | bytes 4194304 | tf_op jit(solution)/shard_map/stack;reshape | solution.py:44
  24.3 11.1 %pad_maximum_fusion.1 = bf16[2,8,131072]{2,0,1:T(2,128)(2,1)} fusion(bf16[1,8,131072]{2,0,1:T(2,128)(2,1)} %stack_reshape.9, bf16[1,8,131072]{2,0,1:T(2,128)(2,1)} %stack_reshape.8), kind=kLoop, calls=%fused_computation.7 | loop fusion | flops 8388608 | bytes 8388608 | tf_op jit(solution)/shard_map/stack | solution.py:44
  35.3 2.8 collective-permute-start
  38.1 3.1 collective-permute-start.1
  41.2 0.0 all-gather.5.cloned.1.call-update
  41.3 0.0 copy-done.3
  41.3 0.0 copy-done.4
  41.3 0.1 fusion.5
  41.4 226.6 %collective-permute-done = bf16[2,8,131072]{2,0,1:T(2,128)(2,1)} collective-permute-done((bf16[2,8,131072]{2,0,1:T(2,128)(2,1)}, bf16[2,8,131072]{2,0,1:T(2,128)(2,1)}, u32[]{:S(2)}, u32[]{:S(2)}) %collective-permute-start) | collective-permute-done | bytes 4194336 | tf_op jit(solution)/shard_map/ppermute | solution.py:15
  268.0 2.6 collective-permute-done.1
  270.6 23.3 %pad_maximum_fusion = bf16[2,24,131072]{2,0,1:T(2,128)(2,1)S(1)} fusion(bf16[2,8,131072]{2,0,1:T(2,128)(2,1)} %collective-permute-done.1, bf16[1,8,131072]{2,0,1:T(2,128)(2,1)} %stack_reshape.9, bf16[1,8,131072]{2,0,1:T(2,128)(2,1)} %stack_reshape.8, bf16[2,8,131072]{2,0,1:T(2,128)(2,1)} %collective-permute-done), kind=kLoop, calls=%fused_computation.2 | loop fusion | flops 50331648 | bytes 25165824 | tf_op jit(solution)/shard_map/concatenate | solution.py:19
  293.8 9.9 %fusion.9 = (bf16[2,24,65536]{2,0,1:T(2,128)(2,1)}, bf16[2,24,65536]{2,0,1:T(2,128)(2,1)}) fusion(bf16[2,24,131072]{2,0,1:T(2,128)(2,1)S(1)} %pad_maximum_fusion), kind=kLoop, calls=%fused_computation.33 | loop fusion | bytes 25165824 | tf_op jit(solution)/shard_map/jit(_take)/gather | solution.py:51
  303.8 7.7 %gather_fusion = bf16[6,2,65536]{2,1,0:T(2,128)(2,1)S(1)} fusion(bf16[2,24,65536]{2,0,1:T(2,128)(2,1)} %get-tuple-element.9, s32[1024]{0:T(1024)S(1)} %pad_clamp_fusion), kind=kCustom, calls=%fused_computation | custom fusion | bytes 3145752 | tf_op jit(solution)/shard_map/jit(_take)/gather | solution.py:51
  311.5 7.8 %gather_fusion.1 = bf16[6,2,65536]{2,1,0:T(2,128)(2,1)S(1)} fusion(bf16[2,24,65536]{2,0,1:T(2,128)(2,1)} %get-tuple-element.10, s32[1024]{0:T(1024)S(1)} %pad_clamp_fusion), kind=kCustom, calls=%fused_computation.1 | custom fusion | bytes 3145752 | tf_op jit(solution)/shard_map/jit(_take)/gather | solution.py:51
  319.3 3.7 broadcast_select_fusion
  323.0 15.2 %slice_reduce_fusion.1 = (bf16[6,131072]{1,0:T(8,128)(2,1)}, bf16[6,131072]{1,0:T(8,128)(2,1)}) fusion(bf16[2,6,131072]{2,0,1:T(2,128)(2,1)S(1)} %broadcast_select_fusion), kind=kLoop, calls=%fused_computation.10 | loop fusion | bytes 6291456 | tf_op jit(solution)/shard_map/slice | solution.py:52
  338.2 5.2 %reshape.48 = bf16[786432]{0:T(1024)(128)(2,1)} reshape(bf16[6,131072]{1,0:T(8,128)(2,1)} %get-tuple-element.5) | data formatting | bytes 3145728
  343.4 5.1 %reshape_squeeze.6 = bf16[6,2048,64]{2,1,0:T(8,128)(2,1)} reshape(bf16[786432]{0:T(1024)(128)(2,1)} %reshape.48) | data formatting | bytes 3145728 | tf_op jit(solution)/shard_map/reshape;squeeze | solution.py:52
  348.6 0.0 copy-done
  348.6 3.1 convolution_bitcast_fusion
  351.7 4.0 all-reduce.1
  355.7 6.8 %convolution_multiply_fusion = f32[6,128,2048]{2,1,0:T(8,128)} fusion(bf16[1,6,64,2048]{3,1,2,0:T(8,128)(2,1)} %bitcast.25, bf16[6,128,64]{1,2,0:T(8,128)(2,1)S(1)} %all-reduce.1), kind=kOutput, calls=%fused_computation.8 | convolution fusion | flops 202899456 | bytes 7962624 | tf_op jit(solution)/shard_map/uzp,upy->uzy/dot_general | solution.py:59
  362.4 19.4 %all-gather.5.cloned.1.call-done = bf16[4096,2048]{1,0:T(8,128)(2,1)} async-done(((bf16[512,2048]{1,0:T(8,128)(2,1)}), bf16[4096,2048]{1,0:T(8,128)(2,1)}) %all-gather.5.cloned.1.call-update) | async-done | bytes 16777232 | tf_op jit(solution)/shard_map/all_gather | solution.py:35
  381.8 20.5 %fusion.1 = bf16[768,2048]{1,0:T(8,128)(2,1)} fusion(f32[6,128,2048]{2,1,0:T(8,128)} %convolution_multiply_fusion, bf16[768,4096]{1,0:T(8,128)(2,1)} %all-gather.3.cloned.1.call-done, bf16[4096,2048]{1,0:T(8,128)(2,1)} %all-gather.5.cloned.1.call-done, pred[768]{0:T(1024)(128)(4,1)S(1)} %fusion.5), kind=kOutput, calls=%fused_computation.5 | convolution fusion | flops 12889620480 | bytes 32506624 | tf_op jit(solution)/shard_map/dot_general | solution.py:33
  (7 shorter events, 0.0 us)
Async XLA Ops:
  6.5 1.6 copy-start.1
  6.5 355.9 %all-gather.3.cloned.1.call-start = ((), (), s32[]{:S(2)}) async-start(), calls=%async_computation | async-start | bytes 9437184 | tf_op jit(solution)/shard_map/all_gather | solution.py:32
  7.3 374.6 %all-gather.5.cloned.1.call-start = ((), (), s32[]{:S(2)}) async-start(), calls=%async_computation.1 | async-start | bytes 18874368 | tf_op jit(solution)/shard_map/all_gather | solution.py:35
  11.3 7.7 %copy-start.2 = (bf16[8,64,2048]{2,1,0:T(8,128)(2,1)S(1)}, bf16[8,64,2048]{2,1,0:T(8,128)(2,1)}, u32[]{:S(2)}) copy-start(bf16[8,64,2048]{2,1,0:T(8,128)(2,1)} %param.9) | copy-start | bytes 6291460
  24.3 17.0 %copy-start.3 = (s32[6]{0:T(128)S(1)}, s32[6]{0:T(128)}, u32[]{:S(2)}) copy-start(s32[6]{0:T(128)} %param.10) | copy-start | bytes 76
  24.3 17.1 %copy-start.4 = (s32[6]{0:T(128)S(1)}, s32[6]{0:T(128)}, u32[]{:S(2)}) copy-start(s32[6]{0:T(128)} %param.11) | copy-start | bytes 76
  35.3 232.7 %collective-permute-start = (bf16[2,8,131072]{2,0,1:T(2,128)(2,1)}, bf16[2,8,131072]{2,0,1:T(2,128)(2,1)}, u32[]{:S(2)}, u32[]{:S(2)}) collective-permute-start(bf16[2,8,131072]{2,0,1:T(2,128)(2,1)} %pad_maximum_fusion.1), channel_id=1, source_target_pairs={{0,2},{2,4},{4,6},{6,8},{8,10},{10,12},{12,14},{14,0},{1,3},{3,5},... | collective-permute-start | bytes 12582920 | tf_op jit(solution)/shard_map/ppermute | solution.py:15
  38.1 232.4 %collective-permute-start.1 = (bf16[2,8,131072]{2,0,1:T(2,128)(2,1)}, bf16[2,8,131072]{2,0,1:T(2,128)(2,1)}, u32[]{:S(2)}, u32[]{:S(2)}) collective-permute-start(bf16[2,8,131072]{2,0,1:T(2,128)(2,1)} %pad_maximum_fusion.1), channel_id=1, source_target_pairs={{2,0},{4,2},{6,4},{8,6},{10,8},{12,10},{14,12},{0,14},{3,1},{5,3},... | collective-permute-start | bytes 12582920 | tf_op jit(solution)/shard_map/ppermute | solution.py:18
  338.2 10.3 %copy-start = (bf16[768,2048]{1,0:T(8,128)(2,1)S(1)}, bf16[768,2048]{1,0:T(8,128)(2,1)}, u32[]{:S(2)}) copy-start(bf16[768,2048]{1,0:T(8,128)(2,1)} %param.6) | copy-start | bytes 9437188
Sparse Core Ops, SparseCore 0:
  8.9 19.4 all-gather.2
  41.4 340.4 all-gather.4
where the time goes:
time: 410 us; the launch traced here: 409 us
  waiting for transfers between devices  249 us (61%)
  local copies, waits for them, and re-layouts  68 us (17%)
  other arithmetic  38.1 us (9%)
  matrix products  30.4 us (7%)
  between operations  13.5 us (3%)
  starting transfers between devices  5.95 us (1%)
    ppermute x1, waiting for transfers between devices, with_halo(): lax.ppermute(lax.slice_in_dim(block, block.shape[dim] - width, None, axis...  227 us
    gather x3, local copies, waits for them, and re-layouts, local(): picked = jnp.take(widened, which_side * local_adapters + slot_local, axis=1)  25.4 us
    concatenate x1, other arithmetic, with_halo(): block = jnp.concatenate([low, block, high], axis=dim)  23.3 us
    dot_general x1, matrix products, local(): jnp.dot(all_feats, lax.all_gather(query_matrix, 'replica', axis=0, tiled=...  20.5 us
    all_gather x1, waiting for transfers between devices, local(): lax.all_gather(query_matrix, 'replica', axis=0, tiled=True)  19.4 us
    slice x1, local copies, waits for them, and re-layouts, local(): down_blocks = picked[0].reshape(block_count, feat_half, rank_columns)  15.2 us
    another operation x2, local copies, waits for them, and re-layouts, local(): jnp.stack([adapter_down_weight.reshape(local_adapters, -1), adapter_up_we...  13 us
    another operation x1, other arithmetic, local(): jnp.stack([adapter_down_weight.reshape(local_adapters, -1), adapter_up_we...  11.1 us
  transfers between devices with their start and end apart: 4, of which 3 were waited for; matrix products, arithmetic and copies ran while one was open for 28% of the time, Pallas kernels for 0%

commit v1 on v0

v1 whole, which is shorter than its diff:
```python
import functools

import jax
import jax.numpy as jnp
import numpy as np
from jax import lax
from jax.experimental import pallas as pl
from jax.experimental.pallas import tpu as pltpu
from jax.sharding import PartitionSpec as P

ADAPTER_SCALE = 2.0
F32 = jnp.float32
VMEM_LIMIT = 48 * 1024 * 1024


def routes(count):
    planes = count // 2
    ring = [2 * z for z in range(planes)] + [2 * z + 1 for z in reversed(range(planes))]
    ahead = [(ring[p], ring[(p + 1) % count]) for p in range(count)]
    back = [(b, a) for a, b in ahead]
    across = [(i, i ^ 1) for i in range(count)]
    diagonal = [(i, (i + 1 if i % 2 else i - 1) % count) for i in range(count)]
    lift = [(i, (i + 2 if i % 2 else i - 2) % count) for i in range(count)]
    return ring, ahead, back, across, diagonal, lift


def params(count):
    return pltpu.CompilerParams(
        dimension_semantics=("arbitrary",) * count, vmem_limit_bytes=VMEM_LIMIT
    )


def pick(index, down_t, up):
    count = index.shape[0]
    block = (1,) + down_t.shape[1:]
    spec = pl.BlockSpec(block, lambda i, at: (at[i], 0, 0))
    out = pl.BlockSpec(block, lambda i, at: (i, 0, 0))

    def body(at, a, b, c, d):
        c[...] = a[...]
        d[...] = b[...]

    shape = jax.ShapeDtypeStruct((count,) + down_t.shape[1:], down_t.dtype)
    size = count * int(np.prod(block)) * 8
    return pl.pallas_call(
        body,
        grid_spec=pltpu.PrefetchScalarGridSpec(
            num_scalar_prefetch=1, grid=(count,), in_specs=[spec, spec], out_specs=[out, out]
        ),
        out_shape=[shape, shape],
        compiler_params=params(1),
        cost_estimate=pl.CostEstimate(flops=0, bytes_accessed=size, transcendentals=0),
    )(index, down_t, up)


def pick_two(which, first, second, a, b):
    count = which.shape[0]
    block = (1,) + a.shape[1:]

    def body(which_ref, first_ref, second_ref, a_ref, b_ref, out_ref):
        side = which_ref[pl.program_id(0)]

        @pl.when(side == 0)
        def _():
            out_ref[...] = a_ref[...]

        @pl.when(side != 0)
        def _():
            out_ref[...] = b_ref[...]

    return pl.pallas_call(
        body,
        grid_spec=pltpu.PrefetchScalarGridSpec(
            num_scalar_prefetch=3,
            grid=(count,),
            in_specs=[
                pl.BlockSpec(block, lambda i, w, f, s: (f[i], 0, 0)),
                pl.BlockSpec(block, lambda i, w, f, s: (s[i], 0, 0)),
            ],
            out_specs=pl.BlockSpec(block, lambda i, w, f, s: (i, 0, 0)),
        ),
        out_shape=jax.ShapeDtypeStruct((count,) + a.shape[1:], a.dtype),
        compiler_params=params(1),
        cost_estimate=pl.CostEstimate(
            flops=0, bytes_accessed=count * int(np.prod(block)) * 6, transcendentals=0
        ),
    )(which, first, second, a, b)


def choose_specs(shape, prefetched):
    block = (1,) + shape[1:]
    return [
        pl.BlockSpec(block, lambda i, table, *rest, n=n: (table[n, i], 0, 0)) for n in (1, 2)
    ]


def low_partial(table, tokens, sources):
    blocks = table.shape[1]
    rows, width = tokens.shape[0] // blocks, tokens.shape[1]
    rank = sources[0].shape[1]

    def body(table_ref, x_ref, own_ref, sent_ref, out_ref):
        place = table_ref[0, pl.program_id(0)]
        for n, ref in enumerate((own_ref, sent_ref)):

            @pl.when(place == n)
            def _(ref=ref):
                out_ref[...] = lax.dot_general(
                    x_ref[...], ref[0], (((1,), (1,)), ((), ())), preferred_element_type=F32
                )

    return pl.pallas_call(
        body,
        grid_spec=pltpu.PrefetchScalarGridSpec(
            num_scalar_prefetch=1,
            grid=(blocks,),
            in_specs=[pl.BlockSpec((rows, width), lambda i, s: (i, 0))]
            + choose_specs(sources[0].shape, 1),
            out_specs=pl.BlockSpec((rows, rank), lambda i, s: (i, 0)),
        ),
        out_shape=jax.ShapeDtypeStruct((tokens.shape[0], rank), F32),
        compiler_params=params(1),
        cost_estimate=pl.CostEstimate(
            flops=2 * tokens.shape[0] * width * rank,
            bytes_accessed=tokens.size * 2 + 8 * rank * width * 2,
            transcendentals=0,
        ),
    )(table, tokens, *sources)


def product(tokens, shards, pieces, out_type):
    rows, width = tokens.shape
    columns = pieces[0].shape[1]
    tile = 256 if rows % 256 == 0 else rows
    count = len(pieces)

    def body(at, x_ref, *refs):
        total = None
        depth = pieces[0].shape[0]
        for k in range(count):
            x = x_ref[:, pl.ds(pl.multiple_of(at[k], depth), depth)]
            if k == count - 2:
                x = x[:, : depth // 2]
            if k == count - 1:
                x = x[:, depth // 2 :]
            term = jnp.dot(x, refs[k][...], preferred_element_type=F32)
            total = term if total is None else total + term
        refs[count][...] = total.astype(out_type)

    return pl.pallas_call(
        body,
        grid_spec=pltpu.PrefetchScalarGridSpec(
            num_scalar_prefetch=1,
            grid=(rows // tile,),
            in_specs=[pl.BlockSpec((tile, width), lambda i, at: (i, 0))]
            + [pl.BlockSpec(p.shape, lambda i, at: (0, 0)) for p in pieces],
            out_specs=pl.BlockSpec((tile, columns), lambda i, at: (i, 0)),
        ),
        out_shape=jax.ShapeDtypeStruct((rows, columns), out_type),
        compiler_params=params(1),
        cost_estimate=pl.CostEstimate(
            flops=2 * rows * width * columns,
            bytes_accessed=(rows * width + width * columns + 2 * rows * columns) * 2,
            transcendentals=0,
        ),
    )(shards, tokens, *pieces)


def finish(table, live, half, low_a, low_b, mine, theirs, sources):
    blocks = table.shape[1]
    rows = mine[0].shape[0] // blocks
    widths = [m.shape[1] for m in mine]
    part = sum(widths)
    rank = sources[0].shape[1]
    chunks = len(mine)

    def body(table_ref, live_ref, half_ref, la, lb, *refs):
        out_ref = refs[-1]
        block = pl.program_id(0)
        place = table_ref[0, block]
        low = (la[...] + lb[...]).astype(jnp.bfloat16)

        def write(source, left, right):
            start = 0
            for ref in tuple(left) + tuple(right):
                width = ref.shape[1]
                delta = jnp.dot(
                    low, source[0, :, start : start + width], preferred_element_type=F32
                )
                total = ref[...].astype(F32) + ADAPTER_SCALE * delta
                alive = lax.broadcasted_iota(jnp.int32, (rows, width), 0) < live_ref[block]
                out_ref[:, start : start + width] = jnp.where(alive, total, 0.0).astype(
                    out_ref.dtype
                )
                start += width

        mine_refs, theirs_refs = refs[:chunks], refs[chunks : 2 * chunks]
        for n in range(2):
            for side in range(2):

                @pl.when(jnp.logical_and(place == n, half_ref[0] == side))
                def _(n=n, side=side):
                    if side == 0:
                        write(refs[2 * chunks + n], mine_refs, theirs_refs)
                    else:
                        write(refs[2 * chunks + n], theirs_refs, mine_refs)

    row = lambda width: pl.BlockSpec((rows, width), lambda i, s, l, h: (i, 0))
    return pl.pallas_call(
        body,
        grid_spec=pltpu.PrefetchScalarGridSpec(
            num_scalar_prefetch=3,
            grid=(blocks,),
            in_specs=[row(rank), row(rank)]
            + [row(w) for w in widths + widths]
            + choose_specs(sources[0].shape, 3),
            out_specs=row(2 * part),
        ),
        out_shape=jax.ShapeDtypeStruct((rows * blocks, 2 * part), jnp.bfloat16),
        compiler_params=params(1),
        cost_estimate=pl.CostEstimate(
            flops=4 * rows * blocks * part * rank,
            bytes_accessed=rows * blocks * part * 10 + 8 * rank * part * 4,
            transcendentals=0,
        ),
    )(table, live, half, low_a, low_b, *mine, *theirs, *sources)


def ranks(ids, owner_of, owner):
    hit = owner_of == owner
    return hit, jnp.cumsum(hit.astype(jnp.int32)) - hit.astype(jnp.int32)


def slots(ids, per_device, owner, count):
    hit, place = ranks(ids, ids // per_device, owner)
    at = jnp.arange(count)[:, None]
    chosen = jnp.logical_and(hit[None, :], place[None, :] == at)
    return jnp.sum(jnp.where(chosen, (ids % per_device)[None, :], 0), axis=1).astype(jnp.int32)


def local(groups, count, tokens, query_matrix, down, up, ids, live):
    ring, ahead, back, across, diagonal, lift = routes(count)
    rep = lambda a, route: lax.ppermute(a, "replica", route)
    partner = lambda a: lax.ppermute(a, "groups", [(i, i ^ 1) for i in range(groups)])
    other_core = lambda a: lax.ppermute(a, "tensor", [(0, 1), (1, 0)])

    depth, out_half = query_matrix.shape
    quarter = out_half // 2
    blocks = ids.shape[0]
    per_device = down.shape[0]
    most = blocks - 1
    half = (lax.axis_index("groups") % 2).astype(jnp.int32)
    me = lax.axis_index("replica").astype(jnp.int32)
    core = lax.axis_index("tensor")

    place = np.argsort(ring)
    offsets = np.zeros((count, count + 1), np.int32)
    for r in range(count):
        for step in range(1, count // 2 + 1):
            offsets[r, 2 * step - 1] = ring[(place[r] - step) % count] * depth
            offsets[r, 2 * step] = ring[(place[r] + step) % count] * depth
        offsets[r, 0] = r * depth
    shards = lax.dynamic_index_in_dim(jnp.asarray(offsets), me, 0, keepdims=False)

    def circulate(start, width):
        own = lax.dynamic_slice(query_matrix, (0, half * quarter + start), (depth, width))
        pieces = [own]
        low_side = high_side = own
        for step in range(1, count // 2 + 1):
            if step == count // 2:
                low_side, high_side = low_side[: depth // 2], high_side[depth // 2 :]
            low_side = rep(low_side, ahead)
            high_side = rep(high_side, back)
            pieces += [low_side, high_side]
        return pieces

    their_tokens = partner(tokens)

    def widen(part):
        swapped = other_core(part)
        return jnp.where(
            core == 0,
            jnp.concatenate([part, swapped], axis=1),
            jnp.concatenate([swapped, part], axis=1),
        )

    ids_across = rep(ids, across)
    ids_diagonal = rep(ids, diagonal)
    down_t = jnp.swapaxes(down, 1, 2)
    sent = pick(slots(ids_diagonal, per_device, me, most), down_t, up)
    feeder = jnp.where(me % 2 == 1, me - 2, me + 2) % count
    across_owner = ids_across // per_device
    _, feeder_place = ranks(ids_across, across_owner, feeder)
    from_feeder = (across_owner == feeder).astype(jnp.int32)
    own_at = jnp.where(across_owner == me, ids_across % per_device, 0).astype(jnp.int32)
    feeder_at = jnp.where(from_feeder == 1, jnp.minimum(feeder_place, most - 1), 0).astype(jnp.int32)
    foreign = (ids // per_device != me).astype(jnp.int32)
    table = jnp.stack(
        [
            foreign,
            jnp.where(foreign == 0, ids % per_device, 0).astype(jnp.int32),
            jnp.where(foreign == 1, jnp.arange(blocks, dtype=jnp.int32), 0),
        ]
    )

    def deliver(kind, owned):
        lifted = rep(sent[kind], lift)
        return [owned, rep(pick_two(from_feeder, own_at, feeder_at, owned, lifted), across)]

    downs = deliver(0, down_t)
    ups = deliver(1, up)
    low = low_partial(table, tokens, downs)
    low_other = other_core(low)

    my_rows, their_rows = widen(tokens), widen(their_tokens)
    mine, theirs, start = [], [], 0
    for width in (quarter // 2, quarter // 4, quarter // 4):
        pieces = circulate(start, width)
        theirs.append(partner(product(their_rows, shards, pieces, jnp.bfloat16)))
        mine.append(product(my_rows, shards, pieces, F32))
        start += width
    return finish(table, live, half.reshape(1), low, low_other, mine, theirs, ups)


def solution(mesh):
    in_specs = (
        P(("groups", "replica"), "tensor"),
        P("replica", "tensor"),
        P(("groups", "replica"), "tensor", None),
        P(("groups", "replica"), None, "tensor"),
        P(("groups", "replica")),
        P(("groups", "replica")),
    )
    out_specs = P(("groups", "replica"), "tensor")
    body = functools.partial(local, mesh.shape["groups"], mesh.shape["replica"])
    return jax.shard_map(body, mesh=mesh, in_specs=in_specs, out_specs=out_specs, check_vma=False)
```

time: 410 us -> 279 us (0.68)
  waiting for transfers between devices: 249 us -> 123 us
  Pallas kernels: 0 us -> 59.6 us
  starting transfers between devices: 5.95 us -> 65.5 us
  local copies, waits for them, and re-layouts: 68 us -> 10.7 us
  matrix products: 30.4 us -> 0 us
  other arithmetic: 38.1 us -> 19 us
  between operations: 13.5 us -> 0.35 us
    ppermute x2 -> x37, waiting for transfers between devices: 229 us -> 123 us  [the longest x30 117 us: local(): rep = lambda a, route: lax.ppermute(a, 'replica', route)]
    pallas_call x0 -> x11, Pallas kernels: none -> 59.6 us  [the longest x6 34.8 us: product(): pl.pallas_call(body, grid_spec=pltpu.PrefetchScalarGridSpec(num_scalar_pr...]
    ppermute x2 -> x37, starting transfers between devices: 5.91 us -> 65.5 us  [the longest x30 60 us: local(): rep = lambda a, route: lax.ppermute(a, 'replica', route)]
    dot_general x3 -> x0, matrix products: 30.4 us -> none  [the longest x1 20.5 us: local(): jnp.dot(all_feats, lax.all_gather(query_matrix, 'replica', axis=0, tiled=...]
    gather x3 -> x0, local copies, waits for them, and re-layouts: 25.4 us -> none  [local(): picked = jnp.take(widened, which_side * local_adapters + slot_local, axis=1)]
    concatenate x1 -> x0, other arithmetic: 23.3 us -> none  [with_halo(): block = jnp.concatenate([low, block, high], axis=dim)]
    all_gather x2 -> x0, waiting for transfers between devices: 19.4 us -> none  [the longest x1 19.4 us: local(): lax.all_gather(query_matrix, 'replica', axis=0, tiled=True)]
    another operation x3 -> x0, local copies, waits for them, and re-layouts: 18.1 us -> none  [the longest x2 13 us: local(): jnp.stack([adapter_down_weight.reshape(local_adapters, -1), adapter_up_we...]
  transfers between devices with their start and end apart: 4 -> 37, of which waited for: 3 -> 13; matrix products, arithmetic and copies ran while one was open for 28% -> 9% of each run, Pallas kernels for 0% -> 19%
where the time goes in v1:
time: 279 us
  waiting for transfers between devices  123 us (44%)
  starting transfers between devices  65.5 us (23%)
  Pallas kernels  59.6 us (21%)
  other arithmetic  19 us (7%)
  local copies, waits for them, and re-layouts  10.7 us (4%)
    ppermute x30, waiting for transfers between devices, local(): rep = lambda a, route: lax.ppermute(a, 'replica', route)  117 us
    ppermute x30, starting transfers between devices, local(): rep = lambda a, route: lax.ppermute(a, 'replica', route)  60 us
    pallas_call x6, Pallas kernels, product(): pl.pallas_call(body, grid_spec=pltpu.PrefetchScalarGridSpec(num_scalar_pr...  34.8 us
    select_n x2, other arithmetic, widen(): jnp.where(core == 0, jnp.concatenate([part, swapped], axis=1), jnp.concat...  18.4 us
    pallas_call x2, Pallas kernels, pick_two(): pl.pallas_call(body, grid_spec=pltpu.PrefetchScalarGridSpec(num_scalar_pr...  9 us
    pallas_call x1, Pallas kernels, finish(): pl.pallas_call(body, grid_spec=pltpu.PrefetchScalarGridSpec(num_scalar_pr...  6.39 us
    ppermute x4, waiting for transfers between devices, local(): lax.ppermute(a, 'groups', [(i, i ^ 1) for i in range(groups)])  6.04 us
  transfers between devices with their start and end apart: 37, of which 13 were waited for; matrix products, arithmetic and copies ran while one was open for 9% of the time, Pallas kernels for 19%

profile of v1, /device:TPU:0, one launch (start us, length us, event | category | flops | bytes accessed | tf_op | source)
XLA Modules:
  0.0 278.6 jit_solution(2793470223403562640)
XLA Ops:
  0.0 2.9 %collective-permute-start.30 = (bf16[768,2048]{1,0:T(8,128)(2,1)}, bf16[768,2048]{1,0:T(8,128)(2,1)}, u32[]{:S(2)}, u32[]{:S(2)}) collective-permute-start(bf16[768,2048]{1,0:T(8,128)(2,1)} %x_ref.1), channel_id=1, source_target_pairs={{0,16},{16,0},{1,17},{17,1},{2,18},{18,2},{3,19},{19,3},{4,20},{20... | collective-permute-start | bytes 9437192 | tf_op jit(solution)/shard_map/ppermute | solution.py:244
  7.6 3.5 %collective-permute-start.1 = (s32[6]{0:T(128)}, s32[6]{0:T(128)S(1)}, u32[]{:S(2)}, u32[]{:S(2)}) collective-permute-start(s32[6]{0:T(128)} %param.11), channel_id=1, source_target_pairs={{0,14},{2,4},{4,2},{6,8},{8,6},{10,12},{12,10},{14,0},{1,15},{3,5}... | collective-permute-start | bytes 80 | tf_op jit(solution)/shard_map/ppermute | solution.py:243
  12.2 2.6 collective-permute-done.1
  19.1 5.1 %collective-permute-done.22.refs_1_ = bf16[512,256]{1,0:T(8,128)(2,1)} collective-permute-done((bf16[512,256]{1,0:T(8,128)(2,1)S(1)}, bf16[512,256]{1,0:T(8,128)(2,1)}, u32[]{:S(2)}, u32[]{:S(2)}) %collective-permute-start.22) | collective-permute-done | bytes 262176 | tf_op jit(solution)/shard_map/ppermute | solution.py:243
  24.2 9.2 %collective-permute-done.23.refs_2_ = bf16[512,256]{1,0:T(8,128)(2,1)} collective-permute-done((bf16[512,256]{1,0:T(8,128)(2,1)S(1)}, bf16[512,256]{1,0:T(8,128)(2,1)}, u32[]{:S(2)}, u32[]{:S(2)}) %collective-permute-start.23) | collective-permute-done | bytes 262176 | tf_op jit(solution)/shard_map/ppermute | solution.py:243
  35.1 4.2 %shard_map.73 = (bf16[5,64,2048]{2,1,0:T(8,128)(2,1)}, bf16[5,64,2048]{2,1,0:T(8,128)(2,1)S(1)}) custom-call(s32[5]{0:T(128)S(1)} %select_reduce_fusion.at, bf16[8,64,2048]{2,1,0:T(8,128)(2,1)S(1)} %bitcast.21, bf16[8,64,2048]{2,1,0:T(8,128)(2,1)} %refs_6_.1), custom_call_target="tpu_custom_call" | custom-call | bytes 5242880 | tf_op jit(solution)/shard_map/pallas_call | solution.py:45
  40.4 2.5 collective-permute-start.2
  44.8 32.5 %collective-permute-done.17.refs_4_ = bf16[512,256]{1,0:T(8,128)(2,1)S(1)} collective-permute-done((bf16[512,256]{1,0:T(8,128)(2,1)}, bf16[512,256]{1,0:T(8,128)(2,1)S(1)}, u32[]{:S(2)}, u32[]{:S(2)}) %collective-permute-start.17) | collective-permute-done | bytes 262176 | tf_op jit(solution)/shard_map/ppermute | solution.py:243
  80.7 4.9 %collective-permute-done.25.refs_4_ = bf16[512,256]{1,0:T(8,128)(2,1)} collective-permute-done((bf16[512,256]{1,0:T(8,128)(2,1)}, bf16[512,256]{1,0:T(8,128)(2,1)}, u32[]{:S(2)}, u32[]{:S(2)}) %collective-permute-start.25) | collective-permute-done | bytes 262176 | tf_op jit(solution)/shard_map/ppermute | solution.py:243
  89.0 4.0 %collective-permute-done.19.refs_6_ = bf16[512,256]{1,0:T(8,128)(2,1)} collective-permute-done((bf16[512,256]{1,0:T(8,128)(2,1)}, bf16[512,256]{1,0:T(8,128)(2,1)}, u32[]{:S(2)}, u32[]{:S(2)}) %collective-permute-start.19) | collective-permute-done | bytes 262176 | tf_op jit(solution)/shard_map/ppermute | solution.py:243
  97.0 25.6 %collective-permute-start.8 = (bf16[512,512]{1,0:T(8,128)(2,1)}, bf16[512,512]{1,0:T(8,128)(2,1)}, u32[]{:S(2)}, u32[]{:S(2)}) collective-permute-start(bf16[512,512]{1,0:T(8,128)(2,1)} %copy-done.9), channel_id=1, source_target_pairs={{0,4},{4,8},{8,12},{12,14},{14,10},{10,6},{6,2},{2,0},{1,5},{5,9},... | collective-permute-start | bytes 1572872 | tf_op jit(solution)/shard_map/ppermute | solution.py:243
  122.6 5.1 %shard_map.74 = bf16[6,64,2048]{2,1,0:T(8,128)(2,1)} custom-call(s32[6]{0:T(128)S(1)} %compare_convert_fusion.which_ref, s32[6]{0:T(128)S(1)} %get-tuple-element.11.first_ref, s32[6]{0:T(128)S(1)} %compare_select_fusion.second_ref, bf16[8,64,2048]{2,1,0:T(8,128)(2,1)S(1)} %bitcast.22, bf16[5,64,2048]{2,1,0:T(8,128)(2,1)} %collective-permute-done.2.b_ref), custom_call_target="tpu_custom_call" | custom-call | bytes 4718592 | tf_op jit(solution)/shard_map/pallas_call | solution.py:71
  127.7 2.4 collective-permute-start.3
  130.0 8.9 %collective-permute-done.8.refs_3_ = bf16[512,512]{1,0:T(8,128)(2,1)} collective-permute-done((bf16[512,512]{1,0:T(8,128)(2,1)}, bf16[512,512]{1,0:T(8,128)(2,1)}, u32[]{:S(2)}, u32[]{:S(2)}) %collective-permute-start.8) | collective-permute-done | bytes 524320 | tf_op jit(solution)/shard_map/ppermute | solution.py:243
  139.7 33.7 %collective-permute-done.9.refs_4_ = bf16[512,512]{1,0:T(8,128)(2,1)} collective-permute-done((bf16[512,512]{1,0:T(8,128)(2,1)}, bf16[512,512]{1,0:T(8,128)(2,1)}, u32[]{:S(2)}, u32[]{:S(2)}) %collective-permute-start.9) | collective-permute-done | bytes 524320 | tf_op jit(solution)/shard_map/ppermute | solution.py:243
  173.3 2.5 collective-permute-start.11
  180.2 3.9 %shard_map.82 = bf16[6,64,2048]{2,1,0:T(8,128)(2,1)S(1)} custom-call(s32[6]{0:T(128)S(1)} %compare_convert_fusion.which_ref, s32[6]{0:T(128)S(1)} %get-tuple-element.11.first_ref, s32[6]{0:T(128)S(1)} %compare_select_fusion.second_ref, bf16[8,64,2048]{2,1,0:T(8,128)(2,1)S(1)} %copy-done.2, bf16[5,64,2048]{2,1,0:T(8,128)(2,1)} %collective-permute-done.35.b_ref), custom_call_target="tpu_custom_call" | custom-call | bytes 4718592 | tf_op jit(solution)/shard_map/pallas_call | solution.py:71
  184.1 4.3 %collective-permute-done.10.refs_5_ = bf16[512,512]{1,0:T(8,128)(2,1)S(1)} collective-permute-done((bf16[512,512]{1,0:T(8,128)(2,1)}, bf16[512,512]{1,0:T(8,128)(2,1)S(1)}, u32[]{:S(2)}, u32[]{:S(2)}) %collective-permute-start.10) | collective-permute-done | bytes 524320 | tf_op jit(solution)/shard_map/ppermute | solution.py:243
  188.5 2.1 collective-permute-start.21
  190.6 5.3 %shard_map.75.la = f32[768,64]{1,0:T(8,128)S(1)} custom-call(s32[3,6]{1,0:T(4,128)S(1)} %pad_add_fusion.table_ref, bf16[768,2048]{1,0:T(8,128)(2,1)} %x_ref.1, bf16[8,64,2048]{2,1,0:T(8,128)(2,1)S(1)} %bitcast.23, bf16[6,64,2048]{2,1,0:T(8,128)(2,1)} %collective-permute-done.3.sent_ref), custom_call_target="tpu_custom_call" | custom-call | flops 201326592 | bytes 5242880 | tf_op jit(solution)/shard_map/pallas_call | solution.py:112
  196.0 8.2 %maximum_select_fusion.x_ref = bf16[768,4096]{1,0:T(8,128)(2,1)} fusion(bf16[768,2048]{1,0:T(8,128)(2,1)} %collective-permute-done.5, bf16[768,2048]{1,0:T(8,128)(2,1)S(1)} %copy-done.15, pred[]{:T(512)S(6)} %eq.64), kind=kLoop, calls=%fused_computation | loop fusion | flops 28311552 | bytes 12582913 | tf_op jit(solution)/shard_map/jit(_where)/select_n | solution.py:281
  204.2 2.0 collective-permute-start.13
  206.2 10.2 %maximum_select_fusion.1.x_ref = bf16[768,4096]{1,0:T(8,128)(2,1)} fusion(bf16[768,2048]{1,0:T(8,128)(2,1)} %collective-permute-done.31, bf16[768,2048]{1,0:T(8,128)(2,1)} %collective-permute-done.30, pred[]{:T(512)S(6)} %eq.64), kind=kLoop, calls=%fused_computation.1 | loop fusion | flops 28311552 | bytes 12582913 | tf_op jit(solution)/shard_map/jit(_where)/select_n | solution.py:281
  216.5 10.3 %collective-permute-done.12.refs_7_ = bf16[256,512]{1,0:T(8,128)(2,1)S(1)} collective-permute-done((bf16[256,512]{1,0:T(8,128)(2,1)S(1)}, bf16[256,512]{1,0:T(8,128)(2,1)S(1)}, u32[]{:S(2)}, u32[]{:S(2)}) %collective-permute-start.12) | collective-permute-done | bytes 262176 | tf_op jit(solution)/shard_map/ppermute | solution.py:243
  228.8 6.5 %shard_map.79 = bf16[768,512]{1,0:T(8,128)(2,1)S(1)} custom-call(s32[9]{0:T(128)S(1)} %fusion.1.at, bf16[768,4096]{1,0:T(8,128)(2,1)} %maximum_select_fusion.1.x_ref, bf16[512,512]{1,0:T(8,128)(2,1)S(1)} %constant_dynamic-slice_fusion.2.refs_0_, bf16[512,512]{1,0:T(8,128)(2,1)S(1)} %copy-done.10, bf16[512,512]{1,0:T(8,128)(2,1)S(1)} %copy-done.12, ...), custom_call_target="tpu_custom_call" | custom-call | flops 3221225472 | bytes 12058624 | tf_op jit(solution)/shard_map/pallas_call | solution.py:150
  235.6 5.4 %shard_map.80 = bf16[768,256]{1,0:T(8,128)(2,1)S(1)} custom-call(s32[9]{0:T(128)S(1)} %fusion.1.at, bf16[768,4096]{1,0:T(8,128)(2,1)} %maximum_select_fusion.1.x_ref, bf16[512,256]{1,0:T(8,128)(2,1)S(1)} %get-tuple-element.16.refs_0_, bf16[512,256]{1,0:T(8,128)(2,1)S(1)} %copy-done.4, bf16[512,256]{1,0:T(8,128)(2,1)} %collective-permute-done.15.refs_2_, ...), custom_call_target="tpu_custom_call" | custom-call | flops 1610612736 | bytes 9175040 | tf_op jit(solution)/shard_map/pallas_call | solution.py:150
  242.9 5.5 %shard_map.81 = bf16[768,256]{1,0:T(8,128)(2,1)S(1)} custom-call(s32[9]{0:T(128)S(1)} %fusion.1.at, bf16[768,4096]{1,0:T(8,128)(2,1)} %maximum_select_fusion.1.x_ref, bf16[512,256]{1,0:T(8,128)(2,1)S(1)} %get-tuple-element.15.refs_0_, bf16[512,256]{1,0:T(8,128)(2,1)} %collective-permute-done.22.refs_1_, bf16[512,256]{1,0:T(8,128)(2,1)} %collective-permute-done.23.refs_2_, ...), custom_call_target="tpu_custom_call" | custom-call | flops 1610612736 | bytes 9175040 | tf_op jit(solution)/shard_map/pallas_call | solution.py:150
  248.7 6.5 %shard_map.76.refs_0_ = f32[768,512]{1,0:T(8,128)S(1)} custom-call(s32[9]{0:T(128)S(1)} %fusion.1.at, bf16[768,4096]{1,0:T(8,128)(2,1)} %maximum_select_fusion.x_ref, bf16[512,512]{1,0:T(8,128)(2,1)S(1)} %constant_dynamic-slice_fusion.2.refs_0_, bf16[512,512]{1,0:T(8,128)(2,1)S(1)} %copy-done.10, bf16[512,512]{1,0:T(8,128)(2,1)S(1)} %copy-done.12, ...), custom_call_target="tpu_custom_call" | custom-call | flops 3221225472 | bytes 12058624 | tf_op jit(solution)/shard_map/pallas_call | solution.py:150
  255.2 5.4 %shard_map.77.refs_1_ = f32[768,256]{1,0:T(8,128)S(1)} custom-call(s32[9]{0:T(128)S(1)} %fusion.1.at, bf16[768,4096]{1,0:T(8,128)(2,1)} %maximum_select_fusion.x_ref, bf16[512,256]{1,0:T(8,128)(2,1)S(1)} %get-tuple-element.16.refs_0_, bf16[512,256]{1,0:T(8,128)(2,1)S(1)} %copy-done.4, bf16[512,256]{1,0:T(8,128)(2,1)} %collective-permute-done.15.refs_2_, ...), custom_call_target="tpu_custom_call" | custom-call | flops 1610612736 | bytes 9175040 | tf_op jit(solution)/shard_map/pallas_call | solution.py:150
  260.6 5.5 %shard_map.78.refs_2_ = f32[768,256]{1,0:T(8,128)S(1)} custom-call(s32[9]{0:T(128)S(1)} %fusion.1.at, bf16[768,4096]{1,0:T(8,128)(2,1)} %maximum_select_fusion.x_ref, bf16[512,256]{1,0:T(8,128)(2,1)S(1)} %get-tuple-element.15.refs_0_, bf16[512,256]{1,0:T(8,128)(2,1)} %collective-permute-done.22.refs_1_, bf16[512,256]{1,0:T(8,128)(2,1)} %collective-permute-done.23.refs_2_, ...), custom_call_target="tpu_custom_call" | custom-call | flops 1610612736 | bytes 9175040 | tf_op jit(solution)/shard_map/pallas_call | solution.py:150
  266.1 6.0 %collective-permute-done.34.refs_5_ = bf16[768,256]{1,0:T(8,128)(2,1)S(1)} collective-permute-done((bf16[768,256]{1,0:T(8,128)(2,1)S(1)}, bf16[768,256]{1,0:T(8,128)(2,1)S(1)}, u32[]{:S(2)}, u32[]{:S(2)}) %collective-permute-start.34) | collective-permute-done | bytes 393248 | tf_op jit(solution)/shard_map/ppermute | solution.py:244
  272.2 6.4 %shard_map.83 = bf16[768,2048]{1,0:T(8,128)(2,1)} custom-call(s32[3,6]{1,0:T(4,128)S(1)} %pad_add_fusion.table_ref, s32[6]{0:T(128)S(1)} %copy-done.13, s32[1]{0:T(128)} %bitcast.3.half_ref, f32[768,64]{1,0:T(8,128)S(1)} %shard_map.75.la, f32[768,64]{1,0:T(8,128)S(1)} %collective-permute-done.4.lb, f32[768,512]{1,0:T(8,128)S(1)} %shard_map.76.refs_0_, ...), custom_call_target="tpu_custom_call" | custom-call | flops 201326592 | bytes 9961472 | tf_op jit(solution)/shard_map/pallas_call | solution.py:209
  (111 shorter events, 35.3 us)
Async XLA Ops:
  0.0 80.6 %collective-permute-start.30 = (bf16[768,2048]{1,0:T(8,128)(2,1)}, bf16[768,2048]{1,0:T(8,128)(2,1)}, u32[]{:S(2)}, u32[]{:S(2)}) collective-permute-start(bf16[768,2048]{1,0:T(8,128)(2,1)} %x_ref.1), channel_id=1, source_target_pairs={{0,16},{16,0},{1,17},{17,1},{2,18},{18,2},{3,19},{19,3},{4,20},{20... | collective-permute-start | bytes 9437192 | tf_op jit(solution)/shard_map/ppermute | solution.py:244
  4.0 12.3 %collective-permute-start.14 = (bf16[512,256]{1,0:T(8,128)(2,1)S(1)}, bf16[512,256]{1,0:T(8,128)(2,1)S(1)}, u32[]{:S(2)}, u32[]{:S(2)}) collective-permute-start(bf16[512,256]{1,0:T(8,128)(2,1)S(1)} %get-tuple-element.16.refs_0_), channel_id=1, source_target_pairs={{0,4},{4,8},{8,12},{12,14},{14,10},{10,6},{6,2},{2,0},{1,5},{5,9},... | collective-permute-start | bytes 786440 | tf_op jit(solution)/shard_map/ppermute | solution.py:243
  5.6 11.5 %collective-permute-start.15 = (bf16[512,256]{1,0:T(8,128)(2,1)S(1)}, bf16[512,256]{1,0:T(8,128)(2,1)}, u32[]{:S(2)}, u32[]{:S(2)}) collective-permute-start(bf16[512,256]{1,0:T(8,128)(2,1)S(1)} %get-tuple-element.16.refs_0_), channel_id=1, source_target_pairs={{4,0},{8,4},{12,8},{14,12},{10,14},{6,10},{2,6},{0,2},{5,1},{9,5},... | collective-permute-start | bytes 786440 | tf_op jit(solution)/shard_map/ppermute | solution.py:243
  6.1 8.9 %collective-permute-start = (s32[6]{0:T(128)}, s32[6]{0:T(128)S(1)}, u32[]{:S(2)}, u32[]{:S(2)}) collective-permute-start(s32[6]{0:T(128)} %param.11), channel_id=1, source_target_pairs={{0,2},{2,0},{4,6},{6,4},{8,10},{10,8},{12,14},{14,12},{1,3},{3,1},... | collective-permute-start | bytes 80 | tf_op jit(solution)/shard_map/ppermute | solution.py:243
  14.8 9.4 %collective-permute-start.22 = (bf16[512,256]{1,0:T(8,128)(2,1)S(1)}, bf16[512,256]{1,0:T(8,128)(2,1)}, u32[]{:S(2)}, u32[]{:S(2)}) collective-permute-start(bf16[512,256]{1,0:T(8,128)(2,1)S(1)} %get-tuple-element.15.refs_0_), channel_id=1, source_target_pairs={{0,4},{4,8},{8,12},{12,14},{14,10},{10,6},{6,2},{2,0},{1,5},{5,9},... | collective-permute-start | bytes 786440 | tf_op jit(solution)/shard_map/ppermute | solution.py:243
  15.0 25.4 %collective-permute-start.6 = (bf16[512,512]{1,0:T(8,128)(2,1)S(1)}, bf16[512,512]{1,0:T(8,128)(2,1)S(1)}, u32[]{:S(2)}, u32[]{:S(2)}) collective-permute-start(bf16[512,512]{1,0:T(8,128)(2,1)S(1)} %constant_dynamic-slice_fusion.2.refs_0_), channel_id=1, source_target_pairs={{0,4},{4,8},{8,12},{12,14},{14,10},{10,6},{6,2},{2,0},{1,5},{5,9},... | collective-permute-start | bytes 1572872 | tf_op jit(solution)/shard_map/ppermute | solution.py:243
  16.3 26.5 %collective-permute-start.7 = (bf16[512,512]{1,0:T(8,128)(2,1)S(1)}, bf16[512,512]{1,0:T(8,128)(2,1)S(1)}, u32[]{:S(2)}, u32[]{:S(2)}) collective-permute-start(bf16[512,512]{1,0:T(8,128)(2,1)S(1)} %constant_dynamic-slice_fusion.2.refs_0_), channel_id=1, source_target_pairs={{4,0},{8,4},{12,8},{14,12},{10,14},{6,10},{2,6},{0,2},{5,1},{9,5},... | collective-permute-start | bytes 1572872 | tf_op jit(solution)/shard_map/ppermute | solution.py:243
  17.1 16.2 %collective-permute-start.23 = (bf16[512,256]{1,0:T(8,128)(2,1)S(1)}, bf16[512,256]{1,0:T(8,128)(2,1)}, u32[]{:S(2)}, u32[]{:S(2)}) collective-permute-start(bf16[512,256]{1,0:T(8,128)(2,1)S(1)} %get-tuple-element.15.refs_0_), channel_id=1, source_target_pairs={{4,0},{8,4},{12,8},{14,12},{10,14},{6,10},{2,6},{0,2},{5,1},{9,5},... | collective-permute-start | bytes 786440 | tf_op jit(solution)/shard_map/ppermute | solution.py:243
  24.1 19.3 %collective-permute-start.16 = (bf16[512,256]{1,0:T(8,128)(2,1)S(1)}, bf16[512,256]{1,0:T(8,128)(2,1)}, u32[]{:S(2)}, u32[]{:S(2)}) collective-permute-start(bf16[512,256]{1,0:T(8,128)(2,1)S(1)} %collective-permute-done.14.refs_1_), channel_id=1, source_target_pairs={{0,4},{4,8},{8,12},{12,14},{14,10},{10,6},{6,2},{2,0},{1,5},{5,9},... | collective-permute-start | bytes 786440 | tf_op jit(solution)/shard_map/ppermute | solution.py:243
  33.3 162.6 %collective-permute-start.5 = (bf16[768,2048]{1,0:T(8,128)(2,1)}, bf16[768,2048]{1,0:T(8,128)(2,1)}, u32[]{:S(2)}, u32[]{:S(2)}) collective-permute-start(bf16[768,2048]{1,0:T(8,128)(2,1)} %x_ref.1), channel_id=1, source_target_pairs={{0,1},{1,0},{2,3},{3,2},{4,5},{5,4},{6,7},{7,6},{8,9},{9,8},{10,11... | collective-permute-start | bytes 9437192 | tf_op jit(solution)/shard_map/ppermute | solution.py:245
  40.4 56.6 %collective-permute-start.2 = (bf16[5,64,2048]{2,1,0:T(8,128)(2,1)}, bf16[5,64,2048]{2,1,0:T(8,128)(2,1)}, u32[]{:S(2)}, u32[]{:S(2)}) collective-permute-start(bf16[5,64,2048]{2,1,0:T(8,128)(2,1)} %get-tuple-element.7), channel_id=1, source_target_pairs={{0,12},{2,6},{4,0},{6,10},{8,4},{10,14},{12,8},{14,2},{1,13},{3,7}... | collective-permute-start | bytes 3932168 | tf_op jit(solution)/shard_map/ppermute | solution.py:243
  42.8 34.6 %collective-permute-start.17 = (bf16[512,256]{1,0:T(8,128)(2,1)}, bf16[512,256]{1,0:T(8,128)(2,1)S(1)}, u32[]{:S(2)}, u32[]{:S(2)}) collective-permute-start(bf16[512,256]{1,0:T(8,128)(2,1)} %collective-permute-done.15.refs_2_), channel_id=1, source_target_pairs={{4,0},{8,4},{12,8},{14,12},{10,14},{6,10},{2,6},{0,2},{5,1},{9,5},... | collective-permute-start | bytes 786440 | tf_op jit(solution)/shard_map/ppermute | solution.py:243
  43.4 34.6 %collective-permute-start.24 = (bf16[512,256]{1,0:T(8,128)(2,1)}, bf16[512,256]{1,0:T(8,128)(2,1)S(1)}, u32[]{:S(2)}, u32[]{:S(2)}) collective-permute-start(bf16[512,256]{1,0:T(8,128)(2,1)} %collective-permute-done.22.refs_1_), channel_id=1, source_target_pairs={{0,4},{4,8},{8,12},{12,14},{14,10},{10,6},{6,2},{2,0},{1,5},{5,9},... | collective-permute-start | bytes 786440 | tf_op jit(solution)/shard_map/ppermute | solution.py:243
  80.6 123.6 %collective-permute-start.31 = (bf16[768,2048]{1,0:T(8,128)(2,1)}, bf16[768,2048]{1,0:T(8,128)(2,1)}, u32[]{:S(2)}, u32[]{:S(2)}) collective-permute-start(bf16[768,2048]{1,0:T(8,128)(2,1)} %collective-permute-done.30), channel_id=1, source_target_pairs={{0,1},{1,0},{2,3},{3,2},{4,5},{5,4},{6,7},{7,6},{8,9},{9,8},{10,11... | collective-permute-start | bytes 9437192 | tf_op jit(solution)/shard_map/ppermute | solution.py:245
  93.0 80.3 %collective-permute-start.35 = (bf16[5,64,2048]{2,1,0:T(8,128)(2,1)}, bf16[5,64,2048]{2,1,0:T(8,128)(2,1)}, u32[]{:S(2)}, u32[]{:S(2)}) collective-permute-start(bf16[5,64,2048]{2,1,0:T(8,128)(2,1)} %copy-done.14), channel_id=1, source_target_pairs={{0,12},{2,6},{4,0},{6,10},{8,4},{10,14},{12,8},{14,2},{1,13},{3,7}... | collective-permute-start | bytes 3932168 | tf_op jit(solution)/shard_map/ppermute | solution.py:243
  95.2 32.5 %collective-permute-start.27 = (bf16[512,256]{1,0:T(8,128)(2,1)}, bf16[512,256]{1,0:T(8,128)(2,1)}, u32[]{:S(2)}, u32[]{:S(2)}) collective-permute-start(bf16[512,256]{1,0:T(8,128)(2,1)} %collective-permute-done.25.refs_4_), channel_id=1, source_target_pairs={{4,0},{8,4},{12,8},{14,12},{10,14},{6,10},{2,6},{0,2},{5,1},{9,5},... | collective-permute-start | bytes 786440 | tf_op jit(solution)/shard_map/ppermute | solution.py:243
  97.0 42.0 %collective-permute-start.8 = (bf16[512,512]{1,0:T(8,128)(2,1)}, bf16[512,512]{1,0:T(8,128)(2,1)}, u32[]{:S(2)}, u32[]{:S(2)}) collective-permute-start(bf16[512,512]{1,0:T(8,128)(2,1)} %copy-done.9), channel_id=1, source_target_pairs={{0,4},{4,8},{8,12},{12,14},{14,10},{10,6},{6,2},{2,0},{1,5},{5,9},... | collective-permute-start | bytes 1572872 | tf_op jit(solution)/shard_map/ppermute | solution.py:243
  127.7 62.9 %collective-permute-start.3 = (bf16[6,64,2048]{2,1,0:T(8,128)(2,1)}, bf16[6,64,2048]{2,1,0:T(8,128)(2,1)}, u32[]{:S(2)}, u32[]{:S(2)}) collective-permute-start(bf16[6,64,2048]{2,1,0:T(8,128)(2,1)} %shard_map.74), channel_id=1, source_target_pairs={{0,2},{2,0},{4,6},{6,4},{8,10},{10,8},{12,14},{14,12},{1,3},{3,1},... | collective-permute-start | bytes 4718600 | tf_op jit(solution)/shard_map/ppermute | solution.py:243
  139.0 34.4 %collective-permute-start.9 = (bf16[512,512]{1,0:T(8,128)(2,1)}, bf16[512,512]{1,0:T(8,128)(2,1)}, u32[]{:S(2)}, u32[]{:S(2)}) collective-permute-start(bf16[512,512]{1,0:T(8,128)(2,1)} %copy-done.11), channel_id=1, source_target_pairs={{4,0},{8,4},{12,8},{14,12},{10,14},{6,10},{2,6},{0,2},{5,1},{9,5},... | collective-permute-start | bytes 1572872 | tf_op jit(solution)/shard_map/ppermute | solution.py:243
  173.3 15.1 %collective-permute-start.10 = (bf16[512,512]{1,0:T(8,128)(2,1)}, bf16[512,512]{1,0:T(8,128)(2,1)S(1)}, u32[]{:S(2)}, u32[]{:S(2)}) collective-permute-start(bf16[512,512]{1,0:T(8,128)(2,1)} %collective-permute-done.8.refs_3_), channel_id=1, source_target_pairs={{0,4},{4,8},{8,12},{12,14},{14,10},{10,6},{6,2},{2,0},{1,5},{5,9},... | collective-permute-start | bytes 1572872 | tf_op jit(solution)/shard_map/ppermute | solution.py:243
  173.3 15.1 %collective-permute-start.11 = (bf16[512,512]{1,0:T(8,128)(2,1)}, bf16[512,512]{1,0:T(8,128)(2,1)S(1)}, u32[]{:S(2)}, u32[]{:S(2)}) collective-permute-start(bf16[512,512]{1,0:T(8,128)(2,1)} %collective-permute-done.9.refs_4_), channel_id=1, source_target_pairs={{4,0},{8,4},{12,8},{14,12},{10,14},{6,10},{2,6},{0,2},{5,1},{9,5},... | collective-permute-start | bytes 1572872 | tf_op jit(solution)/shard_map/ppermute | solution.py:243
  188.4 46.9 %collective-permute-start.20 = (bf16[256,256]{1,0:T(8,128)(2,1)S(1)}, bf16[256,256]{1,0:T(8,128)(2,1)S(1)}, u32[]{:S(2)}, u32[]{:S(2)}) collective-permute-start(bf16[256,256]{1,0:T(8,128)(2,1)S(1)} %slice.26), channel_id=1, source_target_pairs={{0,4},{4,8},{8,12},{12,14},{14,10},{10,6},{6,2},{2,0},{1,5},{5,9},... | collective-permute-start | bytes 393224 | tf_op jit(solution)/shard_map/ppermute | solution.py:243
  188.5 46.9 %collective-permute-start.21 = (bf16[256,256]{1,0:T(8,128)(2,1)S(1)}, bf16[256,256]{1,0:T(8,128)(2,1)S(1)}, u32[]{:S(2)}, u32[]{:S(2)}) collective-permute-start(bf16[256,256]{1,0:T(8,128)(2,1)S(1)} %slice.27), channel_id=1, source_target_pairs={{4,0},{8,4},{12,8},{14,12},{10,14},{6,10},{2,6},{0,2},{5,1},{9,5},... | collective-permute-start | bytes 393224 | tf_op jit(solution)/shard_map/ppermute | solution.py:243
  190.6 75.6 %collective-permute-start.36 = (bf16[6,64,2048]{2,1,0:T(8,128)(2,1)S(1)}, bf16[6,64,2048]{2,1,0:T(8,128)(2,1)}, u32[]{:S(2)}, u32[]{:S(2)}) collective-permute-start(bf16[6,64,2048]{2,1,0:T(8,128)(2,1)S(1)} %shard_map.82), channel_id=1, source_target_pairs={{0,2},{2,0},{4,6},{6,4},{8,10},{10,8},{12,14},{14,12},{1,3},{3,1},... | collective-permute-start | bytes 4718600 | tf_op jit(solution)/shard_map/ppermute | solution.py:243
  195.9 30.8 %collective-permute-start.12 = (bf16[256,512]{1,0:T(8,128)(2,1)S(1)}, bf16[256,512]{1,0:T(8,128)(2,1)S(1)}, u32[]{:S(2)}, u32[]{:S(2)}) collective-permute-start(bf16[256,512]{1,0:T(8,128)(2,1)S(1)} %slice.24), channel_id=1, source_target_pairs={{0,4},{4,8},{8,12},{12,14},{14,10},{10,6},{6,2},{2,0},{1,5},{5,9},... | collective-permute-start | bytes 786440 | tf_op jit(solution)/shard_map/ppermute | solution.py:243
  204.2 22.5 %collective-permute-start.13 = (bf16[256,512]{1,0:T(8,128)(2,1)S(1)}, bf16[256,512]{1,0:T(8,128)(2,1)S(1)}, u32[]{:S(2)}, u32[]{:S(2)}) collective-permute-start(bf16[256,512]{1,0:T(8,128)(2,1)S(1)} %slice.25), channel_id=1, source_target_pairs={{4,0},{8,4},{12,8},{14,12},{10,14},{6,10},{2,6},{0,2},{5,1},{9,5},... | collective-permute-start | bytes 786440 | tf_op jit(solution)/shard_map/ppermute | solution.py:243
  226.7 14.2 %collective-permute-start.28 = (bf16[256,256]{1,0:T(8,128)(2,1)S(1)}, bf16[256,256]{1,0:T(8,128)(2,1)S(1)}, u32[]{:S(2)}, u32[]{:S(2)}) collective-permute-start(bf16[256,256]{1,0:T(8,128)(2,1)S(1)} %slice.28), channel_id=1, source_target_pairs={{0,4},{4,8},{8,12},{12,14},{14,10},{10,6},{6,2},{2,0},{1,5},{5,9},... | collective-permute-start | bytes 393224 | tf_op jit(solution)/shard_map/ppermute | solution.py:243
  226.7 16.2 %collective-permute-start.29 = (bf16[256,256]{1,0:T(8,128)(2,1)S(1)}, bf16[256,256]{1,0:T(8,128)(2,1)S(1)}, u32[]{:S(2)}, u32[]{:S(2)}) collective-permute-start(bf16[256,256]{1,0:T(8,128)(2,1)S(1)} %slice.29), channel_id=1, source_target_pairs={{4,0},{8,4},{12,8},{14,12},{10,14},{6,10},{2,6},{0,2},{5,1},{9,5},... | collective-permute-start | bytes 393224 | tf_op jit(solution)/shard_map/ppermute | solution.py:243
  235.3 30.8 %collective-permute-start.4 = (f32[768,64]{1,0:T(8,128)S(1)}, f32[768,64]{1,0:T(8,128)S(1)}, u32[]{:S(2)}, u32[]{:S(2)}) collective-permute-start(f32[768,64]{1,0:T(8,128)S(1)} %shard_map.75.la), channel_id=1, source_target_pairs={{0,1},{1,0},{2,3},{3,2},{4,5},{5,4},{6,7},{7,6},{8,9},{9,8},{10,11... | collective-permute-start | bytes 589832 | tf_op jit(solution)/shard_map/ppermute | solution.py:245
  235.4 36.8 %collective-permute-start.32 = (bf16[768,512]{1,0:T(8,128)(2,1)S(1)}, bf16[768,512]{1,0:T(8,128)(2,1)S(1)}, u32[]{:S(2)}, u32[]{:S(2)}) collective-permute-start(bf16[768,512]{1,0:T(8,128)(2,1)S(1)} %shard_map.79), channel_id=1, source_target_pairs={{0,16},{16,0},{1,17},{17,1},{2,18},{18,2},{3,19},{19,3},{4,20},{20... | collective-permute-start | bytes 2359304 | tf_op jit(solution)/shard_map/ppermute | solution.py:244
  241.0 25.2 %collective-permute-start.33 = (bf16[768,256]{1,0:T(8,128)(2,1)S(1)}, bf16[768,256]{1,0:T(8,128)(2,1)S(1)}, u32[]{:S(2)}, u32[]{:S(2)}) collective-permute-start(bf16[768,256]{1,0:T(8,128)(2,1)S(1)} %shard_map.80), channel_id=1, source_target_pairs={{0,16},{16,0},{1,17},{17,1},{2,18},{18,2},{3,19},{19,3},{4,20},{20... | collective-permute-start | bytes 1179656 | tf_op jit(solution)/shard_map/ppermute | solution.py:244
  248.5 23.7 %collective-permute-start.34 = (bf16[768,256]{1,0:T(8,128)(2,1)S(1)}, bf16[768,256]{1,0:T(8,128)(2,1)S(1)}, u32[]{:S(2)}, u32[]{:S(2)}) collective-permute-start(bf16[768,256]{1,0:T(8,128)(2,1)S(1)} %shard_map.81), channel_id=1, source_target_pairs={{0,16},{16,0},{1,17},{17,1},{2,18},{18,2},{3,19},{19,3},{4,20},{20... | collective-permute-start | bytes 1179656 | tf_op jit(solution)/shard_map/ppermute | solution.py:244
  (22 other events, 608.1 us)

commit v2 on v1

v2 whole, which is shorter than its diff:
```python
import functools

import jax
import jax.numpy as jnp
import numpy as np
from jax import lax
from jax.experimental import pallas as pl
from jax.experimental.pallas import tpu as pltpu
from jax.sharding import PartitionSpec as P

ADAPTER_SCALE = 2.0
F32 = jnp.float32
VMEM_LIMIT = 48 * 1024 * 1024


CUTS = 2
CHUNKS = (5, 3)
PLAN = [
    ("ring", 0),
    ("lift", 0),
    ("swap_mine", 0),
    ("ring_done", 0),
    ("swap_done", 0),
    ("ring", 0),
    ("lift_done", 0),
    ("across", 0),
    ("lift", 1),
    ("ring_done", 0),
    ("ring", 0),
    ("lift_done", 1),
    ("across_done", 0),
    ("across", 1),
    ("lift", 2),
    ("ring_done", 0),
    ("ring", 0),
    ("tokens_done", 0),
    ("swap_their", 0),
    ("ring_done", 0),
    ("ring", 1),
    ("swap_done", 1),
    ("base", 0),
    ("lift_done", 2),
    ("across_done", 1),
    ("across", 2),
    ("lift", 3),
    ("ring_done", 1),
    ("ring", 1),
    ("keep", 0),
    ("lift_done", 3),
    ("across_done", 2),
    ("across", 3),
    ("low", 0),
    ("ring_done", 1),
    ("ring", 1),
    ("base_done", 0),
    ("ring_done", 1),
    ("ring", 1),
    ("across_done", 3),
    ("ring_done", 1),
    ("base", 1),
    ("keep", 1),
]


def routes(count):
    planes = count // 2
    ring = [2 * z for z in range(planes)] + [2 * z + 1 for z in reversed(range(planes))]
    ahead = [(ring[p], ring[(p + 1) % count]) for p in range(count)]
    back = [(b, a) for a, b in ahead]
    across = [(i, i ^ 1) for i in range(count)]
    diagonal = [(i, (i + 1 if i % 2 else i - 1) % count) for i in range(count)]
    lift = [(i, (i + 2 if i % 2 else i - 2) % count) for i in range(count)]
    return ring, ahead, back, across, diagonal, lift


def params(count):
    return pltpu.CompilerParams(
        dimension_semantics=("arbitrary",) * count, vmem_limit_bytes=VMEM_LIMIT
    )


def pick(index, down_t, up, cuts):
    count = index.shape[0]
    _, rank, width = down_t.shape
    part = rank // cuts
    spec = pl.BlockSpec((1, rank, width), lambda i, at: (at[i], 0, 0))
    out = pl.BlockSpec((1, part, width), lambda i, at: (i, 0, 0))

    def body(at, a, b, *outs):
        for n, ref in enumerate(outs):
            source = a if n < cuts else b
            start = (n % cuts) * part
            ref[...] = source[:, start : start + part, :]

    shape = jax.ShapeDtypeStruct((count, part, width), down_t.dtype)
    return pl.pallas_call(
        body,
        grid_spec=pltpu.PrefetchScalarGridSpec(
            num_scalar_prefetch=1,
            grid=(count,),
            in_specs=[spec, spec],
            out_specs=[out] * (2 * cuts),
        ),
        out_shape=[shape] * (2 * cuts),
        compiler_params=params(1),
        cost_estimate=pl.CostEstimate(
            flops=0, bytes_accessed=count * rank * width * 8, transcendentals=0
        ),
    )(index, down_t, up)


def pick_two(which, first, second, a, b, cut):
    count = which.shape[0]
    block = (1,) + b.shape[1:]

    def body(which_ref, first_ref, second_ref, a_ref, b_ref, out_ref):
        side = which_ref[pl.program_id(0)]

        @pl.when(side == 0)
        def _():
            out_ref[...] = a_ref[...]

        @pl.when(side != 0)
        def _():
            out_ref[...] = b_ref[...]

    return pl.pallas_call(
        body,
        grid_spec=pltpu.PrefetchScalarGridSpec(
            num_scalar_prefetch=3,
            grid=(count,),
            in_specs=[
                pl.BlockSpec(block, lambda i, w, f, s: (f[i], cut, 0)),
                pl.BlockSpec(block, lambda i, w, f, s: (s[i], 0, 0)),
            ],
            out_specs=pl.BlockSpec(block, lambda i, w, f, s: (i, 0, 0)),
        ),
        out_shape=jax.ShapeDtypeStruct((count,) + b.shape[1:], b.dtype),
        compiler_params=params(1),
        cost_estimate=pl.CostEstimate(
            flops=0, bytes_accessed=count * int(np.prod(block)) * 6, transcendentals=0
        ),
    )(which, first, second, a, b)


def choose_specs(sources):
    owned, parts = sources
    specs = [pl.BlockSpec((1,) + owned.shape[1:], lambda i, table, *rest: (table[1, i], 0, 0))]
    for p in parts:
        specs.append(
            pl.BlockSpec((1,) + p.shape[1:], lambda i, table, *rest: (table[2, i], 0, 0))
        )
    return specs


def low_partial(table, tokens, sources):
    blocks = table.shape[1]
    rows, width = tokens.shape[0] // blocks, tokens.shape[1]
    rank = sources[0].shape[1]

    def body(table_ref, x_ref, own_ref, *refs):
        place = table_ref[0, pl.program_id(0)]
        out_ref = refs[-1]

        def write(weight):
            out_ref[...] = lax.dot_general(
                x_ref[...], weight, (((1,), (1,)), ((), ())), preferred_element_type=F32
            )

        @pl.when(place == 0)
        def _():
            write(own_ref[0])

        @pl.when(place != 0)
        def _():
            write(jnp.concatenate([r[0] for r in refs[:-1]], axis=0))

    return pl.pallas_call(
        body,
        grid_spec=pltpu.PrefetchScalarGridSpec(
            num_scalar_prefetch=1,
            grid=(blocks,),
            in_specs=[pl.BlockSpec((rows, width), lambda i, s: (i, 0))] + choose_specs(sources),
            out_specs=pl.BlockSpec((rows, rank), lambda i, s: (i, 0)),
        ),
        out_shape=jax.ShapeDtypeStruct((tokens.shape[0], rank), F32),
        compiler_params=params(1),
        cost_estimate=pl.CostEstimate(
            flops=2 * tokens.shape[0] * width * rank,
            bytes_accessed=tokens.size * 2 + 8 * rank * width * 2,
            transcendentals=0,
        ),
    )(table, tokens, sources[0], *sources[1])


def product(shards, same, swapped, pieces, out_type):
    rows, width = same.shape
    columns = pieces[0].shape[1]
    depth = pieces[0].shape[0]
    tile = 256 if rows % 256 == 0 else rows
    count = len(pieces)

    def body(at, same_ref, swapped_ref, *refs):
        x_ref = refs[-1]

        @pl.when(at[count] == 0)
        def _():
            x_ref[:, :width] = same_ref[...]
            x_ref[:, width:] = swapped_ref[...]

        @pl.when(at[count] != 0)
        def _():
            x_ref[:, :width] = swapped_ref[...]
            x_ref[:, width:] = same_ref[...]

        total = None
        for k in range(count):
            x = x_ref[:, pl.ds(pl.multiple_of(at[k], depth), depth)]
            if k == count - 2:
                x = x[:, : depth // 2]
            if k == count - 1:
                x = x[:, depth // 2 :]
            term = jnp.dot(x, refs[k][...], preferred_element_type=F32)
            total = term if total is None else total + term
        refs[count][...] = total.astype(out_type)

    return pl.pallas_call(
        body,
        grid_spec=pltpu.PrefetchScalarGridSpec(
            num_scalar_prefetch=1,
            grid=(rows // tile,),
            in_specs=[pl.BlockSpec((tile, width), lambda i, at: (i, 0))] * 2
            + [pl.BlockSpec(p.shape, lambda i, at: (0, 0)) for p in pieces],
            out_specs=pl.BlockSpec((tile, columns), lambda i, at: (i, 0)),
            scratch_shapes=[pltpu.VMEM((tile, 2 * width), same.dtype)],
        ),
        out_shape=jax.ShapeDtypeStruct((rows, columns), out_type),
        compiler_params=params(1),
        cost_estimate=pl.CostEstimate(
            flops=4 * rows * width * columns,
            bytes_accessed=(2 * rows * width + 2 * width * columns + 2 * rows * columns) * 2,
            transcendentals=0,
        ),
    )(shards, same, swapped, *pieces)


def finish(table, live, half, low_a, low_b, mine, theirs, sources):
    blocks = table.shape[1]
    rows = mine[0].shape[0] // blocks
    widths = [m.shape[1] for m in mine]
    part = sum(widths)
    rank = sources[0].shape[1]
    chunks = len(mine)

    def body(table_ref, live_ref, half_ref, la, lb, *refs):
        out_ref = refs[-1]
        block = pl.program_id(0)
        place = table_ref[0, block]
        low = (la[...] + lb[...]).astype(jnp.bfloat16)
        mine_refs, theirs_refs = refs[:chunks], refs[chunks : 2 * chunks]
        own_ref, part_refs = refs[2 * chunks], refs[2 * chunks + 1 : -1]

        def write(weight_of, left, right):
            start = 0
            for ref in tuple(left) + tuple(right):
                width = ref.shape[1]
                delta = jnp.dot(low, weight_of(start, width), preferred_element_type=F32)
                total = ref[...].astype(F32) + ADAPTER_SCALE * delta
                alive = lax.broadcasted_iota(jnp.int32, (rows, width), 0) < live_ref[block]
                out_ref[:, start : start + width] = jnp.where(alive, total, 0.0).astype(
                    out_ref.dtype
                )
                start += width

        def from_own(start, width):
            return own_ref[0, :, start : start + width]

        def from_parts(start, width):
            return jnp.concatenate([r[0, :, start : start + width] for r in part_refs], axis=0)

        for n, weight_of in enumerate((from_own, from_parts)):
            for side in range(2):

                @pl.when(jnp.logical_and(place == n, half_ref[0] == side))
                def _(weight_of=weight_of, side=side):
                    if side == 0:
                        write(weight_of, mine_refs, theirs_refs)
                    else:
                        write(weight_of, theirs_refs, mine_refs)

    row = lambda width: pl.BlockSpec((rows, width), lambda i, s, l, h: (i, 0))
    return pl.pallas_call(
        body,
        grid_spec=pltpu.PrefetchScalarGridSpec(
            num_scalar_prefetch=3,
            grid=(blocks,),
            in_specs=[row(rank), row(rank)]
            + [row(w) for w in widths + widths]
            + choose_specs(sources),
            out_specs=row(2 * part),
        ),
        out_shape=jax.ShapeDtypeStruct((rows * blocks, 2 * part), jnp.bfloat16),
        compiler_params=params(1),
        cost_estimate=pl.CostEstimate(
            flops=4 * rows * blocks * part * rank,
            bytes_accessed=rows * blocks * part * 10 + 8 * rank * part * 4,
            transcendentals=0,
        ),
    )(table, live, half, low_a, low_b, *mine, *theirs, sources[0], *sources[1])


def ranks(ids, owner_of, owner):
    hit = owner_of == owner
    return hit, jnp.cumsum(hit.astype(jnp.int32)) - hit.astype(jnp.int32)


def slots(ids, per_device, owner, count):
    hit, place = ranks(ids, ids // per_device, owner)
    at = jnp.arange(count)[:, None]
    chosen = jnp.logical_and(hit[None, :], place[None, :] == at)
    return jnp.sum(jnp.where(chosen, (ids % per_device)[None, :], 0), axis=1).astype(jnp.int32)


class Order:
    def __init__(self):
        self.last = ()

    def after(self, x):
        return lax.optimization_barrier((x,) + self.last)[0] if self.last else x

    def arrived(self, *found):
        self.last = (self.last + found)[-6:]


def local(groups, count, tokens, query_matrix, down, up, ids, live):
    ring, ahead, back, across, diagonal, lift = routes(count)
    rep = lambda a, route: lax.ppermute(a, "replica", route)
    partner = lambda a: lax.ppermute(a, "groups", [(i, i ^ 1) for i in range(groups)])
    other_core = lambda a: lax.ppermute(a, "tensor", [(0, 1), (1, 0)])
    order = Order()

    depth, out_half = query_matrix.shape
    quarter = out_half // 2
    blocks = ids.shape[0]
    per_device = down.shape[0]
    most = blocks - 1
    half = (lax.axis_index("groups") % 2).astype(jnp.int32)
    me = lax.axis_index("replica").astype(jnp.int32)
    core = lax.axis_index("tensor").astype(jnp.int32)

    place = np.argsort(ring)
    offsets = np.zeros((count, count + 1), np.int32)
    for r in range(count):
        for step in range(1, count // 2 + 1):
            offsets[r, 2 * step - 1] = ring[(place[r] - step) % count] * depth
            offsets[r, 2 * step] = ring[(place[r] + step) % count] * depth
        offsets[r, 0] = r * depth
    shards = lax.dynamic_index_in_dim(jnp.asarray(offsets), me, 0, keepdims=False)
    shards = jnp.concatenate([shards, core.reshape(1)])

    widths = [quarter * n // 8 for n in CHUNKS]
    starts = [sum(widths[:n]) for n in range(len(widths))]
    pieces = [
        [lax.dynamic_slice(query_matrix, (0, half * quarter + s), (depth, w))]
        for s, w in zip(starts, widths)
    ]

    def ring_step(chunk):
        held = pieces[chunk]
        step = (len(held) + 1) // 2
        low_side, high_side = (held[0], held[0]) if step == 1 else held[-2:]
        if step == count // 2:
            low_side, high_side = low_side[: depth // 2], high_side[depth // 2 :]
        held += [rep(order.after(low_side), ahead), rep(order.after(high_side), back)]

    their_same = partner(tokens)
    ids_across = rep(ids, across)
    ids_diagonal = rep(ids, diagonal)

    down_t = jnp.swapaxes(down, 1, 2)
    parts = pick(slots(ids_diagonal, per_device, me, most), down_t, up, CUTS)
    feeder = jnp.where(me % 2 == 1, me - 2, me + 2) % count
    across_owner = ids_across // per_device
    _, feeder_place = ranks(ids_across, across_owner, feeder)
    from_feeder = (across_owner == feeder).astype(jnp.int32)
    own_at = jnp.where(across_owner == me, ids_across % per_device, 0).astype(jnp.int32)
    feeder_at = jnp.where(from_feeder == 1, jnp.minimum(feeder_place, most - 1), 0).astype(jnp.int32)
    foreign = (ids // per_device != me).astype(jnp.int32)
    table = jnp.stack(
        [
            foreign,
            jnp.where(foreign == 0, ids % per_device, 0).astype(jnp.int32),
            jnp.where(foreign == 1, jnp.arange(blocks, dtype=jnp.int32), 0),
        ]
    )
    lifted, sent = {}, {}

    def start_lift(n):
        lifted[n] = rep(order.after(parts[n]), lift)

    def start_across(n):
        owned = down_t if n < CUTS else up
        both = pick_two(
            from_feeder, own_at, feeder_at, owned, order.after(lifted[n]), n % CUTS
        )
        sent[n] = rep(both, across)
        order.arrived(both)

    mine, theirs, halves = {}, {}, {}

    def start_base(chunk):
        while len(pieces[chunk]) < count + 1:
            ring_step(chunk)
        result = product(shards, their_same, halves["their"], pieces[chunk], jnp.bfloat16)
        theirs[chunk] = partner(result)
        order.arrived(result)

    def keep_base(chunk):
        mine[chunk] = product(shards, order.after(tokens), halves["mine"], pieces[chunk], F32)
        order.arrived(mine[chunk])

    lows = {}
    for action in PLAN:
        kind, n = action[0], action[1]
        if kind == "ring":
            ring_step(n)
        elif kind == "ring_done":
            order.arrived(*pieces[n][-2:])
        elif kind == "lift":
            start_lift(n)
        elif kind == "lift_done":
            order.arrived(lifted[n])
        elif kind == "across":
            start_across(n)
        elif kind == "across_done":
            order.arrived(sent[n])
        elif kind == "base_done":
            order.arrived(theirs[n])
        elif kind == "swap_mine":
            halves["mine"] = other_core(order.after(tokens))
        elif kind == "swap_their":
            halves["their"] = other_core(order.after(their_same))
        elif kind == "swap_done":
            order.arrived(halves["mine" if n == 0 else "their"])
        elif kind == "tokens_done":
            order.arrived(their_same)
        elif kind == "low":
            lows["a"] = low_partial(
                table, order.after(tokens), (down_t, [sent[i] for i in range(CUTS)])
            )
            lows["b"] = other_core(lows["a"])
            order.arrived(lows["a"])
        elif kind == "base":
            start_base(n)
        elif kind == "keep":
            keep_base(n)
    chunks = range(len(widths))
    ups = (up, [sent[i] for i in range(CUTS, 2 * CUTS)])
    return finish(
        table,
        live,
        half.reshape(1),
        lows["a"],
        lows["b"],
        [mine[c] for c in chunks],
        [theirs[c] for c in chunks],
        ups,
    )


def solution(mesh):
    in_specs = (
        P(("groups", "replica"), "tensor"),
        P("replica", "tensor"),
        P(("groups", "replica"), "tensor", None),
        P(("groups", "replica"), None, "tensor"),
        P(("groups", "replica")),
        P(("groups", "replica")),
    )
    out_specs = P(("groups", "replica"), "tensor")
    body = functools.partial(local, mesh.shape["groups"], mesh.shape["replica"])
    return jax.shard_map(body, mesh=mesh, in_specs=in_specs, out_specs=out_specs, check_vma=False)
```

time: 279 us -> 210 us (0.75)
  waiting for transfers between devices: 123 us -> 98.7 us
  starting transfers between devices: 65.5 us -> 44.2 us
  other arithmetic: 19 us -> 0.64 us
  Pallas kernels: 59.6 us -> 52.7 us
    ppermute x30 -> x26, waiting for transfers between devices: 117 us -> 90.6 us  [local(): rep = lambda a, route: lax.ppermute(a, 'replica', route)]
    ppermute x30 -> x26, starting transfers between devices: 60 us -> 39 us  [local(): rep = lambda a, route: lax.ppermute(a, 'replica', route)]
    select_n x2 -> x0, other arithmetic: 18.4 us -> none  [widen(): jnp.where(core == 0, jnp.concatenate([part, swapped], axis=1), jnp.concat...]
    pallas_call x2 -> x4, Pallas kernels: 9 us -> 4.73 us  [pick_two(): pl.pallas_call(body, grid_spec=pltpu.PrefetchScalarGridSpec(num_scalar_pr...]
    unnamed x34 -> x40, local copies, waits for them, and re-layouts: 5.06 us -> 8.79 us
    pallas_call x6 -> x4, Pallas kernels: 34.8 us -> 32.5 us  [product(): pl.pallas_call(body, grid_spec=pltpu.PrefetchScalarGridSpec(num_scalar_pr...]
    ppermute x4 -> x3, waiting for transfers between devices: 6.04 us -> 8.08 us  [local(): lax.ppermute(a, 'groups', [(i, i ^ 1) for i in range(groups)])]
  transfers between devices with their start and end apart: 37 -> 32, of which waited for: 13 -> 17; matrix products, arithmetic and copies ran while one was open for 9% -> 2% of each run, Pallas kernels for 19% -> 22%
where the time goes in v2:
time: 210 us
  waiting for transfers between devices  98.7 us (47%)
  Pallas kernels  52.7 us (25%)
  starting transfers between devices  44.2 us (21%)
  local copies, waits for them, and re-layouts  13.1 us (6%)
    ppermute x26, waiting for transfers between devices, local(): rep = lambda a, route: lax.ppermute(a, 'replica', route)  90.6 us
    ppermute x26, starting transfers between devices, local(): rep = lambda a, route: lax.ppermute(a, 'replica', route)  39 us
    pallas_call x4, Pallas kernels, product(): pl.pallas_call(body, grid_spec=pltpu.PrefetchScalarGridSpec(num_scalar_pr...  32.5 us
    unnamed x40, local copies, waits for them, and re-layouts  8.79 us
    ppermute x3, waiting for transfers between devices, local(): lax.ppermute(a, 'groups', [(i, i ^ 1) for i in range(groups)])  8.08 us
    pallas_call x1, Pallas kernels, finish(): pl.pallas_call(body, grid_spec=pltpu.PrefetchScalarGridSpec(num_scalar_pr...  6.37 us
    pallas_call x1, Pallas kernels, low_partial(): pl.pallas_call(body, grid_spec=pltpu.PrefetchScalarGridSpec(num_scalar_pr...  5.09 us
    ppermute x3, starting transfers between devices, local(): lax.ppermute(a, 'groups', [(i, i ^ 1) for i in range(groups)])  4.75 us
  transfers between devices with their start and end apart: 32, of which 17 were waited for; matrix products, arithmetic and copies ran while one was open for 2% of the time, Pallas kernels for 22%

profile of v2, /device:TPU:0, one launch (start us, length us, event | category | flops | bytes accessed | tf_op | source)
XLA Modules:
  0.0 209.6 jit_solution(635384179548734827)
XLA Ops:
  0.5 2.6 %collective-permute-start.12 = (bf16[768,2048]{1,0:T(8,128)(2,1)}, bf16[768,2048]{1,0:T(8,128)(2,1)}, u32[]{:S(2)}, u32[]{:S(2)}) collective-permute-start(bf16[768,2048]{1,0:T(8,128)(2,1)} %same_ref.1), channel_id=1, source_target_pairs={{0,16},{16,0},{1,17},{17,1},{2,18},{18,2},{3,19},{19,3},{4,20},{20... | collective-permute-start | bytes 9437192 | tf_op jit(solution)/shard_map/ppermute | solution.py:338
  3.0 4.6 %collective-permute-start.1 = (s32[6]{0:T(128)}, s32[6]{0:T(128)S(1)}, u32[]{:S(2)}, u32[]{:S(2)}) collective-permute-start(s32[6]{0:T(128)} %param.11), channel_id=1, source_target_pairs={{0,14},{2,4},{4,2},{6,8},{8,6},{10,12},{12,10},{14,0},{1,15},{3,5}... | collective-permute-start | bytes 80 | tf_op jit(solution)/shard_map/ppermute | solution.py:337
  7.7 2.1 collective-permute-start.3
  11.7 4.0 %shard_map.73 = (bf16[5,32,2048]{2,1,0:T(8,128)(2,1)}, bf16[5,32,2048]{2,1,0:T(8,128)(2,1)S(1)}, bf16[5,32,2048]{2,1,0:T(8,128)(2,1)S(1)}, bf16[5,32,2048]{2,1,0:T(8,128)(2,1)S(1)}) custom-call(s32[5]{0:T(128)S(1)} %select_reduce_fusion.at, bf16[8,64,2048]{2,1,0:T(8,128)(2,1)S(1)} %bitcast.22, bf16[8,64,2048]{2,1,0:T(8,128)(2,1)} %refs_4_.1), custom_call_target="tpu_custom_call" | custom-call | bytes 5242880 | tf_op jit(solution)/shard_map/pallas_call | solution.py:96
  18.2 4.4 %collective-permute-start.5 = (bf16[5,32,2048]{2,1,0:T(8,128)(2,1)}, bf16[5,32,2048]{2,1,0:T(8,128)(2,1)S(1)}, u32[]{:S(2)}, u32[]{:S(2)}) collective-permute-start(bf16[5,32,2048]{2,1,0:T(8,128)(2,1)} %get-tuple-element.34), channel_id=1, source_target_pairs={{0,12},{2,6},{4,0},{6,10},{8,4},{10,14},{12,8},{14,2},{1,13},{3,7}... | collective-permute-start | bytes 1966088 | tf_op jit(solution)/shard_map/ppermute | solution.py:337
  22.6 2.9 %collective-permute-done.3.refs_2_ = bf16[512,640]{1,0:T(8,128)(2,1)} collective-permute-done((bf16[512,640]{1,0:T(8,128)(2,1)S(1)}, bf16[512,640]{1,0:T(8,128)(2,1)}, u32[]{:S(2)}, u32[]{:S(2)}) %collective-permute-start.3) | collective-permute-done | bytes 655392 | tf_op jit(solution)/shard_map/ppermute | solution.py:337
  28.0 11.3 %collective-permute-done.5.b_ref = bf16[5,32,2048]{2,1,0:T(8,128)(2,1)S(1)} collective-permute-done((bf16[5,32,2048]{2,1,0:T(8,128)(2,1)}, bf16[5,32,2048]{2,1,0:T(8,128)(2,1)S(1)}, u32[]{:S(2)}, u32[]{:S(2)}) %collective-permute-start.5) | collective-permute-done | bytes 655392 | tf_op jit(solution)/shard_map/ppermute | solution.py:337
  41.7 4.9 %collective-permute-start.9 = (bf16[6,32,2048]{2,1,0:T(8,128)(2,1)S(1)}, bf16[6,32,2048]{2,1,0:T(8,128)(2,1)S(1)}, u32[]{:S(2)}, u32[]{:S(2)}) collective-permute-start(bf16[6,32,2048]{2,1,0:T(8,128)(2,1)S(1)} %shard_map.74), channel_id=1, source_target_pairs={{0,2},{2,0},{4,6},{6,4},{8,10},{10,8},{12,14},{14,12},{1,3},{3,1},... | collective-permute-start | bytes 2359304 | tf_op jit(solution)/shard_map/ppermute | solution.py:337
  46.7 6.5 %collective-permute-done.7.refs_3_ = bf16[512,640]{1,0:T(8,128)(2,1)} collective-permute-done((bf16[512,640]{1,0:T(8,128)(2,1)}, bf16[512,640]{1,0:T(8,128)(2,1)}, u32[]{:S(2)}, u32[]{:S(2)}) %collective-permute-start.7) | collective-permute-done | bytes 655392 | tf_op jit(solution)/shard_map/ppermute | solution.py:337
  53.5 2.1 %collective-permute-start.10 = (bf16[512,640]{1,0:T(8,128)(2,1)}, bf16[512,640]{1,0:T(8,128)(2,1)S(1)}, u32[]{:S(2)}, u32[]{:S(2)}) collective-permute-start(bf16[512,640]{1,0:T(8,128)(2,1)} %collective-permute-done.7.refs_3_), channel_id=1, source_target_pairs={{0,4},{4,8},{8,12},{12,14},{14,10},{10,6},{6,2},{2,0},{1,5},{5,9},... | collective-permute-start | bytes 1966088 | tf_op jit(solution)/shard_map/ppermute | solution.py:337
  55.8 11.6 %collective-permute-done.6.b_ref = bf16[5,32,2048]{2,1,0:T(8,128)(2,1)S(1)} collective-permute-done((bf16[5,32,2048]{2,1,0:T(8,128)(2,1)S(1)}, bf16[5,32,2048]{2,1,0:T(8,128)(2,1)S(1)}, u32[]{:S(2)}, u32[]{:S(2)}) %collective-permute-start.6) | collective-permute-done | bytes 655392 | tf_op jit(solution)/shard_map/ppermute | solution.py:337
  68.2 3.8 %collective-permute-done.12.same_ref = bf16[768,2048]{1,0:T(8,128)(2,1)} collective-permute-done((bf16[768,2048]{1,0:T(8,128)(2,1)}, bf16[768,2048]{1,0:T(8,128)(2,1)}, u32[]{:S(2)}, u32[]{:S(2)}) %collective-permute-start.12) | collective-permute-done | bytes 3145760 | tf_op jit(solution)/shard_map/ppermute | solution.py:338
  72.0 7.8 %collective-permute-done.10.refs_5_ = bf16[512,640]{1,0:T(8,128)(2,1)S(1)} collective-permute-done((bf16[512,640]{1,0:T(8,128)(2,1)}, bf16[512,640]{1,0:T(8,128)(2,1)S(1)}, u32[]{:S(2)}, u32[]{:S(2)}) %collective-permute-start.10) | collective-permute-done | bytes 655392 | tf_op jit(solution)/shard_map/ppermute | solution.py:337
  81.3 3.8 %collective-permute-start.19 = (bf16[6,32,2048]{2,1,0:T(8,128)(2,1)S(1)}, bf16[6,32,2048]{2,1,0:T(8,128)(2,1)}, u32[]{:S(2)}, u32[]{:S(2)}) collective-permute-start(bf16[6,32,2048]{2,1,0:T(8,128)(2,1)S(1)} %shard_map.75), channel_id=1, source_target_pairs={{0,2},{2,0},{4,6},{6,4},{8,10},{10,8},{12,14},{14,12},{1,3},{3,1},... | collective-permute-start | bytes 2359304 | tf_op jit(solution)/shard_map/ppermute | solution.py:337
  91.7 17.8 %collective-permute-done.13.refs_7_ = bf16[256,640]{1,0:T(8,128)(2,1)} collective-permute-done((bf16[256,640]{1,0:T(8,128)(2,1)}, bf16[256,640]{1,0:T(8,128)(2,1)}, u32[]{:S(2)}, u32[]{:S(2)}) %collective-permute-start.13) | collective-permute-done | bytes 327712 | tf_op jit(solution)/shard_map/ppermute | solution.py:337
  109.5 1.7 collective-permute-start.16
  113.7 9.7 %shard_map.76 = bf16[768,640]{1,0:T(8,128)(2,1)} custom-call(s32[10]{0:T(128)S(1)} %pad_add_fusion.1.at, bf16[768,2048]{1,0:T(8,128)(2,1)} %collective-permute-done.12.same_ref, bf16[768,2048]{1,0:T(8,128)(2,1)} %collective-permute-done.17.swapped_ref, bf16[512,640]{1,0:T(8,128)(2,1)S(1)} %constant_dynamic-slice_fusion.1.refs_0_, ...), custom_call_target="tpu_custom_call" | custom-call | flops 4026531840 | bytes 13500416 | tf_op jit(solution)/shard_map/pallas_call | solution.py:227
  123.4 2.5 %shard_map.77 = bf16[6,32,2048]{2,1,0:T(8,128)(2,1)S(1)} custom-call(s32[6]{0:T(128)S(1)} %compare_convert_fusion.which_ref, s32[6]{0:T(128)S(1)} %get-tuple-element.63.first_ref, s32[6]{0:T(128)S(1)} %compare_select_fusion.second_ref, bf16[8,64,2048]{2,1,0:T(8,128)(2,1)S(1)} %copy-done.4, bf16[5,32,2048]{2,1,0:T(8,128)(2,1)} %collective-permute-done.18.b_ref), custom_call_target="tpu_custom_call" | custom-call | bytes 2359296 | tf_op jit(solution)/shard_map/pallas_call | solution.py:127
  126.0 1.8 collective-permute-start.21
  131.3 9.8 %shard_map.78.refs_0_ = f32[768,640]{1,0:T(8,128)} custom-call(s32[10]{0:T(128)S(1)} %pad_add_fusion.1.at, bf16[768,2048]{1,0:T(8,128)(2,1)} %same_ref.1, bf16[768,2048]{1,0:T(8,128)(2,1)} %collective-permute-done.4.swapped_ref, bf16[512,640]{1,0:T(8,128)(2,1)S(1)} %constant_dynamic-slice_fusion.1.refs_0_, bf16[512,640]{1,0:T(8,128)(2,1)} %collective-permute-done.2.refs_1_, ...), custom_call_target="tpu_custom_call" | custom-call | flops 4026531840 | bytes 13500416 | tf_op jit(solution)/shard_map/pallas_call | solution.py:227
  141.1 4.9 %collective-permute-done.20.b_ref = bf16[5,32,2048]{2,1,0:T(8,128)(2,1)S(1)} collective-permute-done((bf16[5,32,2048]{2,1,0:T(8,128)(2,1)S(1)}, bf16[5,32,2048]{2,1,0:T(8,128)(2,1)S(1)}, u32[]{:S(2)}, u32[]{:S(2)}) %collective-permute-start.20) | collective-permute-done | bytes 655392 | tf_op jit(solution)/shard_map/ppermute | solution.py:337
  147.3 5.1 %shard_map.80.la = f32[768,64]{1,0:T(8,128)S(1)} custom-call(s32[3,6]{1,0:T(4,128)S(1)} %pad_add_fusion.table_ref, bf16[768,2048]{1,0:T(8,128)(2,1)} %same_ref.1, bf16[8,64,2048]{2,1,0:T(8,128)(2,1)S(1)} %bitcast.25, bf16[6,32,2048]{2,1,0:T(8,128)(2,1)S(1)} %copy-done.6, bf16[6,32,2048]{2,1,0:T(8,128)(2,1)} %collective-permute-done.19.refs_1_), custom_call_target="tpu_custom_call" | custom-call | flops 201326592 | bytes 5242880 | tf_op jit(solution)/shard_map/pallas_call | solution.py:178
  152.6 1.7 collective-permute-start.26
  154.6 1.7 collective-permute-start.27
  156.3 7.5 %collective-permute-done.26.refs_6_ = bf16[512,384]{1,0:T(8,128)(2,1)S(1)} collective-permute-done((bf16[512,384]{1,0:T(8,128)(2,1)S(1)}, bf16[512,384]{1,0:T(8,128)(2,1)S(1)}, u32[]{:S(2)}, u32[]{:S(2)}) %collective-permute-start.26) | collective-permute-done | bytes 393248 | tf_op jit(solution)/shard_map/ppermute | solution.py:337
  163.9 2.4 %collective-permute-done.25.refs_5_ = bf16[512,384]{1,0:T(8,128)(2,1)S(1)} collective-permute-done((bf16[512,384]{1,0:T(8,128)(2,1)S(1)}, bf16[512,384]{1,0:T(8,128)(2,1)S(1)}, u32[]{:S(2)}, u32[]{:S(2)}) %collective-permute-start.25) | collective-permute-done | bytes 393248 | tf_op jit(solution)/shard_map/ppermute | solution.py:337
  166.5 2.0 collective-permute-start.30
  168.5 15.8 %collective-permute-done.29.refs_7_ = bf16[256,384]{1,0:T(8,128)(2,1)S(1)} collective-permute-done((bf16[256,384]{1,0:T(8,128)(2,1)S(1)}, bf16[256,384]{1,0:T(8,128)(2,1)S(1)}, u32[]{:S(2)}, u32[]{:S(2)}) %collective-permute-start.29) | collective-permute-done | bytes 196640 | tf_op jit(solution)/shard_map/ppermute | solution.py:337
  184.3 6.5 %shard_map.81 = bf16[768,384]{1,0:T(8,128)(2,1)S(1)} custom-call(s32[10]{0:T(128)S(1)} %pad_add_fusion.1.at, bf16[768,2048]{1,0:T(8,128)(2,1)} %collective-permute-done.12.same_ref, bf16[768,2048]{1,0:T(8,128)(2,1)} %collective-permute-done.17.swapped_ref, bf16[512,384]{1,0:T(8,128)(2,1)S(1)} %constant_dynamic-slice_fusion.2.refs_0_, ...), custom_call_target="tpu_custom_call" | custom-call | flops 2415919104 | bytes 10616832 | tf_op jit(solution)/shard_map/pallas_call | solution.py:227
  192.4 6.5 %shard_map.82.refs_1_ = f32[768,384]{1,0:T(8,128)S(1)} custom-call(s32[10]{0:T(128)S(1)} %pad_add_fusion.1.at, bf16[768,2048]{1,0:T(8,128)(2,1)} %same_ref.1, bf16[768,2048]{1,0:T(8,128)(2,1)} %collective-permute-done.4.swapped_ref, bf16[512,384]{1,0:T(8,128)(2,1)S(1)} %constant_dynamic-slice_fusion.2.refs_0_, ...), custom_call_target="tpu_custom_call" | custom-call | flops 2415919104 | bytes 10616832 | tf_op jit(solution)/shard_map/pallas_call | solution.py:227
  199.0 4.3 %collective-permute-done.31.refs_3_ = bf16[768,384]{1,0:T(8,128)(2,1)S(1)} collective-permute-done((bf16[768,384]{1,0:T(8,128)(2,1)S(1)}, bf16[768,384]{1,0:T(8,128)(2,1)S(1)}, u32[]{:S(2)}, u32[]{:S(2)}) %collective-permute-start.31) | collective-permute-done | bytes 589856 | tf_op jit(solution)/shard_map/ppermute | solution.py:338
  203.2 6.4 %shard_map.83 = bf16[768,2048]{1,0:T(8,128)(2,1)} custom-call(s32[3,6]{1,0:T(4,128)S(1)} %pad_add_fusion.table_ref, s32[6]{0:T(128)S(1)} %copy-done.13, s32[1]{0:T(128)} %bitcast.3.half_ref, f32[768,64]{1,0:T(8,128)S(1)} %shard_map.80.la, f32[768,64]{1,0:T(8,128)S(1)} %collective-permute-done.22.lb, f32[768,640]{1,0:T(8,128)} %shard_map.78.refs_0_, ...), custom_call_target="tpu_custom_call" | custom-call | flops 201326592 | bytes 9961472 | tf_op jit(solution)/shard_map/pallas_call | solution.py:292
  (104 shorter events, 28.7 us)
Async XLA Ops:
  0.0 25.8 %collective-permute-start.4 = (bf16[768,2048]{1,0:T(8,128)(2,1)}, bf16[768,2048]{1,0:T(8,128)(2,1)}, u32[]{:S(2)}, u32[]{:S(2)}) collective-permute-start(bf16[768,2048]{1,0:T(8,128)(2,1)} %same_ref.1), channel_id=1, source_target_pairs={{0,1},{1,0},{2,3},{3,2},{4,5},{5,4},{6,7},{7,6},{8,9},{9,8},{10,11... | collective-permute-start | bytes 9437192 | tf_op jit(solution)/shard_map/ppermute | solution.py:339
  0.5 71.6 %collective-permute-start.12 = (bf16[768,2048]{1,0:T(8,128)(2,1)}, bf16[768,2048]{1,0:T(8,128)(2,1)}, u32[]{:S(2)}, u32[]{:S(2)}) collective-permute-start(bf16[768,2048]{1,0:T(8,128)(2,1)} %same_ref.1), channel_id=1, source_target_pairs={{0,16},{16,0},{1,17},{17,1},{2,18},{18,2},{3,19},{19,3},{4,20},{20... | collective-permute-start | bytes 9437192 | tf_op jit(solution)/shard_map/ppermute | solution.py:338
  3.0 6.7 %collective-permute-start.1 = (s32[6]{0:T(128)}, s32[6]{0:T(128)S(1)}, u32[]{:S(2)}, u32[]{:S(2)}) collective-permute-start(s32[6]{0:T(128)} %param.11), channel_id=1, source_target_pairs={{0,14},{2,4},{4,2},{6,8},{8,6},{10,12},{12,10},{14,0},{1,15},{3,5}... | collective-permute-start | bytes 80 | tf_op jit(solution)/shard_map/ppermute | solution.py:337
  7.6 10.6 %collective-permute-start = (s32[6]{0:T(128)}, s32[6]{0:T(128)S(1)}, u32[]{:S(2)}, u32[]{:S(2)}) collective-permute-start(s32[6]{0:T(128)} %param.11), channel_id=1, source_target_pairs={{0,2},{2,0},{4,6},{6,4},{8,10},{10,8},{12,14},{14,12},{1,3},{3,1},... | collective-permute-start | bytes 80 | tf_op jit(solution)/shard_map/ppermute | solution.py:337
  7.7 17.8 %collective-permute-start.3 = (bf16[512,640]{1,0:T(8,128)(2,1)S(1)}, bf16[512,640]{1,0:T(8,128)(2,1)}, u32[]{:S(2)}, u32[]{:S(2)}) collective-permute-start(bf16[512,640]{1,0:T(8,128)(2,1)S(1)} %constant_dynamic-slice_fusion.1.refs_0_), channel_id=1, source_target_pairs={{4,0},{8,4},{12,8},{14,12},{10,14},{6,10},{2,6},{0,2},{5,1},{9,5},... | collective-permute-start | bytes 1966088 | tf_op jit(solution)/shard_map/ppermute | solution.py:337
  9.7 16.1 %collective-permute-start.2 = (bf16[512,640]{1,0:T(8,128)(2,1)S(1)}, bf16[512,640]{1,0:T(8,128)(2,1)}, u32[]{:S(2)}, u32[]{:S(2)}) collective-permute-start(bf16[512,640]{1,0:T(8,128)(2,1)S(1)} %constant_dynamic-slice_fusion.1.refs_0_), channel_id=1, source_target_pairs={{0,4},{4,8},{8,12},{12,14},{14,10},{10,6},{6,2},{2,0},{1,5},{5,9},... | collective-permute-start | bytes 1966088 | tf_op jit(solution)/shard_map/ppermute | solution.py:337
  18.2 21.2 %collective-permute-start.5 = (bf16[5,32,2048]{2,1,0:T(8,128)(2,1)}, bf16[5,32,2048]{2,1,0:T(8,128)(2,1)S(1)}, u32[]{:S(2)}, u32[]{:S(2)}) collective-permute-start(bf16[5,32,2048]{2,1,0:T(8,128)(2,1)} %get-tuple-element.34), channel_id=1, source_target_pairs={{0,12},{2,6},{4,0},{6,10},{8,4},{10,14},{12,8},{14,2},{1,13},{3,7}... | collective-permute-start | bytes 1966088 | tf_op jit(solution)/shard_map/ppermute | solution.py:337
  25.8 27.3 %collective-permute-start.7 = (bf16[512,640]{1,0:T(8,128)(2,1)}, bf16[512,640]{1,0:T(8,128)(2,1)}, u32[]{:S(2)}, u32[]{:S(2)}) collective-permute-start(bf16[512,640]{1,0:T(8,128)(2,1)} %collective-permute-done.2.refs_1_), channel_id=1, source_target_pairs={{0,4},{4,8},{8,12},{12,14},{14,10},{10,6},{6,2},{2,0},{1,5},{5,9},... | collective-permute-start | bytes 1966088 | tf_op jit(solution)/shard_map/ppermute | solution.py:337
  27.5 26.0 %collective-permute-start.8 = (bf16[512,640]{1,0:T(8,128)(2,1)}, bf16[512,640]{1,0:T(8,128)(2,1)}, u32[]{:S(2)}, u32[]{:S(2)}) collective-permute-start(bf16[512,640]{1,0:T(8,128)(2,1)} %collective-permute-done.3.refs_2_), channel_id=1, source_target_pairs={{4,0},{8,4},{12,8},{14,12},{10,14},{6,10},{2,6},{0,2},{5,1},{9,5},... | collective-permute-start | bytes 1966088 | tf_op jit(solution)/shard_map/ppermute | solution.py:337
  41.7 25.7 %collective-permute-start.9 = (bf16[6,32,2048]{2,1,0:T(8,128)(2,1)S(1)}, bf16[6,32,2048]{2,1,0:T(8,128)(2,1)S(1)}, u32[]{:S(2)}, u32[]{:S(2)}) collective-permute-start(bf16[6,32,2048]{2,1,0:T(8,128)(2,1)S(1)} %shard_map.74), channel_id=1, source_target_pairs={{0,2},{2,0},{4,6},{6,4},{8,10},{10,8},{12,14},{14,12},{1,3},{3,1},... | collective-permute-start | bytes 2359304 | tf_op jit(solution)/shard_map/ppermute | solution.py:337
  46.7 20.8 %collective-permute-start.6 = (bf16[5,32,2048]{2,1,0:T(8,128)(2,1)S(1)}, bf16[5,32,2048]{2,1,0:T(8,128)(2,1)S(1)}, u32[]{:S(2)}, u32[]{:S(2)}) collective-permute-start(bf16[5,32,2048]{2,1,0:T(8,128)(2,1)S(1)} %copy-done.18), channel_id=1, source_target_pairs={{0,12},{2,6},{4,0},{6,10},{8,4},{10,14},{12,8},{14,2},{1,13},{3,7}... | collective-permute-start | bytes 1966088 | tf_op jit(solution)/shard_map/ppermute | solution.py:337
  53.5 26.4 %collective-permute-start.10 = (bf16[512,640]{1,0:T(8,128)(2,1)}, bf16[512,640]{1,0:T(8,128)(2,1)S(1)}, u32[]{:S(2)}, u32[]{:S(2)}) collective-permute-start(bf16[512,640]{1,0:T(8,128)(2,1)} %collective-permute-done.7.refs_3_), channel_id=1, source_target_pairs={{0,4},{4,8},{8,12},{12,14},{14,10},{10,6},{6,2},{2,0},{1,5},{5,9},... | collective-permute-start | bytes 1966088 | tf_op jit(solution)/shard_map/ppermute | solution.py:337
  55.6 24.8 %collective-permute-start.11 = (bf16[512,640]{1,0:T(8,128)(2,1)}, bf16[512,640]{1,0:T(8,128)(2,1)S(1)}, u32[]{:S(2)}, u32[]{:S(2)}) collective-permute-start(bf16[512,640]{1,0:T(8,128)(2,1)} %collective-permute-done.8.refs_4_), channel_id=1, source_target_pairs={{4,0},{8,4},{12,8},{14,12},{10,14},{6,10},{2,6},{0,2},{5,1},{9,5},... | collective-permute-start | bytes 1966088 | tf_op jit(solution)/shard_map/ppermute | solution.py:337
  80.4 31.1 %collective-permute-start.17 = (bf16[768,2048]{1,0:T(8,128)(2,1)}, bf16[768,2048]{1,0:T(8,128)(2,1)}, u32[]{:S(2)}, u32[]{:S(2)}) collective-permute-start(bf16[768,2048]{1,0:T(8,128)(2,1)} %collective-permute-done.12.same_ref), channel_id=1, source_target_pairs={{0,1},{1,0},{2,3},{3,2},{4,5},{5,4},{6,7},{7,6},{8,9},{9,8},{10,11... | collective-permute-start | bytes 9437192 | tf_op jit(solution)/shard_map/ppermute | solution.py:339
  81.3 42.2 %collective-permute-start.19 = (bf16[6,32,2048]{2,1,0:T(8,128)(2,1)S(1)}, bf16[6,32,2048]{2,1,0:T(8,128)(2,1)}, u32[]{:S(2)}, u32[]{:S(2)}) collective-permute-start(bf16[6,32,2048]{2,1,0:T(8,128)(2,1)S(1)} %shard_map.75), channel_id=1, source_target_pairs={{0,2},{2,0},{4,6},{6,4},{8,10},{10,8},{12,14},{14,12},{1,3},{3,1},... | collective-permute-start | bytes 2359304 | tf_op jit(solution)/shard_map/ppermute | solution.py:337
  85.1 38.3 %collective-permute-start.18 = (bf16[5,32,2048]{2,1,0:T(8,128)(2,1)}, bf16[5,32,2048]{2,1,0:T(8,128)(2,1)}, u32[]{:S(2)}, u32[]{:S(2)}) collective-permute-start(bf16[5,32,2048]{2,1,0:T(8,128)(2,1)} %copy-done.16), channel_id=1, source_target_pairs={{0,12},{2,6},{4,0},{6,10},{8,4},{10,14},{12,8},{14,2},{1,13},{3,7}... | collective-permute-start | bytes 1966088 | tf_op jit(solution)/shard_map/ppermute | solution.py:337
  88.9 20.6 %collective-permute-start.13 = (bf16[256,640]{1,0:T(8,128)(2,1)}, bf16[256,640]{1,0:T(8,128)(2,1)}, u32[]{:S(2)}, u32[]{:S(2)}) collective-permute-start(bf16[256,640]{1,0:T(8,128)(2,1)} %slice.16), channel_id=1, source_target_pairs={{0,4},{4,8},{8,12},{12,14},{14,10},{10,6},{6,2},{2,0},{1,5},{5,9},... | collective-permute-start | bytes 983048 | tf_op jit(solution)/shard_map/ppermute | solution.py:337
  90.6 18.9 %collective-permute-start.14 = (bf16[256,640]{1,0:T(8,128)(2,1)}, bf16[256,640]{1,0:T(8,128)(2,1)}, u32[]{:S(2)}, u32[]{:S(2)}) collective-permute-start(bf16[256,640]{1,0:T(8,128)(2,1)} %slice.17), channel_id=1, source_target_pairs={{4,0},{8,4},{12,8},{14,12},{10,14},{6,10},{2,6},{0,2},{5,1},{9,5},... | collective-permute-start | bytes 983048 | tf_op jit(solution)/shard_map/ppermute | solution.py:337
  109.5 19.7 %collective-permute-start.16 = (bf16[512,384]{1,0:T(8,128)(2,1)S(1)}, bf16[512,384]{1,0:T(8,128)(2,1)S(1)}, u32[]{:S(2)}, u32[]{:S(2)}) collective-permute-start(bf16[512,384]{1,0:T(8,128)(2,1)S(1)} %constant_dynamic-slice_fusion.2.refs_0_), channel_id=1, source_target_pairs={{4,0},{8,4},{12,8},{14,12},{10,14},{6,10},{2,6},{0,2},{5,1},{9,5},... | collective-permute-start | bytes 1179656 | tf_op jit(solution)/shard_map/ppermute | solution.py:337
  111.2 18.0 %collective-permute-start.15 = (bf16[512,384]{1,0:T(8,128)(2,1)S(1)}, bf16[512,384]{1,0:T(8,128)(2,1)S(1)}, u32[]{:S(2)}, u32[]{:S(2)}) collective-permute-start(bf16[512,384]{1,0:T(8,128)(2,1)S(1)} %constant_dynamic-slice_fusion.2.refs_0_), channel_id=1, source_target_pairs={{0,4},{4,8},{8,12},{12,14},{14,10},{10,6},{6,2},{2,0},{1,5},{5,9},... | collective-permute-start | bytes 1179656 | tf_op jit(solution)/shard_map/ppermute | solution.py:337
  126.0 20.5 %collective-permute-start.21 = (bf16[6,32,2048]{2,1,0:T(8,128)(2,1)S(1)}, bf16[6,32,2048]{2,1,0:T(8,128)(2,1)S(1)}, u32[]{:S(2)}, u32[]{:S(2)}) collective-permute-start(bf16[6,32,2048]{2,1,0:T(8,128)(2,1)S(1)} %shard_map.77), channel_id=1, source_target_pairs={{0,2},{2,0},{4,6},{6,4},{8,10},{10,8},{12,14},{14,12},{1,3},{3,1},... | collective-permute-start | bytes 2359304 | tf_op jit(solution)/shard_map/ppermute | solution.py:337
  127.8 36.1 %collective-permute-start.28 = (bf16[768,640]{1,0:T(8,128)(2,1)}, bf16[768,640]{1,0:T(8,128)(2,1)S(1)}, u32[]{:S(2)}, u32[]{:S(2)}) collective-permute-start(bf16[768,640]{1,0:T(8,128)(2,1)} %shard_map.76), channel_id=1, source_target_pairs={{0,16},{16,0},{1,17},{17,1},{2,18},{18,2},{3,19},{19,3},{4,20},{20... | collective-permute-start | bytes 2949128 | tf_op jit(solution)/shard_map/ppermute | solution.py:338
  128.3 17.7 %collective-permute-start.20 = (bf16[5,32,2048]{2,1,0:T(8,128)(2,1)S(1)}, bf16[5,32,2048]{2,1,0:T(8,128)(2,1)S(1)}, u32[]{:S(2)}, u32[]{:S(2)}) collective-permute-start(bf16[5,32,2048]{2,1,0:T(8,128)(2,1)S(1)} %copy-done.15), channel_id=1, source_target_pairs={{0,12},{2,6},{4,0},{6,10},{8,4},{10,14},{12,8},{14,2},{1,13},{3,7}... | collective-permute-start | bytes 1966088 | tf_op jit(solution)/shard_map/ppermute | solution.py:337
  129.2 23.4 %collective-permute-start.23 = (bf16[512,384]{1,0:T(8,128)(2,1)S(1)}, bf16[512,384]{1,0:T(8,128)(2,1)S(1)}, u32[]{:S(2)}, u32[]{:S(2)}) collective-permute-start(bf16[512,384]{1,0:T(8,128)(2,1)S(1)} %collective-permute-done.15.refs_1_), channel_id=1, source_target_pairs={{0,4},{4,8},{8,12},{12,14},{14,10},{10,6},{6,2},{2,0},{1,5},{5,9},... | collective-permute-start | bytes 1179656 | tf_op jit(solution)/shard_map/ppermute | solution.py:337
  130.5 22.1 %collective-permute-start.24 = (bf16[512,384]{1,0:T(8,128)(2,1)S(1)}, bf16[512,384]{1,0:T(8,128)(2,1)S(1)}, u32[]{:S(2)}, u32[]{:S(2)}) collective-permute-start(bf16[512,384]{1,0:T(8,128)(2,1)S(1)} %collective-permute-done.16.refs_2_), channel_id=1, source_target_pairs={{4,0},{8,4},{12,8},{14,12},{10,14},{6,10},{2,6},{0,2},{5,1},{9,5},... | collective-permute-start | bytes 1179656 | tf_op jit(solution)/shard_map/ppermute | solution.py:337
  152.6 11.3 %collective-permute-start.26 = (bf16[512,384]{1,0:T(8,128)(2,1)S(1)}, bf16[512,384]{1,0:T(8,128)(2,1)S(1)}, u32[]{:S(2)}, u32[]{:S(2)}) collective-permute-start(bf16[512,384]{1,0:T(8,128)(2,1)S(1)} %collective-permute-done.24.refs_4_), channel_id=1, source_target_pairs={{4,0},{8,4},{12,8},{14,12},{10,14},{6,10},{2,6},{0,2},{5,1},{9,5},... | collective-permute-start | bytes 1179656 | tf_op jit(solution)/shard_map/ppermute | solution.py:337
  154.3 12.1 %collective-permute-start.25 = (bf16[512,384]{1,0:T(8,128)(2,1)S(1)}, bf16[512,384]{1,0:T(8,128)(2,1)S(1)}, u32[]{:S(2)}, u32[]{:S(2)}) collective-permute-start(bf16[512,384]{1,0:T(8,128)(2,1)S(1)} %collective-permute-done.23.refs_3_), channel_id=1, source_target_pairs={{0,4},{4,8},{8,12},{12,14},{14,10},{10,6},{6,2},{2,0},{1,5},{5,9},... | collective-permute-start | bytes 1179656 | tf_op jit(solution)/shard_map/ppermute | solution.py:337
  154.6 37.8 %collective-permute-start.27 = (bf16[6,32,2048]{2,1,0:T(8,128)(2,1)S(1)}, bf16[6,32,2048]{2,1,0:T(8,128)(2,1)S(1)}, u32[]{:S(2)}, u32[]{:S(2)}) collective-permute-start(bf16[6,32,2048]{2,1,0:T(8,128)(2,1)S(1)} %shard_map.79), channel_id=1, source_target_pairs={{0,2},{2,0},{4,6},{6,4},{8,10},{10,8},{12,14},{14,12},{1,3},{3,1},... | collective-permute-start | bytes 2359304 | tf_op jit(solution)/shard_map/ppermute | solution.py:337
  166.4 17.9 %collective-permute-start.29 = (bf16[256,384]{1,0:T(8,128)(2,1)S(1)}, bf16[256,384]{1,0:T(8,128)(2,1)S(1)}, u32[]{:S(2)}, u32[]{:S(2)}) collective-permute-start(bf16[256,384]{1,0:T(8,128)(2,1)S(1)} %slice.18), channel_id=1, source_target_pairs={{0,4},{4,8},{8,12},{12,14},{14,10},{10,6},{6,2},{2,0},{1,5},{5,9},... | collective-permute-start | bytes 589832 | tf_op jit(solution)/shard_map/ppermute | solution.py:337
  166.5 17.8 %collective-permute-start.30 = (bf16[256,384]{1,0:T(8,128)(2,1)S(1)}, bf16[256,384]{1,0:T(8,128)(2,1)S(1)}, u32[]{:S(2)}, u32[]{:S(2)}) collective-permute-start(bf16[256,384]{1,0:T(8,128)(2,1)S(1)} %slice.19), channel_id=1, source_target_pairs={{4,0},{8,4},{12,8},{14,12},{10,14},{6,10},{2,6},{0,2},{5,1},{9,5},... | collective-permute-start | bytes 589832 | tf_op jit(solution)/shard_map/ppermute | solution.py:337
  190.8 12.4 %collective-permute-start.31 = (bf16[768,384]{1,0:T(8,128)(2,1)S(1)}, bf16[768,384]{1,0:T(8,128)(2,1)S(1)}, u32[]{:S(2)}, u32[]{:S(2)}) collective-permute-start(bf16[768,384]{1,0:T(8,128)(2,1)S(1)} %shard_map.81), channel_id=1, source_target_pairs={{0,16},{16,0},{1,17},{17,1},{2,18},{18,2},{3,19},{19,3},{4,20},{20... | collective-permute-start | bytes 1769480 | tf_op jit(solution)/shard_map/ppermute | solution.py:338
  192.4 6.5 %collective-permute-start.22 = (f32[768,64]{1,0:T(8,128)S(1)}, f32[768,64]{1,0:T(8,128)S(1)}, u32[]{:S(2)}, u32[]{:S(2)}) collective-permute-start(f32[768,64]{1,0:T(8,128)S(1)} %shard_map.80.la), channel_id=1, source_target_pairs={{0,1},{1,0},{2,3},{3,2},{4,5},{5,4},{6,7},{7,6},{8,9},{9,8},{10,11... | collective-permute-start | bytes 589832 | tf_op jit(solution)/shard_map/ppermute | solution.py:339
  (20 other events, 117.4 us)

commit v3 on v2

--- a/solution.py
+++ b/solution.py
@@ -16,48 +16,47 @@
 CUTS = 2
 CHUNKS = (5, 3)
 PLAN = [
+    ("lift", 0),
     ("ring", 0),
-    ("lift", 0),
     ("swap_mine", 0),
+    ("swap_done", 0),
     ("ring_done", 0),
-    ("swap_done", 0),
     ("ring", 0),
     ("lift_done", 0),
     ("across", 0),
     ("lift", 1),
+    ("ring", 0),
+    ("across_done", 0),
+    ("lift_done", 1),
+    ("across", 1),
     ("ring_done", 0),
+    ("swap_their", 0),
+    ("tokens_done", 0),
+    ("lift", 2),
+    ("ring", 1),
     ("ring", 0),
-    ("lift_done", 1),
-    ("across_done", 0),
-    ("across", 1),
-    ("lift", 2),
     ("ring_done", 0),
-    ("ring", 0),
-    ("tokens_done", 0),
-    ("swap_their", 0),
-    ("ring_done", 0),
-    ("ring", 1),
-    ("swap_done", 1),
     ("base", 0),
     ("lift_done", 2),
     ("across_done", 1),
     ("across", 2),
     ("lift", 3),
     ("ring_done", 1),
+    ("ring_done", 1),
     ("ring", 1),
     ("keep", 0),
+    ("low", 0),
     ("lift_done", 3),
+    ("across", 3),
     ("across_done", 2),
-    ("across", 3),
-    ("low", 0),
     ("ring_done", 1),
     ("ring", 1),
-    ("base_done", 0),
     ("ring_done", 1),
     ("ring", 1),
-    ("across_done", 3),
     ("ring_done", 1),
     ("base", 1),
+    ("base_done", 0),
+    ("base_done", 0),
     ("keep", 1),
 ]
 

time: 210 us -> 196 us (0.933)
  waiting for transfers between devices: 98.7 us -> 84.2 us
    ppermute x26, waiting for transfers between devices: 90.6 us -> 77.4 us  [local(): rep = lambda a, route: lax.ppermute(a, 'replica', route)]
    unnamed x40 -> x38, local copies, waits for them, and re-layouts: 8.79 us -> 7.95 us
  transfers between devices with their start and end apart: 32 -> 32, of which waited for: 17 -> 16; matrix products, arithmetic and copies ran while one was open for 2% -> 3% of each run, Pallas kernels for 22% -> 25%
where the time goes in v3:
time: 196 us
  waiting for transfers between devices  84.2 us (43%)
  Pallas kernels  54.7 us (28%)
  starting transfers between devices  43.8 us (22%)
  local copies, waits for them, and re-layouts  12.2 us (6%)
    ppermute x26, waiting for transfers between devices, local(): rep = lambda a, route: lax.ppermute(a, 'replica', route)  77.4 us
    ppermute x26, starting transfers between devices, local(): rep = lambda a, route: lax.ppermute(a, 'replica', route)  39.1 us
    pallas_call x4, Pallas kernels, product(): pl.pallas_call(body, grid_spec=pltpu.PrefetchScalarGridSpec(num_scalar_pr...  32.5 us
    unnamed x38, local copies, waits for them, and re-layouts  7.95 us
    ppermute x3, waiting for transfers between devices, local(): lax.ppermute(a, 'groups', [(i, i ^ 1) for i in range(groups)])  6.85 us
    pallas_call x4, Pallas kernels, pick_two(): pl.pallas_call(body, grid_spec=pltpu.PrefetchScalarGridSpec(num_scalar_pr...  6.57 us
    pallas_call x1, Pallas kernels, finish(): pl.pallas_call(body, grid_spec=pltpu.PrefetchScalarGridSpec(num_scalar_pr...  6.39 us
    pallas_call x1, Pallas kernels, low_partial(): pl.pallas_call(body, grid_spec=pltpu.PrefetchScalarGridSpec(num_scalar_pr...  5.09 us
  transfers between devices with their start and end apart: 32, of which 16 were waited for; matrix products, arithmetic and copies ran while one was open for 3% of the time, Pallas kernels for 25%

profile of v3, /device:TPU:0, one launch (start us, length us, event | category | flops | bytes accessed | tf_op | source)
XLA Modules:
  0.0 195.8 jit_solution(4629624133823772722)
XLA Ops:
  0.5 2.6 %collective-permute-start.12 = (bf16[768,2048]{1,0:T(8,128)(2,1)}, bf16[768,2048]{1,0:T(8,128)(2,1)}, u32[]{:S(2)}, u32[]{:S(2)}) collective-permute-start(bf16[768,2048]{1,0:T(8,128)(2,1)} %same_ref.1), channel_id=1, source_target_pairs={{0,16},{16,0},{1,17},{17,1},{2,18},{18,2},{3,19},{19,3},{4,20},{20... | collective-permute-start | bytes 9437192 | tf_op jit(solution)/shard_map/ppermute | solution.py:337
  3.0 4.6 %collective-permute-start.1 = (s32[6]{0:T(128)}, s32[6]{0:T(128)S(1)}, u32[]{:S(2)}, u32[]{:S(2)}) collective-permute-start(s32[6]{0:T(128)} %param.11), channel_id=1, source_target_pairs={{0,14},{2,4},{4,2},{6,8},{8,6},{10,12},{12,10},{14,0},{1,15},{3,5}... | collective-permute-start | bytes 80 | tf_op jit(solution)/shard_map/ppermute | solution.py:336
  7.7 2.1 %collective-permute-start.5 = (bf16[512,640]{1,0:T(8,128)(2,1)S(1)}, bf16[512,640]{1,0:T(8,128)(2,1)}, u32[]{:S(2)}, u32[]{:S(2)}) collective-permute-start(bf16[512,640]{1,0:T(8,128)(2,1)S(1)} %constant_dynamic-slice_fusion.2.refs_0_), channel_id=1, source_target_pairs={{4,0},{8,4},{12,8},{14,12},{10,14},{6,10},{2,6},{0,2},{5,1},{9,5},... | collective-permute-start | bytes 1966088 | tf_op jit(solution)/shard_map/ppermute | solution.py:336
  11.7 4.2 %shard_map.73 = (bf16[5,32,2048]{2,1,0:T(8,128)(2,1)}, bf16[5,32,2048]{2,1,0:T(8,128)(2,1)S(1)}, bf16[5,32,2048]{2,1,0:T(8,128)(2,1)S(1)}, bf16[5,32,2048]{2,1,0:T(8,128)(2,1)}) custom-call(s32[5]{0:T(128)S(1)} %select_reduce_fusion.at, bf16[8,64,2048]{2,1,0:T(8,128)(2,1)S(1)} %bitcast.22, bf16[8,64,2048]{2,1,0:T(8,128)(2,1)} %refs_4_.1), custom_call_target="tpu_custom_call" | custom-call | bytes 5242880 | tf_op jit(solution)/shard_map/pallas_call | solution.py:95
  17.6 5.2 %collective-permute-start.2 = (bf16[5,32,2048]{2,1,0:T(8,128)(2,1)}, bf16[5,32,2048]{2,1,0:T(8,128)(2,1)S(1)}, u32[]{:S(2)}, u32[]{:S(2)}) collective-permute-start(bf16[5,32,2048]{2,1,0:T(8,128)(2,1)} %get-tuple-element.34), channel_id=1, source_target_pairs={{0,12},{2,6},{4,0},{6,10},{8,4},{10,14},{12,8},{14,2},{1,13},{3,7}... | collective-permute-start | bytes 1966088 | tf_op jit(solution)/shard_map/ppermute | solution.py:336
  22.8 2.7 %collective-permute-done.5.refs_2_ = bf16[512,640]{1,0:T(8,128)(2,1)} collective-permute-done((bf16[512,640]{1,0:T(8,128)(2,1)S(1)}, bf16[512,640]{1,0:T(8,128)(2,1)}, u32[]{:S(2)}, u32[]{:S(2)}) %collective-permute-start.5) | collective-permute-done | bytes 655392 | tf_op jit(solution)/shard_map/ppermute | solution.py:336
  28.0 11.3 %collective-permute-done.2.b_ref = bf16[5,32,2048]{2,1,0:T(8,128)(2,1)S(1)} collective-permute-done((bf16[5,32,2048]{2,1,0:T(8,128)(2,1)}, bf16[5,32,2048]{2,1,0:T(8,128)(2,1)S(1)}, u32[]{:S(2)}, u32[]{:S(2)}) %collective-permute-start.2) | collective-permute-done | bytes 655392 | tf_op jit(solution)/shard_map/ppermute | solution.py:336
  41.7 4.9 %collective-permute-start.6 = (bf16[6,32,2048]{2,1,0:T(8,128)(2,1)S(1)}, bf16[6,32,2048]{2,1,0:T(8,128)(2,1)S(1)}, u32[]{:S(2)}, u32[]{:S(2)}) collective-permute-start(bf16[6,32,2048]{2,1,0:T(8,128)(2,1)S(1)} %shard_map.74), channel_id=1, source_target_pairs={{0,2},{2,0},{4,6},{6,4},{8,10},{10,8},{12,14},{14,12},{1,3},{3,1},... | collective-permute-start | bytes 2359304 | tf_op jit(solution)/shard_map/ppermute | solution.py:336
  46.7 6.9 %collective-permute-done.10.refs_4_ = bf16[512,640]{1,0:T(8,128)(2,1)} collective-permute-done((bf16[512,640]{1,0:T(8,128)(2,1)}, bf16[512,640]{1,0:T(8,128)(2,1)}, u32[]{:S(2)}, u32[]{:S(2)}) %collective-permute-start.10) | collective-permute-done | bytes 655392 | tf_op jit(solution)/shard_map/ppermute | solution.py:336
  53.5 2.1 %collective-permute-start.9 = (bf16[512,640]{1,0:T(8,128)(2,1)}, bf16[512,640]{1,0:T(8,128)(2,1)S(1)}, u32[]{:S(2)}, u32[]{:S(2)}) collective-permute-start(bf16[512,640]{1,0:T(8,128)(2,1)} %collective-permute-done.8.refs_3_), channel_id=1, source_target_pairs={{0,4},{4,8},{8,12},{12,14},{14,10},{10,6},{6,2},{2,0},{1,5},{5,9},... | collective-permute-start | bytes 1966088 | tf_op jit(solution)/shard_map/ppermute | solution.py:336
  55.8 11.6 %collective-permute-done.7.b_ref = bf16[5,32,2048]{2,1,0:T(8,128)(2,1)S(1)} collective-permute-done((bf16[5,32,2048]{2,1,0:T(8,128)(2,1)S(1)}, bf16[5,32,2048]{2,1,0:T(8,128)(2,1)S(1)}, u32[]{:S(2)}, u32[]{:S(2)}) %collective-permute-start.7) | collective-permute-done | bytes 655392 | tf_op jit(solution)/shard_map/ppermute | solution.py:336
  68.2 3.8 %collective-permute-done.12.same_ref = bf16[768,2048]{1,0:T(8,128)(2,1)} collective-permute-done((bf16[768,2048]{1,0:T(8,128)(2,1)}, bf16[768,2048]{1,0:T(8,128)(2,1)}, u32[]{:S(2)}, u32[]{:S(2)}) %collective-permute-start.12) | collective-permute-done | bytes 3145760 | tf_op jit(solution)/shard_map/ppermute | solution.py:337
  72.0 7.8 %collective-permute-done.9.refs_5_ = bf16[512,640]{1,0:T(8,128)(2,1)S(1)} collective-permute-done((bf16[512,640]{1,0:T(8,128)(2,1)}, bf16[512,640]{1,0:T(8,128)(2,1)S(1)}, u32[]{:S(2)}, u32[]{:S(2)}) %collective-permute-start.9) | collective-permute-done | bytes 655392 | tf_op jit(solution)/shard_map/ppermute | solution.py:336
  81.2 3.9 %collective-permute-start.17 = (bf16[6,32,2048]{2,1,0:T(8,128)(2,1)S(1)}, bf16[6,32,2048]{2,1,0:T(8,128)(2,1)}, u32[]{:S(2)}, u32[]{:S(2)}) collective-permute-start(bf16[6,32,2048]{2,1,0:T(8,128)(2,1)S(1)} %shard_map.75), channel_id=1, source_target_pairs={{0,2},{2,0},{4,6},{6,4},{8,10},{10,8},{12,14},{14,12},{1,3},{3,1},... | collective-permute-start | bytes 2359304 | tf_op jit(solution)/shard_map/ppermute | solution.py:336
  86.8 1.7 slice.16
  92.0 17.4 %collective-permute-done.14.refs_7_ = bf16[256,640]{1,0:T(8,128)(2,1)} collective-permute-done((bf16[256,640]{1,0:T(8,128)(2,1)}, bf16[256,640]{1,0:T(8,128)(2,1)}, u32[]{:S(2)}, u32[]{:S(2)}) %collective-permute-start.14) | collective-permute-done | bytes 327712 | tf_op jit(solution)/shard_map/ppermute | solution.py:336
  109.5 2.0 %collective-permute-start.18 = (bf16[512,384]{1,0:T(8,128)(2,1)S(1)}, bf16[512,384]{1,0:T(8,128)(2,1)S(1)}, u32[]{:S(2)}, u32[]{:S(2)}) collective-permute-start(bf16[512,384]{1,0:T(8,128)(2,1)S(1)} %constant_dynamic-slice_fusion.refs_0_), channel_id=1, source_target_pairs={{0,4},{4,8},{8,12},{12,14},{14,10},{10,6},{6,2},{2,0},{1,5},{5,9},... | collective-permute-start | bytes 1179656 | tf_op jit(solution)/shard_map/ppermute | solution.py:336
  113.7 9.7 %shard_map.76 = bf16[768,640]{1,0:T(8,128)(2,1)} custom-call(s32[10]{0:T(128)S(1)} %pad_add_fusion.1.at, bf16[768,2048]{1,0:T(8,128)(2,1)} %collective-permute-done.12.same_ref, bf16[768,2048]{1,0:T(8,128)(2,1)} %collective-permute-done.16.swapped_ref, bf16[512,640]{1,0:T(8,128)(2,1)S(1)} %constant_dynamic-slice_fusion.2.refs_0_, ...), custom_call_target="tpu_custom_call" | custom-call | flops 4026531840 | bytes 13500416 | tf_op jit(solution)/shard_map/pallas_call | solution.py:226
  123.4 2.5 %shard_map.77 = bf16[6,32,2048]{2,1,0:T(8,128)(2,1)S(1)} custom-call(s32[6]{0:T(128)S(1)} %compare_convert_fusion.which_ref, s32[6]{0:T(128)S(1)} %get-tuple-element.63.first_ref, s32[6]{0:T(128)S(1)} %compare_select_fusion.second_ref, bf16[8,64,2048]{2,1,0:T(8,128)(2,1)S(1)} %copy-done.4, bf16[5,32,2048]{2,1,0:T(8,128)(2,1)} %collective-permute-done.13.b_ref), custom_call_target="tpu_custom_call" | custom-call | bytes 2359296 | tf_op jit(solution)/shard_map/pallas_call | solution.py:126
  128.8 2.0 %collective-permute-start.24 = (bf16[512,384]{1,0:T(8,128)(2,1)S(1)}, bf16[512,384]{1,0:T(8,128)(2,1)S(1)}, u32[]{:S(2)}, u32[]{:S(2)}) collective-permute-start(bf16[512,384]{1,0:T(8,128)(2,1)S(1)} %collective-permute-done.18.refs_1_), channel_id=1, source_target_pairs={{0,4},{4,8},{8,12},{12,14},{14,10},{10,6},{6,2},{2,0},{1,5},{5,9},... | collective-permute-start | bytes 1179656 | tf_op jit(solution)/shard_map/ppermute | solution.py:336
  130.8 9.8 %shard_map.78.refs_0_ = f32[768,640]{1,0:T(8,128)} custom-call(s32[10]{0:T(128)S(1)} %pad_add_fusion.1.at, bf16[768,2048]{1,0:T(8,128)(2,1)} %same_ref.1, bf16[768,2048]{1,0:T(8,128)(2,1)} %collective-permute-done.3.swapped_ref, bf16[512,640]{1,0:T(8,128)(2,1)S(1)} %constant_dynamic-slice_fusion.2.refs_0_, bf16[512,640]{1,0:T(8,128)(2,1)} %collective-permute-done.4.refs_1_, ...), custom_call_target="tpu_custom_call" | custom-call | flops 4026531840 | bytes 13500416 | tf_op jit(solution)/shard_map/pallas_call | solution.py:226
  140.6 5.1 %shard_map.79.la = f32[768,64]{1,0:T(8,128)S(1)} custom-call(s32[3,6]{1,0:T(4,128)S(1)} %pad_add_fusion.table_ref, bf16[768,2048]{1,0:T(8,128)(2,1)} %same_ref.1, bf16[8,64,2048]{2,1,0:T(8,128)(2,1)S(1)} %bitcast.25, bf16[6,32,2048]{2,1,0:T(8,128)(2,1)S(1)} %copy-done.6, bf16[6,32,2048]{2,1,0:T(8,128)(2,1)} %collective-permute-done.17.refs_1_), custom_call_target="tpu_custom_call" | custom-call | flops 201326592 | bytes 5242880 | tf_op jit(solution)/shard_map/pallas_call | solution.py:177
  145.7 2.5 %shard_map.80 = bf16[6,32,2048]{2,1,0:T(8,128)(2,1)S(1)} custom-call(s32[6]{0:T(128)S(1)} %compare_convert_fusion.which_ref, s32[6]{0:T(128)S(1)} %get-tuple-element.63.first_ref, s32[6]{0:T(128)S(1)} %compare_select_fusion.second_ref, bf16[8,64,2048]{2,1,0:T(8,128)(2,1)S(1)} %copy-done.4, bf16[5,32,2048]{2,1,0:T(8,128)(2,1)} %collective-permute-done.22.b_ref), custom_call_target="tpu_custom_call" | custom-call | bytes 2359296 | tf_op jit(solution)/shard_map/pallas_call | solution.py:126
  148.2 2.7 %collective-permute-done.21.refs_4_ = bf16[512,384]{1,0:T(8,128)(2,1)S(1)} collective-permute-done((bf16[512,384]{1,0:T(8,128)(2,1)S(1)}, bf16[512,384]{1,0:T(8,128)(2,1)S(1)}, u32[]{:S(2)}, u32[]{:S(2)}) %collective-permute-start.21) | collective-permute-done | bytes 393248 | tf_op jit(solution)/shard_map/ppermute | solution.py:336
  155.7 6.1 %collective-permute-done.25.refs_6_ = bf16[512,384]{1,0:T(8,128)(2,1)S(1)} collective-permute-done((bf16[512,384]{1,0:T(8,128)(2,1)S(1)}, bf16[512,384]{1,0:T(8,128)(2,1)S(1)}, u32[]{:S(2)}, u32[]{:S(2)}) %collective-permute-start.25) | collective-permute-done | bytes 393248 | tf_op jit(solution)/shard_map/ppermute | solution.py:336
  161.9 2.2 %collective-permute-done.26.refs_5_ = bf16[512,384]{1,0:T(8,128)(2,1)S(1)} collective-permute-done((bf16[512,384]{1,0:T(8,128)(2,1)S(1)}, bf16[512,384]{1,0:T(8,128)(2,1)S(1)}, u32[]{:S(2)}, u32[]{:S(2)}) %collective-permute-start.26) | collective-permute-done | bytes 393248 | tf_op jit(solution)/shard_map/ppermute | solution.py:336
  164.4 1.7 collective-permute-start.28
  166.8 5.2 %collective-permute-done.27.refs_7_ = bf16[256,384]{1,0:T(8,128)(2,1)S(1)} collective-permute-done((bf16[256,384]{1,0:T(8,128)(2,1)S(1)}, bf16[256,384]{1,0:T(8,128)(2,1)S(1)}, u32[]{:S(2)}, u32[]{:S(2)}) %collective-permute-start.27) | collective-permute-done | bytes 196640 | tf_op jit(solution)/shard_map/ppermute | solution.py:336
  171.9 6.5 %shard_map.81 = bf16[768,384]{1,0:T(8,128)(2,1)S(1)} custom-call(s32[10]{0:T(128)S(1)} %pad_add_fusion.1.at, bf16[768,2048]{1,0:T(8,128)(2,1)} %collective-permute-done.12.same_ref, bf16[768,2048]{1,0:T(8,128)(2,1)} %collective-permute-done.16.swapped_ref, bf16[512,384]{1,0:T(8,128)(2,1)S(1)} %constant_dynamic-slice_fusion.refs_0_, ...), custom_call_target="tpu_custom_call" | custom-call | flops 2415919104 | bytes 10616832 | tf_op jit(solution)/shard_map/pallas_call | solution.py:226
  178.8 6.5 %shard_map.82.refs_1_ = f32[768,384]{1,0:T(8,128)S(1)} custom-call(s32[10]{0:T(128)S(1)} %pad_add_fusion.1.at, bf16[768,2048]{1,0:T(8,128)(2,1)} %same_ref.1, bf16[768,2048]{1,0:T(8,128)(2,1)} %collective-permute-done.3.swapped_ref, bf16[512,384]{1,0:T(8,128)(2,1)S(1)} %constant_dynamic-slice_fusion.refs_0_, ...), custom_call_target="tpu_custom_call" | custom-call | flops 2415919104 | bytes 10616832 | tf_op jit(solution)/shard_map/pallas_call | solution.py:226
  186.4 3.0 %collective-permute-done.30.refs_3_ = bf16[768,384]{1,0:T(8,128)(2,1)S(1)} collective-permute-done((bf16[768,384]{1,0:T(8,128)(2,1)S(1)}, bf16[768,384]{1,0:T(8,128)(2,1)S(1)}, u32[]{:S(2)}, u32[]{:S(2)}) %collective-permute-start.30) | collective-permute-done | bytes 589856 | tf_op jit(solution)/shard_map/ppermute | solution.py:337
  189.4 6.4 %shard_map.83 = bf16[768,2048]{1,0:T(8,128)(2,1)} custom-call(s32[3,6]{1,0:T(4,128)S(1)} %pad_add_fusion.table_ref, s32[6]{0:T(128)S(1)} %copy-done.13, s32[1]{0:T(128)} %bitcast.3.half_ref, f32[768,64]{1,0:T(8,128)S(1)} %shard_map.79.la, f32[768,64]{1,0:T(8,128)S(1)} %collective-permute-done.20.lb, f32[768,640]{1,0:T(8,128)} %shard_map.78.refs_0_, ...), custom_call_target="tpu_custom_call" | custom-call | flops 201326592 | bytes 9961472 | tf_op jit(solution)/shard_map/pallas_call | solution.py:291
  (102 shorter events, 28.8 us)
Async XLA Ops:
  0.0 25.8 %collective-permute-start.3 = (bf16[768,2048]{1,0:T(8,128)(2,1)}, bf16[768,2048]{1,0:T(8,128)(2,1)}, u32[]{:S(2)}, u32[]{:S(2)}) collective-permute-start(bf16[768,2048]{1,0:T(8,128)(2,1)} %same_ref.1), channel_id=1, source_target_pairs={{0,1},{1,0},{2,3},{3,2},{4,5},{5,4},{6,7},{7,6},{8,9},{9,8},{10,11... | collective-permute-start | bytes 9437192 | tf_op jit(solution)/shard_map/ppermute | solution.py:338
  0.5 71.6 %collective-permute-start.12 = (bf16[768,2048]{1,0:T(8,128)(2,1)}, bf16[768,2048]{1,0:T(8,128)(2,1)}, u32[]{:S(2)}, u32[]{:S(2)}) collective-permute-start(bf16[768,2048]{1,0:T(8,128)(2,1)} %same_ref.1), channel_id=1, source_target_pairs={{0,16},{16,0},{1,17},{17,1},{2,18},{18,2},{3,19},{19,3},{4,20},{20... | collective-permute-start | bytes 9437192 | tf_op jit(solution)/shard_map/ppermute | solution.py:337
  3.0 6.7 %collective-permute-start.1 = (s32[6]{0:T(128)}, s32[6]{0:T(128)S(1)}, u32[]{:S(2)}, u32[]{:S(2)}) collective-permute-start(s32[6]{0:T(128)} %param.11), channel_id=1, source_target_pairs={{0,14},{2,4},{4,2},{6,8},{8,6},{10,12},{12,10},{14,0},{1,15},{3,5}... | collective-permute-start | bytes 80 | tf_op jit(solution)/shard_map/ppermute | solution.py:336
  7.6 10.0 %collective-permute-start = (s32[6]{0:T(128)}, s32[6]{0:T(128)S(1)}, u32[]{:S(2)}, u32[]{:S(2)}) collective-permute-start(s32[6]{0:T(128)} %param.11), channel_id=1, source_target_pairs={{0,2},{2,0},{4,6},{6,4},{8,10},{10,8},{12,14},{14,12},{1,3},{3,1},... | collective-permute-start | bytes 80 | tf_op jit(solution)/shard_map/ppermute | solution.py:336
  7.7 17.8 %collective-permute-start.5 = (bf16[512,640]{1,0:T(8,128)(2,1)S(1)}, bf16[512,640]{1,0:T(8,128)(2,1)}, u32[]{:S(2)}, u32[]{:S(2)}) collective-permute-start(bf16[512,640]{1,0:T(8,128)(2,1)S(1)} %constant_dynamic-slice_fusion.2.refs_0_), channel_id=1, source_target_pairs={{4,0},{8,4},{12,8},{14,12},{10,14},{6,10},{2,6},{0,2},{5,1},{9,5},... | collective-permute-start | bytes 1966088 | tf_op jit(solution)/shard_map/ppermute | solution.py:336
  9.7 16.1 %collective-permute-start.4 = (bf16[512,640]{1,0:T(8,128)(2,1)S(1)}, bf16[512,640]{1,0:T(8,128)(2,1)}, u32[]{:S(2)}, u32[]{:S(2)}) collective-permute-start(bf16[512,640]{1,0:T(8,128)(2,1)S(1)} %constant_dynamic-slice_fusion.2.refs_0_), channel_id=1, source_target_pairs={{0,4},{4,8},{8,12},{12,14},{14,10},{10,6},{6,2},{2,0},{1,5},{5,9},... | collective-permute-start | bytes 1966088 | tf_op jit(solution)/shard_map/ppermute | solution.py:336
  17.6 21.8 %collective-permute-start.2 = (bf16[5,32,2048]{2,1,0:T(8,128)(2,1)}, bf16[5,32,2048]{2,1,0:T(8,128)(2,1)S(1)}, u32[]{:S(2)}, u32[]{:S(2)}) collective-permute-start(bf16[5,32,2048]{2,1,0:T(8,128)(2,1)} %get-tuple-element.34), channel_id=1, source_target_pairs={{0,12},{2,6},{4,0},{6,10},{8,4},{10,14},{12,8},{14,2},{1,13},{3,7}... | collective-permute-start | bytes 1966088 | tf_op jit(solution)/shard_map/ppermute | solution.py:336
  25.8 27.7 %collective-permute-start.8 = (bf16[512,640]{1,0:T(8,128)(2,1)}, bf16[512,640]{1,0:T(8,128)(2,1)}, u32[]{:S(2)}, u32[]{:S(2)}) collective-permute-start(bf16[512,640]{1,0:T(8,128)(2,1)} %collective-permute-done.4.refs_1_), channel_id=1, source_target_pairs={{0,4},{4,8},{8,12},{12,14},{14,10},{10,6},{6,2},{2,0},{1,5},{5,9},... | collective-permute-start | bytes 1966088 | tf_op jit(solution)/shard_map/ppermute | solution.py:336
  27.5 26.0 %collective-permute-start.10 = (bf16[512,640]{1,0:T(8,128)(2,1)}, bf16[512,640]{1,0:T(8,128)(2,1)}, u32[]{:S(2)}, u32[]{:S(2)}) collective-permute-start(bf16[512,640]{1,0:T(8,128)(2,1)} %collective-permute-done.5.refs_2_), channel_id=1, source_target_pairs={{4,0},{8,4},{12,8},{14,12},{10,14},{6,10},{2,6},{0,2},{5,1},{9,5},... | collective-permute-start | bytes 1966088 | tf_op jit(solution)/shard_map/ppermute | solution.py:336
  41.7 25.7 %collective-permute-start.6 = (bf16[6,32,2048]{2,1,0:T(8,128)(2,1)S(1)}, bf16[6,32,2048]{2,1,0:T(8,128)(2,1)S(1)}, u32[]{:S(2)}, u32[]{:S(2)}) collective-permute-start(bf16[6,32,2048]{2,1,0:T(8,128)(2,1)S(1)} %shard_map.74), channel_id=1, source_target_pairs={{0,2},{2,0},{4,6},{6,4},{8,10},{10,8},{12,14},{14,12},{1,3},{3,1},... | collective-permute-start | bytes 2359304 | tf_op jit(solution)/shard_map/ppermute | solution.py:336
  46.7 20.8 %collective-permute-start.7 = (bf16[5,32,2048]{2,1,0:T(8,128)(2,1)S(1)}, bf16[5,32,2048]{2,1,0:T(8,128)(2,1)S(1)}, u32[]{:S(2)}, u32[]{:S(2)}) collective-permute-start(bf16[5,32,2048]{2,1,0:T(8,128)(2,1)S(1)} %copy-done.16), channel_id=1, source_target_pairs={{0,12},{2,6},{4,0},{6,10},{8,4},{10,14},{12,8},{14,2},{1,13},{3,7}... | collective-permute-start | bytes 1966088 | tf_op jit(solution)/shard_map/ppermute | solution.py:336
  53.5 26.4 %collective-permute-start.9 = (bf16[512,640]{1,0:T(8,128)(2,1)}, bf16[512,640]{1,0:T(8,128)(2,1)S(1)}, u32[]{:S(2)}, u32[]{:S(2)}) collective-permute-start(bf16[512,640]{1,0:T(8,128)(2,1)} %collective-permute-done.8.refs_3_), channel_id=1, source_target_pairs={{0,4},{4,8},{8,12},{12,14},{14,10},{10,6},{6,2},{2,0},{1,5},{5,9},... | collective-permute-start | bytes 1966088 | tf_op jit(solution)/shard_map/ppermute | solution.py:336
  55.6 24.8 %collective-permute-start.11 = (bf16[512,640]{1,0:T(8,128)(2,1)}, bf16[512,640]{1,0:T(8,128)(2,1)S(1)}, u32[]{:S(2)}, u32[]{:S(2)}) collective-permute-start(bf16[512,640]{1,0:T(8,128)(2,1)} %collective-permute-done.10.refs_4_), channel_id=1, source_target_pairs={{4,0},{8,4},{12,8},{14,12},{10,14},{6,10},{2,6},{0,2},{5,1},{9,5},... | collective-permute-start | bytes 1966088 | tf_op jit(solution)/shard_map/ppermute | solution.py:336
  80.4 31.1 %collective-permute-start.16 = (bf16[768,2048]{1,0:T(8,128)(2,1)}, bf16[768,2048]{1,0:T(8,128)(2,1)}, u32[]{:S(2)}, u32[]{:S(2)}) collective-permute-start(bf16[768,2048]{1,0:T(8,128)(2,1)} %collective-permute-done.12.same_ref), channel_id=1, source_target_pairs={{0,1},{1,0},{2,3},{3,2},{4,5},{5,4},{6,7},{7,6},{8,9},{9,8},{10,11... | collective-permute-start | bytes 9437192 | tf_op jit(solution)/shard_map/ppermute | solution.py:338
  81.2 42.2 %collective-permute-start.17 = (bf16[6,32,2048]{2,1,0:T(8,128)(2,1)S(1)}, bf16[6,32,2048]{2,1,0:T(8,128)(2,1)}, u32[]{:S(2)}, u32[]{:S(2)}) collective-permute-start(bf16[6,32,2048]{2,1,0:T(8,128)(2,1)S(1)} %shard_map.75), channel_id=1, source_target_pairs={{0,2},{2,0},{4,6},{6,4},{8,10},{10,8},{12,14},{14,12},{1,3},{3,1},... | collective-permute-start | bytes 2359304 | tf_op jit(solution)/shard_map/ppermute | solution.py:336
  88.5 20.9 %collective-permute-start.14 = (bf16[256,640]{1,0:T(8,128)(2,1)}, bf16[256,640]{1,0:T(8,128)(2,1)}, u32[]{:S(2)}, u32[]{:S(2)}) collective-permute-start(bf16[256,640]{1,0:T(8,128)(2,1)} %slice.16), channel_id=1, source_target_pairs={{0,4},{4,8},{8,12},{12,14},{14,10},{10,6},{6,2},{2,0},{1,5},{5,9},... | collective-permute-start | bytes 983048 | tf_op jit(solution)/shard_map/ppermute | solution.py:336
  89.4 20.1 %collective-permute-start.15 = (bf16[256,640]{1,0:T(8,128)(2,1)}, bf16[256,640]{1,0:T(8,128)(2,1)}, u32[]{:S(2)}, u32[]{:S(2)}) collective-permute-start(bf16[256,640]{1,0:T(8,128)(2,1)} %slice.17), channel_id=1, source_target_pairs={{4,0},{8,4},{12,8},{14,12},{10,14},{6,10},{2,6},{0,2},{5,1},{9,5},... | collective-permute-start | bytes 983048 | tf_op jit(solution)/shard_map/ppermute | solution.py:336
  90.5 32.9 %collective-permute-start.13 = (bf16[5,32,2048]{2,1,0:T(8,128)(2,1)}, bf16[5,32,2048]{2,1,0:T(8,128)(2,1)}, u32[]{:S(2)}, u32[]{:S(2)}) collective-permute-start(bf16[5,32,2048]{2,1,0:T(8,128)(2,1)} %copy-done.14), channel_id=1, source_target_pairs={{0,12},{2,6},{4,0},{6,10},{8,4},{10,14},{12,8},{14,2},{1,13},{3,7}... | collective-permute-start | bytes 1966088 | tf_op jit(solution)/shard_map/ppermute | solution.py:336
  109.5 19.2 %collective-permute-start.19 = (bf16[512,384]{1,0:T(8,128)(2,1)S(1)}, bf16[512,384]{1,0:T(8,128)(2,1)S(1)}, u32[]{:S(2)}, u32[]{:S(2)}) collective-permute-start(bf16[512,384]{1,0:T(8,128)(2,1)S(1)} %constant_dynamic-slice_fusion.refs_0_), channel_id=1, source_target_pairs={{4,0},{8,4},{12,8},{14,12},{10,14},{6,10},{2,6},{0,2},{5,1},{9,5},... | collective-permute-start | bytes 1179656 | tf_op jit(solution)/shard_map/ppermute | solution.py:336
  109.5 19.2 %collective-permute-start.18 = (bf16[512,384]{1,0:T(8,128)(2,1)S(1)}, bf16[512,384]{1,0:T(8,128)(2,1)S(1)}, u32[]{:S(2)}, u32[]{:S(2)}) collective-permute-start(bf16[512,384]{1,0:T(8,128)(2,1)S(1)} %constant_dynamic-slice_fusion.refs_0_), channel_id=1, source_target_pairs={{0,4},{4,8},{8,12},{12,14},{14,10},{10,6},{6,2},{2,0},{1,5},{5,9},... | collective-permute-start | bytes 1179656 | tf_op jit(solution)/shard_map/ppermute | solution.py:336
  126.0 26.3 %collective-permute-start.23 = (bf16[6,32,2048]{2,1,0:T(8,128)(2,1)S(1)}, bf16[6,32,2048]{2,1,0:T(8,128)(2,1)S(1)}, u32[]{:S(2)}, u32[]{:S(2)}) collective-permute-start(bf16[6,32,2048]{2,1,0:T(8,128)(2,1)S(1)} %shard_map.77), channel_id=1, source_target_pairs={{0,2},{2,0},{4,6},{6,4},{8,10},{10,8},{12,14},{14,12},{1,3},{3,1},... | collective-permute-start | bytes 2359304 | tf_op jit(solution)/shard_map/ppermute | solution.py:336
  126.9 18.8 %collective-permute-start.22 = (bf16[5,32,2048]{2,1,0:T(8,128)(2,1)}, bf16[5,32,2048]{2,1,0:T(8,128)(2,1)}, u32[]{:S(2)}, u32[]{:S(2)}) collective-permute-start(bf16[5,32,2048]{2,1,0:T(8,128)(2,1)} %get-tuple-element.53), channel_id=1, source_target_pairs={{0,12},{2,6},{4,0},{6,10},{8,4},{10,14},{12,8},{14,2},{1,13},{3,7}... | collective-permute-start | bytes 1966088 | tf_op jit(solution)/shard_map/ppermute | solution.py:336
  128.7 22.3 %collective-permute-start.21 = (bf16[512,384]{1,0:T(8,128)(2,1)S(1)}, bf16[512,384]{1,0:T(8,128)(2,1)S(1)}, u32[]{:S(2)}, u32[]{:S(2)}) collective-permute-start(bf16[512,384]{1,0:T(8,128)(2,1)S(1)} %collective-permute-done.19.refs_2_), channel_id=1, source_target_pairs={{4,0},{8,4},{12,8},{14,12},{10,14},{6,10},{2,6},{0,2},{5,1},{9,5},... | collective-permute-start | bytes 1179656 | tf_op jit(solution)/shard_map/ppermute | solution.py:336
  128.8 23.5 %collective-permute-start.24 = (bf16[512,384]{1,0:T(8,128)(2,1)S(1)}, bf16[512,384]{1,0:T(8,128)(2,1)S(1)}, u32[]{:S(2)}, u32[]{:S(2)}) collective-permute-start(bf16[512,384]{1,0:T(8,128)(2,1)S(1)} %collective-permute-done.18.refs_1_), channel_id=1, source_target_pairs={{0,4},{4,8},{8,12},{12,14},{14,10},{10,6},{6,2},{2,0},{1,5},{5,9},... | collective-permute-start | bytes 1179656 | tf_op jit(solution)/shard_map/ppermute | solution.py:336
  152.3 9.5 %collective-permute-start.25 = (bf16[512,384]{1,0:T(8,128)(2,1)S(1)}, bf16[512,384]{1,0:T(8,128)(2,1)S(1)}, u32[]{:S(2)}, u32[]{:S(2)}) collective-permute-start(bf16[512,384]{1,0:T(8,128)(2,1)S(1)} %collective-permute-done.21.refs_4_), channel_id=1, source_target_pairs={{4,0},{8,4},{12,8},{14,12},{10,14},{6,10},{2,6},{0,2},{5,1},{9,5},... | collective-permute-start | bytes 1179656 | tf_op jit(solution)/shard_map/ppermute | solution.py:336
  153.4 10.6 %collective-permute-start.26 = (bf16[512,384]{1,0:T(8,128)(2,1)S(1)}, bf16[512,384]{1,0:T(8,128)(2,1)S(1)}, u32[]{:S(2)}, u32[]{:S(2)}) collective-permute-start(bf16[512,384]{1,0:T(8,128)(2,1)S(1)} %collective-permute-done.24.refs_3_), channel_id=1, source_target_pairs={{0,4},{4,8},{8,12},{12,14},{14,10},{10,6},{6,2},{2,0},{1,5},{5,9},... | collective-permute-start | bytes 1179656 | tf_op jit(solution)/shard_map/ppermute | solution.py:336
  154.3 24.4 %collective-permute-start.29 = (bf16[768,640]{1,0:T(8,128)(2,1)S(1)}, bf16[768,640]{1,0:T(8,128)(2,1)S(1)}, u32[]{:S(2)}, u32[]{:S(2)}) collective-permute-start(bf16[768,640]{1,0:T(8,128)(2,1)S(1)} %copy-done.18), channel_id=1, source_target_pairs={{0,16},{16,0},{1,17},{17,1},{2,18},{18,2},{3,19},{19,3},{4,20},{20... | collective-permute-start | bytes 2949128 | tf_op jit(solution)/shard_map/ppermute | solution.py:337
  164.1 7.9 %collective-permute-start.27 = (bf16[256,384]{1,0:T(8,128)(2,1)S(1)}, bf16[256,384]{1,0:T(8,128)(2,1)S(1)}, u32[]{:S(2)}, u32[]{:S(2)}) collective-permute-start(bf16[256,384]{1,0:T(8,128)(2,1)S(1)} %slice.18), channel_id=1, source_target_pairs={{0,4},{4,8},{8,12},{12,14},{14,10},{10,6},{6,2},{2,0},{1,5},{5,9},... | collective-permute-start | bytes 589832 | tf_op jit(solution)/shard_map/ppermute | solution.py:336
  164.4 7.6 %collective-permute-start.28 = (bf16[256,384]{1,0:T(8,128)(2,1)S(1)}, bf16[256,384]{1,0:T(8,128)(2,1)S(1)}, u32[]{:S(2)}, u32[]{:S(2)}) collective-permute-start(bf16[256,384]{1,0:T(8,128)(2,1)S(1)} %slice.19), channel_id=1, source_target_pairs={{4,0},{8,4},{12,8},{14,12},{10,14},{6,10},{2,6},{0,2},{5,1},{9,5},... | collective-permute-start | bytes 589832 | tf_op jit(solution)/shard_map/ppermute | solution.py:336
  166.1 20.3 %collective-permute-start.31 = (bf16[6,32,2048]{2,1,0:T(8,128)(2,1)S(1)}, bf16[6,32,2048]{2,1,0:T(8,128)(2,1)S(1)}, u32[]{:S(2)}, u32[]{:S(2)}) collective-permute-start(bf16[6,32,2048]{2,1,0:T(8,128)(2,1)S(1)} %shard_map.80), channel_id=1, source_target_pairs={{0,2},{2,0},{4,6},{6,4},{8,10},{10,8},{12,14},{14,12},{1,3},{3,1},... | collective-permute-start | bytes 2359304 | tf_op jit(solution)/shard_map/ppermute | solution.py:336
  178.5 11.0 %collective-permute-start.30 = (bf16[768,384]{1,0:T(8,128)(2,1)S(1)}, bf16[768,384]{1,0:T(8,128)(2,1)S(1)}, u32[]{:S(2)}, u32[]{:S(2)}) collective-permute-start(bf16[768,384]{1,0:T(8,128)(2,1)S(1)} %shard_map.81), channel_id=1, source_target_pairs={{0,16},{16,0},{1,17},{17,1},{2,18},{18,2},{3,19},{19,3},{4,20},{20... | collective-permute-start | bytes 1769480 | tf_op jit(solution)/shard_map/ppermute | solution.py:337
  178.8 6.5 %collective-permute-start.20 = (f32[768,64]{1,0:T(8,128)S(1)}, f32[768,64]{1,0:T(8,128)S(1)}, u32[]{:S(2)}, u32[]{:S(2)}) collective-permute-start(f32[768,64]{1,0:T(8,128)S(1)} %shard_map.79.la), channel_id=1, source_target_pairs={{0,1},{1,0},{2,3},{3,2},{4,5},{5,4},{6,7},{7,6},{8,9},{9,8},{10,11... | collective-permute-start | bytes 589832 | tf_op jit(solution)/shard_map/ppermute | solution.py:338
  (19 other events, 128.2 us)

commit v4 on v3

--- a/solution.py
+++ b/solution.py
@@ -22,10 +22,10 @@
     ("swap_done", 0),
     ("ring_done", 0),
     ("ring", 0),
-    ("lift_done", 0),
     ("across", 0),
     ("lift", 1),
     ("ring", 0),
+    ("lift_done", 0),
     ("across_done", 0),
     ("lift_done", 1),
     ("across", 1),
@@ -34,29 +34,33 @@
     ("tokens_done", 0),
     ("lift", 2),
     ("ring", 1),
+    ("tokens_done", 0),
     ("ring", 0),
     ("ring_done", 0),
     ("base", 0),
-    ("lift_done", 2),
-    ("across_done", 1),
     ("across", 2),
-    ("lift", 3),
     ("ring_done", 1),
     ("ring_done", 1),
+    ("lift", 3),
+    ("swap_done", 0),
     ("ring", 1),
     ("keep", 0),
+    ("swap_done", 1),
     ("low", 0),
-    ("lift_done", 3),
+    ("ring", 1),
     ("across", 3),
     ("across_done", 2),
+    ("swap_done", 1),
     ("ring_done", 1),
+    ("lift_done", 3),
     ("ring", 1),
+    ("tokens_done", 0),
+    ("ring_done", 0),
+    ("tokens_done", 0),
     ("ring_done", 1),
-    ("ring", 1),
+    ("base_done", 0),
     ("ring_done", 1),
     ("base", 1),
-    ("base_done", 0),
-    ("base_done", 0),
     ("keep", 1),
 ]
 

time: 196 us -> 192 us (0.980)
  waiting for transfers between devices: 84.2 us -> 79.3 us
  local copies, waits for them, and re-layouts: 12.2 us -> 9.93 us
    ppermute x26, waiting for transfers between devices: 77.4 us -> 72 us  [local(): rep = lambda a, route: lax.ppermute(a, 'replica', route)]
    unnamed x38 -> x26, local copies, waits for them, and re-layouts: 7.95 us -> 5.07 us
    ppermute x26, starting transfers between devices: 39.1 us -> 41.3 us  [local(): rep = lambda a, route: lax.ppermute(a, 'replica', route)]
  transfers between devices with their start and end apart: 32 -> 32, of which waited for: 16 -> 17; matrix products, arithmetic and copies ran while one was open for 3% -> 3% of each run, Pallas kernels for 25% -> 25%
where the time goes in v4:
time: 192 us; the launch traced here: 191 us
  waiting for transfers between devices  79.3 us (41%)
  Pallas kernels  55.3 us (29%)
  starting transfers between devices  45.4 us (24%)
  local copies, waits for them, and re-layouts  9.93 us (5%)
    ppermute x26, waiting for transfers between devices, local(): rep = lambda a, route: lax.ppermute(a, 'replica', route)  72 us
    ppermute x26, starting transfers between devices, local(): rep = lambda a, route: lax.ppermute(a, 'replica', route)  41.3 us
    pallas_call x4, Pallas kernels, product(): pl.pallas_call(body, grid_spec=pltpu.PrefetchScalarGridSpec(num_scalar_pr...  33.4 us
    ppermute x3, waiting for transfers between devices, local(): lax.ppermute(a, 'groups', [(i, i ^ 1) for i in range(groups)])  7.32 us
    pallas_call x4, Pallas kernels, pick_two(): pl.pallas_call(body, grid_spec=pltpu.PrefetchScalarGridSpec(num_scalar_pr...  6.63 us
    pallas_call x1, Pallas kernels, finish(): pl.pallas_call(body, grid_spec=pltpu.PrefetchScalarGridSpec(num_scalar_pr...  6.6 us
    unnamed x26, local copies, waits for them, and re-layouts  5.07 us
    pallas_call x1, Pallas kernels, low_partial(): pl.pallas_call(body, grid_spec=pltpu.PrefetchScalarGridSpec(num_scalar_pr...  4.98 us
  transfers between devices with their start and end apart: 32, of which 17 were waited for; matrix products, arithmetic and copies ran while one was open for 3% of the time, Pallas kernels for 25%

profile of v4, /device:TPU:0, one launch (start us, length us, event | category | flops | bytes accessed | tf_op | source)
XLA Modules:
  0.0 191.5 jit_solution(17095989653108811807)
XLA Ops:
  0.5 2.6 %collective-permute-start.12 = (bf16[768,2048]{1,0:T(8,128)(2,1)}, bf16[768,2048]{1,0:T(8,128)(2,1)}, u32[]{:S(2)}, u32[]{:S(2)}) collective-permute-start(bf16[768,2048]{1,0:T(8,128)(2,1)} %same_ref.1), channel_id=1, source_target_pairs={{0,16},{16,0},{1,17},{17,1},{2,18},{18,2},{3,19},{19,3},{4,20},{20... | collective-permute-start | bytes 9437192 | tf_op jit(solution)/shard_map/ppermute | solution.py:341
  3.0 4.6 %collective-permute-start.1 = (s32[6]{0:T(128)}, s32[6]{0:T(128)S(1)}, u32[]{:S(2)}, u32[]{:S(2)}) collective-permute-start(s32[6]{0:T(128)} %param.11), channel_id=1, source_target_pairs={{0,14},{2,4},{4,2},{6,8},{8,6},{10,12},{12,10},{14,0},{1,15},{3,5}... | collective-permute-start | bytes 80 | tf_op jit(solution)/shard_map/ppermute | solution.py:340
  7.7 2.1 %collective-permute-start.5 = (bf16[512,640]{1,0:T(8,128)(2,1)S(1)}, bf16[512,640]{1,0:T(8,128)(2,1)}, u32[]{:S(2)}, u32[]{:S(2)}) collective-permute-start(bf16[512,640]{1,0:T(8,128)(2,1)S(1)} %constant_dynamic-slice_fusion.1.refs_0_), channel_id=1, source_target_pairs={{4,0},{8,4},{12,8},{14,12},{10,14},{6,10},{2,6},{0,2},{5,1},{9,5},... | collective-permute-start | bytes 1966088 | tf_op jit(solution)/shard_map/ppermute | solution.py:340
  11.7 3.7 %shard_map.73 = (bf16[5,32,2048]{2,1,0:T(8,128)(2,1)}, bf16[5,32,2048]{2,1,0:T(8,128)(2,1)S(1)}, bf16[5,32,2048]{2,1,0:T(8,128)(2,1)S(1)}, bf16[5,32,2048]{2,1,0:T(8,128)(2,1)}) custom-call(s32[5]{0:T(128)S(1)} %select_reduce_fusion.at, bf16[8,64,2048]{2,1,0:T(8,128)(2,1)S(1)} %bitcast.22, bf16[8,64,2048]{2,1,0:T(8,128)(2,1)} %refs_4_.1), custom_call_target="tpu_custom_call" | custom-call | bytes 5242880 | tf_op jit(solution)/shard_map/pallas_call | solution.py:99
  17.1 5.2 %collective-permute-start.2 = (bf16[5,32,2048]{2,1,0:T(8,128)(2,1)}, bf16[5,32,2048]{2,1,0:T(8,128)(2,1)S(1)}, u32[]{:S(2)}, u32[]{:S(2)}) collective-permute-start(bf16[5,32,2048]{2,1,0:T(8,128)(2,1)} %get-tuple-element.33), channel_id=1, source_target_pairs={{0,12},{2,6},{4,0},{6,10},{8,4},{10,14},{12,8},{14,2},{1,13},{3,7}... | collective-permute-start | bytes 1966088 | tf_op jit(solution)/shard_map/ppermute | solution.py:340
  22.3 3.1 %collective-permute-done.5.refs_2_ = bf16[512,640]{1,0:T(8,128)(2,1)} collective-permute-done((bf16[512,640]{1,0:T(8,128)(2,1)S(1)}, bf16[512,640]{1,0:T(8,128)(2,1)}, u32[]{:S(2)}, u32[]{:S(2)}) %collective-permute-start.5) | collective-permute-done | bytes 655392 | tf_op jit(solution)/shard_map/ppermute | solution.py:340
  28.0 11.3 %collective-permute-done.2.b_ref = bf16[5,32,2048]{2,1,0:T(8,128)(2,1)S(1)} collective-permute-done((bf16[5,32,2048]{2,1,0:T(8,128)(2,1)}, bf16[5,32,2048]{2,1,0:T(8,128)(2,1)S(1)}, u32[]{:S(2)}, u32[]{:S(2)}) %collective-permute-start.2) | collective-permute-done | bytes 655392 | tf_op jit(solution)/shard_map/ppermute | solution.py:340
  41.7 4.9 %collective-permute-start.6 = (bf16[6,32,2048]{2,1,0:T(8,128)(2,1)S(1)}, bf16[6,32,2048]{2,1,0:T(8,128)(2,1)S(1)}, u32[]{:S(2)}, u32[]{:S(2)}) collective-permute-start(bf16[6,32,2048]{2,1,0:T(8,128)(2,1)S(1)} %shard_map.74), channel_id=1, source_target_pairs={{0,2},{2,0},{4,6},{6,4},{8,10},{10,8},{12,14},{14,12},{1,3},{3,1},... | collective-permute-start | bytes 2359304 | tf_op jit(solution)/shard_map/ppermute | solution.py:340
  46.7 6.8 %collective-permute-done.10.refs_4_ = bf16[512,640]{1,0:T(8,128)(2,1)} collective-permute-done((bf16[512,640]{1,0:T(8,128)(2,1)}, bf16[512,640]{1,0:T(8,128)(2,1)}, u32[]{:S(2)}, u32[]{:S(2)}) %collective-permute-start.10) | collective-permute-done | bytes 655392 | tf_op jit(solution)/shard_map/ppermute | solution.py:340
  53.5 2.1 %collective-permute-start.9 = (bf16[512,640]{1,0:T(8,128)(2,1)}, bf16[512,640]{1,0:T(8,128)(2,1)}, u32[]{:S(2)}, u32[]{:S(2)}) collective-permute-start(bf16[512,640]{1,0:T(8,128)(2,1)} %collective-permute-done.8.refs_3_), channel_id=1, source_target_pairs={{0,4},{4,8},{8,12},{12,14},{14,10},{10,6},{6,2},{2,0},{1,5},{5,9},... | collective-permute-start | bytes 1966088 | tf_op jit(solution)/shard_map/ppermute | solution.py:340
  55.8 11.6 %collective-permute-done.7.b_ref = bf16[5,32,2048]{2,1,0:T(8,128)(2,1)S(1)} collective-permute-done((bf16[5,32,2048]{2,1,0:T(8,128)(2,1)S(1)}, bf16[5,32,2048]{2,1,0:T(8,128)(2,1)S(1)}, u32[]{:S(2)}, u32[]{:S(2)}) %collective-permute-start.7) | collective-permute-done | bytes 655392 | tf_op jit(solution)/shard_map/ppermute | solution.py:340
  68.4 3.7 %collective-permute-done.12.same_ref = bf16[768,2048]{1,0:T(8,128)(2,1)} collective-permute-done((bf16[768,2048]{1,0:T(8,128)(2,1)}, bf16[768,2048]{1,0:T(8,128)(2,1)}, u32[]{:S(2)}, u32[]{:S(2)}) %collective-permute-start.12) | collective-permute-done | bytes 3145760 | tf_op jit(solution)/shard_map/ppermute | solution.py:341
  72.0 7.8 %collective-permute-done.9.refs_5_ = bf16[512,640]{1,0:T(8,128)(2,1)} collective-permute-done((bf16[512,640]{1,0:T(8,128)(2,1)}, bf16[512,640]{1,0:T(8,128)(2,1)}, u32[]{:S(2)}, u32[]{:S(2)}) %collective-permute-start.9) | collective-permute-done | bytes 655392 | tf_op jit(solution)/shard_map/ppermute | solution.py:340
  84.0 1.9 collective-permute-start.16
  87.6 2.1 %collective-permute-start.15 = (bf16[5,32,2048]{2,1,0:T(8,128)(2,1)}, bf16[5,32,2048]{2,1,0:T(8,128)(2,1)}, u32[]{:S(2)}, u32[]{:S(2)}) collective-permute-start(bf16[5,32,2048]{2,1,0:T(8,128)(2,1)} %copy-done.8), channel_id=1, source_target_pairs={{0,12},{2,6},{4,0},{6,10},{8,4},{10,14},{12,8},{14,2},{1,13},{3,7}... | collective-permute-start | bytes 1966088 | tf_op jit(solution)/shard_map/ppermute | solution.py:340
  92.0 4.5 %collective-permute-done.16.refs_7_ = bf16[256,640]{1,0:T(8,128)(2,1)} collective-permute-done((bf16[256,640]{1,0:T(8,128)(2,1)}, bf16[256,640]{1,0:T(8,128)(2,1)}, u32[]{:S(2)}, u32[]{:S(2)}) %collective-permute-start.16) | collective-permute-done | bytes 327712 | tf_op jit(solution)/shard_map/ppermute | solution.py:340
  96.7 1.8 collective-permute-start.13
  99.3 10.2 %shard_map.76 = bf16[768,640]{1,0:T(8,128)(2,1)} custom-call(s32[10]{0:T(128)S(1)} %pad_add_fusion.1.at, bf16[768,2048]{1,0:T(8,128)(2,1)} %collective-permute-done.12.same_ref, bf16[768,2048]{1,0:T(8,128)(2,1)} %collective-permute-done.18.swapped_ref, bf16[512,640]{1,0:T(8,128)(2,1)S(1)} %constant_dynamic-slice_fusion.1.refs_0_, ...), custom_call_target="tpu_custom_call" | custom-call | flops 4026531840 | bytes 13500416 | tf_op jit(solution)/shard_map/pallas_call | solution.py:230
  110.7 3.5 %shard_map.77 = bf16[6,32,2048]{2,1,0:T(8,128)(2,1)} custom-call(s32[6]{0:T(128)S(1)} %compare_convert_fusion.which_ref, s32[6]{0:T(128)S(1)} %get-tuple-element.63.first_ref, s32[6]{0:T(128)S(1)} %compare_select_fusion.second_ref, bf16[8,64,2048]{2,1,0:T(8,128)(2,1)S(1)} %copy-done.4, bf16[5,32,2048]{2,1,0:T(8,128)(2,1)} %collective-permute-done.15.b_ref), custom_call_target="tpu_custom_call" | custom-call | bytes 2359296 | tf_op jit(solution)/shard_map/pallas_call | solution.py:130
  114.2 2.4 %collective-permute-start.24 = (bf16[6,32,2048]{2,1,0:T(8,128)(2,1)}, bf16[6,32,2048]{2,1,0:T(8,128)(2,1)}, u32[]{:S(2)}, u32[]{:S(2)}) collective-permute-start(bf16[6,32,2048]{2,1,0:T(8,128)(2,1)} %shard_map.77), channel_id=1, source_target_pairs={{0,2},{2,0},{4,6},{6,4},{8,10},{10,8},{12,14},{14,12},{1,3},{3,1},... | collective-permute-start | bytes 2359304 | tf_op jit(solution)/shard_map/ppermute | solution.py:340
  116.7 5.0 %collective-permute-done.14.refs_1_ = bf16[512,384]{1,0:T(8,128)(2,1)S(1)} collective-permute-done((bf16[512,384]{1,0:T(8,128)(2,1)S(1)}, bf16[512,384]{1,0:T(8,128)(2,1)S(1)}, u32[]{:S(2)}, u32[]{:S(2)}) %collective-permute-start.14) | collective-permute-done | bytes 393248 | tf_op jit(solution)/shard_map/ppermute | solution.py:340
  121.7 2.0 %collective-permute-start.25 = (bf16[512,384]{1,0:T(8,128)(2,1)S(1)}, bf16[512,384]{1,0:T(8,128)(2,1)S(1)}, u32[]{:S(2)}, u32[]{:S(2)}) collective-permute-start(bf16[512,384]{1,0:T(8,128)(2,1)S(1)} %collective-permute-done.13.refs_2_), channel_id=1, source_target_pairs={{4,0},{8,4},{12,8},{14,12},{10,14},{6,10},{2,6},{0,2},{5,1},{9,5},... | collective-permute-start | bytes 1179656 | tf_op jit(solution)/shard_map/ppermute | solution.py:340
  123.7 2.6 %collective-permute-start.23 = (bf16[5,32,2048]{2,1,0:T(8,128)(2,1)}, bf16[5,32,2048]{2,1,0:T(8,128)(2,1)}, u32[]{:S(2)}, u32[]{:S(2)}) collective-permute-start(bf16[5,32,2048]{2,1,0:T(8,128)(2,1)} %get-tuple-element.54), channel_id=1, source_target_pairs={{0,12},{2,6},{4,0},{6,10},{8,4},{10,14},{12,8},{14,2},{1,13},{3,7}... | collective-permute-start | bytes 1966088 | tf_op jit(solution)/shard_map/ppermute | solution.py:340
  126.3 10.2 %shard_map.78.refs_0_ = f32[768,640]{1,0:T(8,128)} custom-call(s32[10]{0:T(128)S(1)} %pad_add_fusion.1.at, bf16[768,2048]{1,0:T(8,128)(2,1)} %same_ref.1, bf16[768,2048]{1,0:T(8,128)(2,1)} %collective-permute-done.3.swapped_ref, bf16[512,640]{1,0:T(8,128)(2,1)S(1)} %constant_dynamic-slice_fusion.1.refs_0_, bf16[512,640]{1,0:T(8,128)(2,1)} %collective-permute-done.4.refs_1_, ...), custom_call_target="tpu_custom_call" | custom-call | flops 4026531840 | bytes 13500416 | tf_op jit(solution)/shard_map/pallas_call | solution.py:230
  136.5 5.0 %shard_map.79.la = f32[768,64]{1,0:T(8,128)S(1)} custom-call(s32[3,6]{1,0:T(4,128)S(1)} %pad_add_fusion.table_ref, bf16[768,2048]{1,0:T(8,128)(2,1)} %same_ref.1, bf16[8,64,2048]{2,1,0:T(8,128)(2,1)S(1)} %bitcast.25, bf16[6,32,2048]{2,1,0:T(8,128)(2,1)S(1)} %copy-done.6, bf16[6,32,2048]{2,1,0:T(8,128)(2,1)S(1)} %collective-permute-done.19.refs_1_), custom_call_target="tpu_custom_call" | custom-call | flops 201326592 | bytes 5242880 | tf_op jit(solution)/shard_map/pallas_call | solution.py:181
  141.5 5.3 %collective-permute-done.21.refs_3_ = bf16[512,384]{1,0:T(8,128)(2,1)S(1)} collective-permute-done((bf16[512,384]{1,0:T(8,128)(2,1)S(1)}, bf16[512,384]{1,0:T(8,128)(2,1)S(1)}, u32[]{:S(2)}, u32[]{:S(2)}) %collective-permute-start.21) | collective-permute-done | bytes 393248 | tf_op jit(solution)/shard_map/ppermute | solution.py:340
  151.0 6.8 %collective-permute-done.26.refs_6_ = bf16[512,384]{1,0:T(8,128)(2,1)S(1)} collective-permute-done((bf16[512,384]{1,0:T(8,128)(2,1)S(1)}, bf16[512,384]{1,0:T(8,128)(2,1)S(1)}, u32[]{:S(2)}, u32[]{:S(2)}) %collective-permute-start.26) | collective-permute-done | bytes 393248 | tf_op jit(solution)/shard_map/ppermute | solution.py:340
  161.4 5.5 %collective-permute-done.27.refs_7_ = bf16[256,384]{1,0:T(8,128)(2,1)S(1)} collective-permute-done((bf16[256,384]{1,0:T(8,128)(2,1)S(1)}, bf16[256,384]{1,0:T(8,128)(2,1)S(1)}, u32[]{:S(2)}, u32[]{:S(2)}) %collective-permute-start.27) | collective-permute-done | bytes 196640 | tf_op jit(solution)/shard_map/ppermute | solution.py:340
  166.9 6.5 %shard_map.81 = bf16[768,384]{1,0:T(8,128)(2,1)S(1)} custom-call(s32[10]{0:T(128)S(1)} %pad_add_fusion.1.at, bf16[768,2048]{1,0:T(8,128)(2,1)} %collective-permute-done.12.same_ref, bf16[768,2048]{1,0:T(8,128)(2,1)} %collective-permute-done.18.swapped_ref, bf16[512,384]{1,0:T(8,128)(2,1)S(1)} %constant_dynamic-slice_fusion.2.refs_0_, ...), custom_call_target="tpu_custom_call" | custom-call | flops 2415919104 | bytes 10616832 | tf_op jit(solution)/shard_map/pallas_call | solution.py:230
  174.0 6.5 %shard_map.82.refs_1_ = f32[768,384]{1,0:T(8,128)S(1)} custom-call(s32[10]{0:T(128)S(1)} %pad_add_fusion.1.at, bf16[768,2048]{1,0:T(8,128)(2,1)} %same_ref.1, bf16[768,2048]{1,0:T(8,128)(2,1)} %collective-permute-done.3.swapped_ref, bf16[512,384]{1,0:T(8,128)(2,1)S(1)} %constant_dynamic-slice_fusion.2.refs_0_, ...), custom_call_target="tpu_custom_call" | custom-call | flops 2415919104 | bytes 10616832 | tf_op jit(solution)/shard_map/pallas_call | solution.py:230
  181.2 3.6 %collective-permute-done.30.refs_3_ = bf16[768,384]{1,0:T(8,128)(2,1)S(1)} collective-permute-done((bf16[768,384]{1,0:T(8,128)(2,1)S(1)}, bf16[768,384]{1,0:T(8,128)(2,1)S(1)}, u32[]{:S(2)}, u32[]{:S(2)}) %collective-permute-start.30) | collective-permute-done | bytes 589856 | tf_op jit(solution)/shard_map/ppermute | solution.py:341
  184.9 6.6 %shard_map.83 = bf16[768,2048]{1,0:T(8,128)(2,1)} custom-call(s32[3,6]{1,0:T(4,128)S(1)} %pad_add_fusion.table_ref, s32[6]{0:T(128)S(1)} %copy-done.7, s32[1]{0:T(128)} %bitcast.3.half_ref, f32[768,64]{1,0:T(8,128)S(1)} %shard_map.79.la, f32[768,64]{1,0:T(8,128)S(1)} %collective-permute-done.20.lb, f32[768,640]{1,0:T(8,128)} %shard_map.78.refs_0_, ...), custom_call_target="tpu_custom_call" | custom-call | flops 201326592 | bytes 9961472 | tf_op jit(solution)/shard_map/pallas_call | solution.py:295
  (90 shorter events, 29.7 us)
Async XLA Ops:
  0.0 25.8 %collective-permute-start.3 = (bf16[768,2048]{1,0:T(8,128)(2,1)}, bf16[768,2048]{1,0:T(8,128)(2,1)}, u32[]{:S(2)}, u32[]{:S(2)}) collective-permute-start(bf16[768,2048]{1,0:T(8,128)(2,1)} %same_ref.1), channel_id=1, source_target_pairs={{0,1},{1,0},{2,3},{3,2},{4,5},{5,4},{6,7},{7,6},{8,9},{9,8},{10,11... | collective-permute-start | bytes 9437192 | tf_op jit(solution)/shard_map/ppermute | solution.py:342
  0.5 71.6 %collective-permute-start.12 = (bf16[768,2048]{1,0:T(8,128)(2,1)}, bf16[768,2048]{1,0:T(8,128)(2,1)}, u32[]{:S(2)}, u32[]{:S(2)}) collective-permute-start(bf16[768,2048]{1,0:T(8,128)(2,1)} %same_ref.1), channel_id=1, source_target_pairs={{0,16},{16,0},{1,17},{17,1},{2,18},{18,2},{3,19},{19,3},{4,20},{20... | collective-permute-start | bytes 9437192 | tf_op jit(solution)/shard_map/ppermute | solution.py:341
  3.0 6.7 %collective-permute-start.1 = (s32[6]{0:T(128)}, s32[6]{0:T(128)S(1)}, u32[]{:S(2)}, u32[]{:S(2)}) collective-permute-start(s32[6]{0:T(128)} %param.11), channel_id=1, source_target_pairs={{0,14},{2,4},{4,2},{6,8},{8,6},{10,12},{12,10},{14,0},{1,15},{3,5}... | collective-permute-start | bytes 80 | tf_op jit(solution)/shard_map/ppermute | solution.py:340
  7.6 9.5 %collective-permute-start = (s32[6]{0:T(128)}, s32[6]{0:T(128)S(1)}, u32[]{:S(2)}, u32[]{:S(2)}) collective-permute-start(s32[6]{0:T(128)} %param.11), channel_id=1, source_target_pairs={{0,2},{2,0},{4,6},{6,4},{8,10},{10,8},{12,14},{14,12},{1,3},{3,1},... | collective-permute-start | bytes 80 | tf_op jit(solution)/shard_map/ppermute | solution.py:340
  7.7 17.8 %collective-permute-start.5 = (bf16[512,640]{1,0:T(8,128)(2,1)S(1)}, bf16[512,640]{1,0:T(8,128)(2,1)}, u32[]{:S(2)}, u32[]{:S(2)}) collective-permute-start(bf16[512,640]{1,0:T(8,128)(2,1)S(1)} %constant_dynamic-slice_fusion.1.refs_0_), channel_id=1, source_target_pairs={{4,0},{8,4},{12,8},{14,12},{10,14},{6,10},{2,6},{0,2},{5,1},{9,5},... | collective-permute-start | bytes 1966088 | tf_op jit(solution)/shard_map/ppermute | solution.py:340
  9.7 16.1 %collective-permute-start.4 = (bf16[512,640]{1,0:T(8,128)(2,1)S(1)}, bf16[512,640]{1,0:T(8,128)(2,1)}, u32[]{:S(2)}, u32[]{:S(2)}) collective-permute-start(bf16[512,640]{1,0:T(8,128)(2,1)S(1)} %constant_dynamic-slice_fusion.1.refs_0_), channel_id=1, source_target_pairs={{0,4},{4,8},{8,12},{12,14},{14,10},{10,6},{6,2},{2,0},{1,5},{5,9},... | collective-permute-start | bytes 1966088 | tf_op jit(solution)/shard_map/ppermute | solution.py:340
  17.1 22.3 %collective-permute-start.2 = (bf16[5,32,2048]{2,1,0:T(8,128)(2,1)}, bf16[5,32,2048]{2,1,0:T(8,128)(2,1)S(1)}, u32[]{:S(2)}, u32[]{:S(2)}) collective-permute-start(bf16[5,32,2048]{2,1,0:T(8,128)(2,1)} %get-tuple-element.33), channel_id=1, source_target_pairs={{0,12},{2,6},{4,0},{6,10},{8,4},{10,14},{12,8},{14,2},{1,13},{3,7}... | collective-permute-start | bytes 1966088 | tf_op jit(solution)/shard_map/ppermute | solution.py:340
  25.8 27.7 %collective-permute-start.8 = (bf16[512,640]{1,0:T(8,128)(2,1)}, bf16[512,640]{1,0:T(8,128)(2,1)}, u32[]{:S(2)}, u32[]{:S(2)}) collective-permute-start(bf16[512,640]{1,0:T(8,128)(2,1)} %collective-permute-done.4.refs_1_), channel_id=1, source_target_pairs={{0,4},{4,8},{8,12},{12,14},{14,10},{10,6},{6,2},{2,0},{1,5},{5,9},... | collective-permute-start | bytes 1966088 | tf_op jit(solution)/shard_map/ppermute | solution.py:340
  27.5 26.0 %collective-permute-start.10 = (bf16[512,640]{1,0:T(8,128)(2,1)}, bf16[512,640]{1,0:T(8,128)(2,1)}, u32[]{:S(2)}, u32[]{:S(2)}) collective-permute-start(bf16[512,640]{1,0:T(8,128)(2,1)} %collective-permute-done.5.refs_2_), channel_id=1, source_target_pairs={{4,0},{8,4},{12,8},{14,12},{10,14},{6,10},{2,6},{0,2},{5,1},{9,5},... | collective-permute-start | bytes 1966088 | tf_op jit(solution)/shard_map/ppermute | solution.py:340
  41.7 25.7 %collective-permute-start.6 = (bf16[6,32,2048]{2,1,0:T(8,128)(2,1)S(1)}, bf16[6,32,2048]{2,1,0:T(8,128)(2,1)S(1)}, u32[]{:S(2)}, u32[]{:S(2)}) collective-permute-start(bf16[6,32,2048]{2,1,0:T(8,128)(2,1)S(1)} %shard_map.74), channel_id=1, source_target_pairs={{0,2},{2,0},{4,6},{6,4},{8,10},{10,8},{12,14},{14,12},{1,3},{3,1},... | collective-permute-start | bytes 2359304 | tf_op jit(solution)/shard_map/ppermute | solution.py:340
  46.7 20.8 %collective-permute-start.7 = (bf16[5,32,2048]{2,1,0:T(8,128)(2,1)S(1)}, bf16[5,32,2048]{2,1,0:T(8,128)(2,1)S(1)}, u32[]{:S(2)}, u32[]{:S(2)}) collective-permute-start(bf16[5,32,2048]{2,1,0:T(8,128)(2,1)S(1)} %copy-done.10), channel_id=1, source_target_pairs={{0,12},{2,6},{4,0},{6,10},{8,4},{10,14},{12,8},{14,2},{1,13},{3,7}... | collective-permute-start | bytes 1966088 | tf_op jit(solution)/shard_map/ppermute | solution.py:340
  53.5 26.4 %collective-permute-start.9 = (bf16[512,640]{1,0:T(8,128)(2,1)}, bf16[512,640]{1,0:T(8,128)(2,1)}, u32[]{:S(2)}, u32[]{:S(2)}) collective-permute-start(bf16[512,640]{1,0:T(8,128)(2,1)} %collective-permute-done.8.refs_3_), channel_id=1, source_target_pairs={{0,4},{4,8},{8,12},{12,14},{14,10},{10,6},{6,2},{2,0},{1,5},{5,9},... | collective-permute-start | bytes 1966088 | tf_op jit(solution)/shard_map/ppermute | solution.py:340
  55.6 24.9 %collective-permute-start.11 = (bf16[512,640]{1,0:T(8,128)(2,1)}, bf16[512,640]{1,0:T(8,128)(2,1)}, u32[]{:S(2)}, u32[]{:S(2)}) collective-permute-start(bf16[512,640]{1,0:T(8,128)(2,1)} %collective-permute-done.10.refs_4_), channel_id=1, source_target_pairs={{4,0},{8,4},{12,8},{14,12},{10,14},{6,10},{2,6},{0,2},{5,1},{9,5},... | collective-permute-start | bytes 1966088 | tf_op jit(solution)/shard_map/ppermute | solution.py:340
  80.5 18.8 %collective-permute-start.18 = (bf16[768,2048]{1,0:T(8,128)(2,1)}, bf16[768,2048]{1,0:T(8,128)(2,1)}, u32[]{:S(2)}, u32[]{:S(2)}) collective-permute-start(bf16[768,2048]{1,0:T(8,128)(2,1)} %collective-permute-done.12.same_ref), channel_id=1, source_target_pairs={{0,1},{1,0},{2,3},{3,2},{4,5},{5,4},{6,7},{7,6},{8,9},{9,8},{10,11... | collective-permute-start | bytes 9437192 | tf_op jit(solution)/shard_map/ppermute | solution.py:342
  84.0 12.5 %collective-permute-start.16 = (bf16[256,640]{1,0:T(8,128)(2,1)}, bf16[256,640]{1,0:T(8,128)(2,1)}, u32[]{:S(2)}, u32[]{:S(2)}) collective-permute-start(bf16[256,640]{1,0:T(8,128)(2,1)} %slice.16), channel_id=1, source_target_pairs={{0,4},{4,8},{8,12},{12,14},{14,10},{10,6},{6,2},{2,0},{1,5},{5,9},... | collective-permute-start | bytes 983048 | tf_op jit(solution)/shard_map/ppermute | solution.py:340
  85.8 10.9 %collective-permute-start.17 = (bf16[256,640]{1,0:T(8,128)(2,1)}, bf16[256,640]{1,0:T(8,128)(2,1)}, u32[]{:S(2)}, u32[]{:S(2)}) collective-permute-start(bf16[256,640]{1,0:T(8,128)(2,1)} %slice.17), channel_id=1, source_target_pairs={{4,0},{8,4},{12,8},{14,12},{10,14},{6,10},{2,6},{0,2},{5,1},{9,5},... | collective-permute-start | bytes 983048 | tf_op jit(solution)/shard_map/ppermute | solution.py:340
  87.6 23.1 %collective-permute-start.15 = (bf16[5,32,2048]{2,1,0:T(8,128)(2,1)}, bf16[5,32,2048]{2,1,0:T(8,128)(2,1)}, u32[]{:S(2)}, u32[]{:S(2)}) collective-permute-start(bf16[5,32,2048]{2,1,0:T(8,128)(2,1)} %copy-done.8), channel_id=1, source_target_pairs={{0,12},{2,6},{4,0},{6,10},{8,4},{10,14},{12,8},{14,2},{1,13},{3,7}... | collective-permute-start | bytes 1966088 | tf_op jit(solution)/shard_map/ppermute | solution.py:340
  91.0 45.5 %collective-permute-start.19 = (bf16[6,32,2048]{2,1,0:T(8,128)(2,1)S(1)}, bf16[6,32,2048]{2,1,0:T(8,128)(2,1)S(1)}, u32[]{:S(2)}, u32[]{:S(2)}) collective-permute-start(bf16[6,32,2048]{2,1,0:T(8,128)(2,1)S(1)} %shard_map.75), channel_id=1, source_target_pairs={{0,2},{2,0},{4,6},{6,4},{8,10},{10,8},{12,14},{14,12},{1,3},{3,1},... | collective-permute-start | bytes 2359304 | tf_op jit(solution)/shard_map/ppermute | solution.py:340
  96.5 25.2 %collective-permute-start.14 = (bf16[512,384]{1,0:T(8,128)(2,1)S(1)}, bf16[512,384]{1,0:T(8,128)(2,1)S(1)}, u32[]{:S(2)}, u32[]{:S(2)}) collective-permute-start(bf16[512,384]{1,0:T(8,128)(2,1)S(1)} %constant_dynamic-slice_fusion.2.refs_0_), channel_id=1, source_target_pairs={{0,4},{4,8},{8,12},{12,14},{14,10},{10,6},{6,2},{2,0},{1,5},{5,9},... | collective-permute-start | bytes 1179656 | tf_op jit(solution)/shard_map/ppermute | solution.py:340
  96.7 25.0 %collective-permute-start.13 = (bf16[512,384]{1,0:T(8,128)(2,1)S(1)}, bf16[512,384]{1,0:T(8,128)(2,1)S(1)}, u32[]{:S(2)}, u32[]{:S(2)}) collective-permute-start(bf16[512,384]{1,0:T(8,128)(2,1)S(1)} %constant_dynamic-slice_fusion.2.refs_0_), channel_id=1, source_target_pairs={{4,0},{8,4},{12,8},{14,12},{10,14},{6,10},{2,6},{0,2},{5,1},{9,5},... | collective-permute-start | bytes 1179656 | tf_op jit(solution)/shard_map/ppermute | solution.py:340
  114.2 44.7 %collective-permute-start.24 = (bf16[6,32,2048]{2,1,0:T(8,128)(2,1)}, bf16[6,32,2048]{2,1,0:T(8,128)(2,1)}, u32[]{:S(2)}, u32[]{:S(2)}) collective-permute-start(bf16[6,32,2048]{2,1,0:T(8,128)(2,1)} %shard_map.77), channel_id=1, source_target_pairs={{0,2},{2,0},{4,6},{6,4},{8,10},{10,8},{12,14},{14,12},{1,3},{3,1},... | collective-permute-start | bytes 2359304 | tf_op jit(solution)/shard_map/ppermute | solution.py:340
  121.7 25.1 %collective-permute-start.21 = (bf16[512,384]{1,0:T(8,128)(2,1)S(1)}, bf16[512,384]{1,0:T(8,128)(2,1)S(1)}, u32[]{:S(2)}, u32[]{:S(2)}) collective-permute-start(bf16[512,384]{1,0:T(8,128)(2,1)S(1)} %collective-permute-done.14.refs_1_), channel_id=1, source_target_pairs={{0,4},{4,8},{8,12},{12,14},{14,10},{10,6},{6,2},{2,0},{1,5},{5,9},... | collective-permute-start | bytes 1179656 | tf_op jit(solution)/shard_map/ppermute | solution.py:340
  121.7 25.0 %collective-permute-start.25 = (bf16[512,384]{1,0:T(8,128)(2,1)S(1)}, bf16[512,384]{1,0:T(8,128)(2,1)S(1)}, u32[]{:S(2)}, u32[]{:S(2)}) collective-permute-start(bf16[512,384]{1,0:T(8,128)(2,1)S(1)} %collective-permute-done.13.refs_2_), channel_id=1, source_target_pairs={{4,0},{8,4},{12,8},{14,12},{10,14},{6,10},{2,6},{0,2},{5,1},{9,5},... | collective-permute-start | bytes 1179656 | tf_op jit(solution)/shard_map/ppermute | solution.py:340
  123.7 25.6 %collective-permute-start.23 = (bf16[5,32,2048]{2,1,0:T(8,128)(2,1)}, bf16[5,32,2048]{2,1,0:T(8,128)(2,1)}, u32[]{:S(2)}, u32[]{:S(2)}) collective-permute-start(bf16[5,32,2048]{2,1,0:T(8,128)(2,1)} %get-tuple-element.54), channel_id=1, source_target_pairs={{0,12},{2,6},{4,0},{6,10},{8,4},{10,14},{12,8},{14,2},{1,13},{3,7}... | collective-permute-start | bytes 1966088 | tf_op jit(solution)/shard_map/ppermute | solution.py:340
  146.8 11.0 %collective-permute-start.26 = (bf16[512,384]{1,0:T(8,128)(2,1)S(1)}, bf16[512,384]{1,0:T(8,128)(2,1)S(1)}, u32[]{:S(2)}, u32[]{:S(2)}) collective-permute-start(bf16[512,384]{1,0:T(8,128)(2,1)S(1)} %collective-permute-done.25.refs_4_), channel_id=1, source_target_pairs={{4,0},{8,4},{12,8},{14,12},{10,14},{6,10},{2,6},{0,2},{5,1},{9,5},... | collective-permute-start | bytes 1179656 | tf_op jit(solution)/shard_map/ppermute | solution.py:340
  148.5 10.5 %collective-permute-start.22 = (bf16[512,384]{1,0:T(8,128)(2,1)S(1)}, bf16[512,384]{1,0:T(8,128)(2,1)S(1)}, u32[]{:S(2)}, u32[]{:S(2)}) collective-permute-start(bf16[512,384]{1,0:T(8,128)(2,1)S(1)} %collective-permute-done.21.refs_3_), channel_id=1, source_target_pairs={{0,4},{4,8},{8,12},{12,14},{14,10},{10,6},{6,2},{2,0},{1,5},{5,9},... | collective-permute-start | bytes 1179656 | tf_op jit(solution)/shard_map/ppermute | solution.py:340
  148.8 25.2 %collective-permute-start.29 = (bf16[768,640]{1,0:T(8,128)(2,1)S(1)}, bf16[768,640]{1,0:T(8,128)(2,1)S(1)}, u32[]{:S(2)}, u32[]{:S(2)}) collective-permute-start(bf16[768,640]{1,0:T(8,128)(2,1)S(1)} %copy-done.12), channel_id=1, source_target_pairs={{0,16},{16,0},{1,17},{17,1},{2,18},{18,2},{3,19},{19,3},{4,20},{20... | collective-permute-start | bytes 2949128 | tf_op jit(solution)/shard_map/ppermute | solution.py:341
  159.0 7.9 %collective-permute-start.27 = (bf16[256,384]{1,0:T(8,128)(2,1)S(1)}, bf16[256,384]{1,0:T(8,128)(2,1)S(1)}, u32[]{:S(2)}, u32[]{:S(2)}) collective-permute-start(bf16[256,384]{1,0:T(8,128)(2,1)S(1)} %slice.18), channel_id=1, source_target_pairs={{0,4},{4,8},{8,12},{12,14},{14,10},{10,6},{6,2},{2,0},{1,5},{5,9},... | collective-permute-start | bytes 589832 | tf_op jit(solution)/shard_map/ppermute | solution.py:340
  159.6 7.2 %collective-permute-start.28 = (bf16[256,384]{1,0:T(8,128)(2,1)S(1)}, bf16[256,384]{1,0:T(8,128)(2,1)S(1)}, u32[]{:S(2)}, u32[]{:S(2)}) collective-permute-start(bf16[256,384]{1,0:T(8,128)(2,1)S(1)} %slice.19), channel_id=1, source_target_pairs={{4,0},{8,4},{12,8},{14,12},{10,14},{6,10},{2,6},{0,2},{5,1},{9,5},... | collective-permute-start | bytes 589832 | tf_op jit(solution)/shard_map/ppermute | solution.py:340
  161.1 20.2 %collective-permute-start.31 = (bf16[6,32,2048]{2,1,0:T(8,128)(2,1)S(1)}, bf16[6,32,2048]{2,1,0:T(8,128)(2,1)S(1)}, u32[]{:S(2)}, u32[]{:S(2)}) collective-permute-start(bf16[6,32,2048]{2,1,0:T(8,128)(2,1)S(1)} %shard_map.80), channel_id=1, source_target_pairs={{0,2},{2,0},{4,6},{6,4},{8,10},{10,8},{12,14},{14,12},{1,3},{3,1},... | collective-permute-start | bytes 2359304 | tf_op jit(solution)/shard_map/ppermute | solution.py:340
  173.4 11.4 %collective-permute-start.30 = (bf16[768,384]{1,0:T(8,128)(2,1)S(1)}, bf16[768,384]{1,0:T(8,128)(2,1)S(1)}, u32[]{:S(2)}, u32[]{:S(2)}) collective-permute-start(bf16[768,384]{1,0:T(8,128)(2,1)S(1)} %shard_map.81), channel_id=1, source_target_pairs={{0,16},{16,0},{1,17},{17,1},{2,18},{18,2},{3,19},{19,3},{4,20},{20... | collective-permute-start | bytes 1769480 | tf_op jit(solution)/shard_map/ppermute | solution.py:341
  174.0 6.5 %collective-permute-start.20 = (f32[768,64]{1,0:T(8,128)S(1)}, f32[768,64]{1,0:T(8,128)S(1)}, u32[]{:S(2)}, u32[]{:S(2)}) collective-permute-start(f32[768,64]{1,0:T(8,128)S(1)} %shard_map.79.la), channel_id=1, source_target_pairs={{0,1},{1,0},{2,3},{3,2},{4,5},{5,4},{6,7},{7,6},{8,9},{9,8},{10,11... | collective-permute-start | bytes 589832 | tf_op jit(solution)/shard_map/ppermute | solution.py:342
  (13 other events, 122.8 us)

commit v5 on v4

--- a/solution.py
+++ b/solution.py
@@ -202,16 +202,17 @@
     depth = pieces[0].shape[0]
     tile = 256 if rows % 256 == 0 else rows
     count = len(pieces)
+    last = shards.shape[0] - 1
 
     def body(at, same_ref, swapped_ref, *refs):
         x_ref = refs[-1]
 
-        @pl.when(at[count] == 0)
+        @pl.when(at[last] == 0)
         def _():
             x_ref[:, :width] = same_ref[...]
             x_ref[:, width:] = swapped_ref[...]
 
-        @pl.when(at[count] != 0)
+        @pl.when(at[last] != 0)
         def _():
             x_ref[:, :width] = swapped_ref[...]
             x_ref[:, width:] = same_ref[...]
@@ -219,10 +220,8 @@
         total = None
         for k in range(count):
             x = x_ref[:, pl.ds(pl.multiple_of(at[k], depth), depth)]
-            if k == count - 2:
-                x = x[:, : depth // 2]
-            if k == count - 1:
-                x = x[:, depth // 2 :]
+            if refs[k].shape[0] < depth:
+                x = x[:, : depth // 2] if k == count - 2 else x[:, depth // 2 :]
             term = jnp.dot(x, refs[k][...], preferred_element_type=F32)
             total = term if total is None else total + term
         refs[count][...] = total.astype(out_type)
@@ -240,11 +239,58 @@
         out_shape=jax.ShapeDtypeStruct((rows, columns), out_type),
         compiler_params=params(1),
         cost_estimate=pl.CostEstimate(
+            flops=4 * rows * width * columns if count > 7 else 0,
+            bytes_accessed=(2 * rows * width + 2 * width * columns + 2 * rows * columns) * 2 if count > 7 else 0,
+            transcendentals=0,
+        ),
+    )(shards, same, swapped, *pieces)
+
+
+def complete(shards, same, swapped, pieces, partial, out_type):
+    rows, width = same.shape
+    columns = pieces[0].shape[1]
+    depth = 2 * pieces[0].shape[0]
+    tile = 256 if rows % 256 == 0 else rows
+    last = shards.shape[0] - 1
+
+    def body(at, same_ref, swapped_ref, upper_ref, lower_ref, partial_ref, out_ref):
+        def write(x_ref):
+            total = partial_ref[...]
+            total += jnp.dot(x_ref[:, : depth // 2], upper_ref[...], preferred_element_type=F32)
+            total += jnp.dot(x_ref[:, depth // 2 :], lower_ref[...], preferred_element_type=F32)
+            out_ref[...] = total.astype(out_type)
+
+        here = at[last - 1] // width == at[last]
+
+        @pl.when(here)
+        def _():
+            write(same_ref)
+
+        @pl.when(jnp.logical_not(here))
+        def _():
+            write(swapped_ref)
+
+    column = lambda i, at: (i, (at[last - 1] % width) // depth)
+    whole = lambda i, at: (0, 0)
+    row = pl.BlockSpec((tile, columns), lambda i, at: (i, 0))
+    return pl.pallas_call(
+        body,
+        grid_spec=pltpu.PrefetchScalarGridSpec(
+            num_scalar_prefetch=1,
+            grid=(rows // tile,),
+            in_specs=[pl.BlockSpec((tile, depth), column)] * 2
+            + [pl.BlockSpec(p.shape, whole) for p in pieces]
+            + [row],
+            out_specs=row,
+        ),
+        out_shape=jax.ShapeDtypeStruct((rows, columns), out_type),
+        compiler_params=params(1),
+        cost_estimate=pl.CostEstimate(
             flops=4 * rows * width * columns,
             bytes_accessed=(2 * rows * width + 2 * width * columns + 2 * rows * columns) * 2,
             transcendentals=0,
         ),
-    )(shards, same, swapped, *pieces)
+    )(shards, same, swapped, *pieces, partial)
 
 
 def finish(table, live, half, low_a, low_b, mine, theirs, sources):
@@ -414,7 +460,12 @@
     def start_base(chunk):
         while len(pieces[chunk]) < count + 1:
             ring_step(chunk)
-        result = product(shards, their_same, halves["their"], pieces[chunk], jnp.bfloat16)
+        rows_in = (shards, their_same, halves["their"])
+        if chunk == len(CHUNKS) - 1:
+            partial = product(*rows_in, pieces[chunk][:-2], F32)
+            result = complete(*rows_in, pieces[chunk][-2:], partial, jnp.bfloat16)
+        else:
+            result = product(*rows_in, pieces[chunk], jnp.bfloat16)
         theirs[chunk] = partner(result)
         order.arrived(result)
 

time: 192 us -> 192 us (level)
  Pallas kernels: 55.3 us -> 58.2 us
  waiting for transfers between devices: 79.3 us -> 76.5 us
    pallas_call x0 -> x1, Pallas kernels: none -> 3.27 us  [complete(): pl.pallas_call(body, grid_spec=pltpu.PrefetchScalarGridSpec(num_scalar_pr...]
    ppermute x26, waiting for transfers between devices: 72 us -> 69.2 us  [local(): rep = lambda a, route: lax.ppermute(a, 'replica', route)]
  transfers between devices with their start and end apart: 32 -> 32, of which waited for: 17 -> 17; matrix products, arithmetic and copies ran while one was open for 3% -> 3% of each run, Pallas kernels for 25% -> 27%
where the time goes in v5:
time: 192 us; the launch traced here: 191 us
  waiting for transfers between devices  76.5 us (40%)
  Pallas kernels  58.2 us (30%)
  starting transfers between devices  45 us (23%)
  local copies, waits for them, and re-layouts  9.84 us (5%)
    ppermute x26, waiting for transfers between devices, local(): rep = lambda a, route: lax.ppermute(a, 'replica', route)  69.2 us
    ppermute x26, starting transfers between devices, local(): rep = lambda a, route: lax.ppermute(a, 'replica', route)  40.9 us
    pallas_call x4, Pallas kernels, product(): pl.pallas_call(body, grid_spec=pltpu.PrefetchScalarGridSpec(num_scalar_pr...  33.1 us
    ppermute x3, waiting for transfers between devices, local(): lax.ppermute(a, 'groups', [(i, i ^ 1) for i in range(groups)])  7.31 us
    pallas_call x4, Pallas kernels, pick_two(): pl.pallas_call(body, grid_spec=pltpu.PrefetchScalarGridSpec(num_scalar_pr...  6.59 us
    pallas_call x1, Pallas kernels, finish(): pl.pallas_call(body, grid_spec=pltpu.PrefetchScalarGridSpec(num_scalar_pr...  6.48 us
    pallas_call x1, Pallas kernels, low_partial(): pl.pallas_call(body, grid_spec=pltpu.PrefetchScalarGridSpec(num_scalar_pr...  5.08 us
    unnamed x26, local copies, waits for them, and re-layouts  5.04 us
  transfers between devices with their start and end apart: 32, of which 17 were waited for; matrix products, arithmetic and copies ran while one was open for 3% of the time, Pallas kernels for 27%

profile of v5, /device:TPU:0, one launch (start us, length us, event | category | flops | bytes accessed | tf_op | source)
XLA Modules:
  0.0 191.0 jit_solution(7384417870193232849)
XLA Ops:
  0.5 2.6 %collective-permute-start.12 = (bf16[768,2048]{1,0:T(8,128)(2,1)}, bf16[768,2048]{1,0:T(8,128)(2,1)}, u32[]{:S(2)}, u32[]{:S(2)}) collective-permute-start(bf16[768,2048]{1,0:T(8,128)(2,1)} %same_ref.1), channel_id=1, source_target_pairs={{0,16},{16,0},{1,17},{17,1},{2,18},{18,2},{3,19},{19,3},{4,20},{20... | collective-permute-start | bytes 9437192 | tf_op jit(solution)/shard_map/ppermute | solution.py:387
  3.0 4.6 %collective-permute-start.1 = (s32[6]{0:T(128)}, s32[6]{0:T(128)S(1)}, u32[]{:S(2)}, u32[]{:S(2)}) collective-permute-start(s32[6]{0:T(128)} %param.11), channel_id=1, source_target_pairs={{0,14},{2,4},{4,2},{6,8},{8,6},{10,12},{12,10},{14,0},{1,15},{3,5}... | collective-permute-start | bytes 80 | tf_op jit(solution)/shard_map/ppermute | solution.py:386
  7.7 2.1 %collective-permute-start.5 = (bf16[512,640]{1,0:T(8,128)(2,1)S(1)}, bf16[512,640]{1,0:T(8,128)(2,1)}, u32[]{:S(2)}, u32[]{:S(2)}) collective-permute-start(bf16[512,640]{1,0:T(8,128)(2,1)S(1)} %constant_dynamic-slice_fusion.1.refs_0_), channel_id=1, source_target_pairs={{4,0},{8,4},{12,8},{14,12},{10,14},{6,10},{2,6},{0,2},{5,1},{9,5},... | collective-permute-start | bytes 1966088 | tf_op jit(solution)/shard_map/ppermute | solution.py:386
  11.7 3.7 %shard_map.73 = (bf16[5,32,2048]{2,1,0:T(8,128)(2,1)}, bf16[5,32,2048]{2,1,0:T(8,128)(2,1)S(1)}, bf16[5,32,2048]{2,1,0:T(8,128)(2,1)S(1)}, bf16[5,32,2048]{2,1,0:T(8,128)(2,1)}) custom-call(s32[5]{0:T(128)S(1)} %select_reduce_fusion.at, bf16[8,64,2048]{2,1,0:T(8,128)(2,1)S(1)} %bitcast.22, bf16[8,64,2048]{2,1,0:T(8,128)(2,1)} %refs_4_.1), custom_call_target="tpu_custom_call" | custom-call | bytes 5242880 | tf_op jit(solution)/shard_map/pallas_call | solution.py:99
  17.1 4.8 %collective-permute-start.2 = (bf16[5,32,2048]{2,1,0:T(8,128)(2,1)}, bf16[5,32,2048]{2,1,0:T(8,128)(2,1)S(1)}, u32[]{:S(2)}, u32[]{:S(2)}) collective-permute-start(bf16[5,32,2048]{2,1,0:T(8,128)(2,1)} %get-tuple-element.33), channel_id=1, source_target_pairs={{0,12},{2,6},{4,0},{6,10},{8,4},{10,14},{12,8},{14,2},{1,13},{3,7}... | collective-permute-start | bytes 1966088 | tf_op jit(solution)/shard_map/ppermute | solution.py:386
  21.8 3.6 %collective-permute-done.5.refs_2_ = bf16[512,640]{1,0:T(8,128)(2,1)} collective-permute-done((bf16[512,640]{1,0:T(8,128)(2,1)S(1)}, bf16[512,640]{1,0:T(8,128)(2,1)}, u32[]{:S(2)}, u32[]{:S(2)}) %collective-permute-start.5) | collective-permute-done | bytes 655392 | tf_op jit(solution)/shard_map/ppermute | solution.py:386
  28.0 11.3 %collective-permute-done.2.b_ref = bf16[5,32,2048]{2,1,0:T(8,128)(2,1)S(1)} collective-permute-done((bf16[5,32,2048]{2,1,0:T(8,128)(2,1)}, bf16[5,32,2048]{2,1,0:T(8,128)(2,1)S(1)}, u32[]{:S(2)}, u32[]{:S(2)}) %collective-permute-start.2) | collective-permute-done | bytes 655392 | tf_op jit(solution)/shard_map/ppermute | solution.py:386
  41.7 4.9 %collective-permute-start.6 = (bf16[6,32,2048]{2,1,0:T(8,128)(2,1)S(1)}, bf16[6,32,2048]{2,1,0:T(8,128)(2,1)S(1)}, u32[]{:S(2)}, u32[]{:S(2)}) collective-permute-start(bf16[6,32,2048]{2,1,0:T(8,128)(2,1)S(1)} %shard_map.74), channel_id=1, source_target_pairs={{0,2},{2,0},{4,6},{6,4},{8,10},{10,8},{12,14},{14,12},{1,3},{3,1},... | collective-permute-start | bytes 2359304 | tf_op jit(solution)/shard_map/ppermute | solution.py:386
  46.7 6.8 %collective-permute-done.10.refs_4_ = bf16[512,640]{1,0:T(8,128)(2,1)} collective-permute-done((bf16[512,640]{1,0:T(8,128)(2,1)}, bf16[512,640]{1,0:T(8,128)(2,1)}, u32[]{:S(2)}, u32[]{:S(2)}) %collective-permute-start.10) | collective-permute-done | bytes 655392 | tf_op jit(solution)/shard_map/ppermute | solution.py:386
  53.5 2.1 %collective-permute-start.9 = (bf16[512,640]{1,0:T(8,128)(2,1)}, bf16[512,640]{1,0:T(8,128)(2,1)}, u32[]{:S(2)}, u32[]{:S(2)}) collective-permute-start(bf16[512,640]{1,0:T(8,128)(2,1)} %collective-permute-done.8.refs_3_), channel_id=1, source_target_pairs={{0,4},{4,8},{8,12},{12,14},{14,10},{10,6},{6,2},{2,0},{1,5},{5,9},... | collective-permute-start | bytes 1966088 | tf_op jit(solution)/shard_map/ppermute | solution.py:386
  55.8 11.6 %collective-permute-done.7.b_ref = bf16[5,32,2048]{2,1,0:T(8,128)(2,1)S(1)} collective-permute-done((bf16[5,32,2048]{2,1,0:T(8,128)(2,1)S(1)}, bf16[5,32,2048]{2,1,0:T(8,128)(2,1)S(1)}, u32[]{:S(2)}, u32[]{:S(2)}) %collective-permute-start.7) | collective-permute-done | bytes 655392 | tf_op jit(solution)/shard_map/ppermute | solution.py:386
  68.4 3.7 %collective-permute-done.12.same_ref = bf16[768,2048]{1,0:T(8,128)(2,1)} collective-permute-done((bf16[768,2048]{1,0:T(8,128)(2,1)}, bf16[768,2048]{1,0:T(8,128)(2,1)}, u32[]{:S(2)}, u32[]{:S(2)}) %collective-permute-start.12) | collective-permute-done | bytes 3145760 | tf_op jit(solution)/shard_map/ppermute | solution.py:387
  72.0 7.8 %collective-permute-done.9.refs_5_ = bf16[512,640]{1,0:T(8,128)(2,1)} collective-permute-done((bf16[512,640]{1,0:T(8,128)(2,1)}, bf16[512,640]{1,0:T(8,128)(2,1)}, u32[]{:S(2)}, u32[]{:S(2)}) %collective-permute-start.9) | collective-permute-done | bytes 655392 | tf_op jit(solution)/shard_map/ppermute | solution.py:386
  84.0 1.9 collective-permute-start.16
  87.6 2.1 %collective-permute-start.15 = (bf16[5,32,2048]{2,1,0:T(8,128)(2,1)}, bf16[5,32,2048]{2,1,0:T(8,128)(2,1)}, u32[]{:S(2)}, u32[]{:S(2)}) collective-permute-start(bf16[5,32,2048]{2,1,0:T(8,128)(2,1)} %copy-done.8), channel_id=1, source_target_pairs={{0,12},{2,6},{4,0},{6,10},{8,4},{10,14},{12,8},{14,2},{1,13},{3,7}... | collective-permute-start | bytes 1966088 | tf_op jit(solution)/shard_map/ppermute | solution.py:386
  91.9 4.6 %collective-permute-done.16.refs_7_ = bf16[256,640]{1,0:T(8,128)(2,1)} collective-permute-done((bf16[256,640]{1,0:T(8,128)(2,1)}, bf16[256,640]{1,0:T(8,128)(2,1)}, u32[]{:S(2)}, u32[]{:S(2)}) %collective-permute-start.16) | collective-permute-done | bytes 327712 | tf_op jit(solution)/shard_map/ppermute | solution.py:386
  99.2 10.2 %shard_map.76 = bf16[768,640]{1,0:T(8,128)(2,1)} custom-call(s32[10]{0:T(128)S(1)} %pad_add_fusion.1.at, bf16[768,2048]{1,0:T(8,128)(2,1)} %collective-permute-done.12.same_ref, bf16[768,2048]{1,0:T(8,128)(2,1)} %collective-permute-done.18.swapped_ref, bf16[512,640]{1,0:T(8,128)(2,1)S(1)} %constant_dynamic-slice_fusion.1.refs_0_, ...), custom_call_target="tpu_custom_call" | custom-call | flops 4026531840 | bytes 13500416 | tf_op jit(solution)/shard_map/pallas_call | solution.py:229
  110.8 4.4 %shard_map.77 = bf16[6,32,2048]{2,1,0:T(8,128)(2,1)} custom-call(s32[6]{0:T(128)S(1)} %compare_convert_fusion.which_ref, s32[6]{0:T(128)S(1)} %get-tuple-element.63.first_ref, s32[6]{0:T(128)S(1)} %compare_select_fusion.second_ref, bf16[8,64,2048]{2,1,0:T(8,128)(2,1)S(1)} %copy-done.4, bf16[5,32,2048]{2,1,0:T(8,128)(2,1)} %collective-permute-done.15.b_ref), custom_call_target="tpu_custom_call" | custom-call | bytes 2359296 | tf_op jit(solution)/shard_map/pallas_call | solution.py:130
  115.1 2.5 %collective-permute-start.24 = (bf16[6,32,2048]{2,1,0:T(8,128)(2,1)}, bf16[6,32,2048]{2,1,0:T(8,128)(2,1)}, u32[]{:S(2)}, u32[]{:S(2)}) collective-permute-start(bf16[6,32,2048]{2,1,0:T(8,128)(2,1)} %shard_map.77), channel_id=1, source_target_pairs={{0,2},{2,0},{4,6},{6,4},{8,10},{10,8},{12,14},{14,12},{1,3},{3,1},... | collective-permute-start | bytes 2359304 | tf_op jit(solution)/shard_map/ppermute | solution.py:386
  117.6 4.1 %collective-permute-done.14.refs_1_ = bf16[512,384]{1,0:T(8,128)(2,1)S(1)} collective-permute-done((bf16[512,384]{1,0:T(8,128)(2,1)S(1)}, bf16[512,384]{1,0:T(8,128)(2,1)S(1)}, u32[]{:S(2)}, u32[]{:S(2)}) %collective-permute-start.14) | collective-permute-done | bytes 393248 | tf_op jit(solution)/shard_map/ppermute | solution.py:386
  121.7 2.0 %collective-permute-start.25 = (bf16[512,384]{1,0:T(8,128)(2,1)S(1)}, bf16[512,384]{1,0:T(8,128)(2,1)S(1)}, u32[]{:S(2)}, u32[]{:S(2)}) collective-permute-start(bf16[512,384]{1,0:T(8,128)(2,1)S(1)} %collective-permute-done.13.refs_2_), channel_id=1, source_target_pairs={{4,0},{8,4},{12,8},{14,12},{10,14},{6,10},{2,6},{0,2},{5,1},{9,5},... | collective-permute-start | bytes 1179656 | tf_op jit(solution)/shard_map/ppermute | solution.py:386
  123.8 2.6 %collective-permute-start.23 = (bf16[5,32,2048]{2,1,0:T(8,128)(2,1)}, bf16[5,32,2048]{2,1,0:T(8,128)(2,1)S(1)}, u32[]{:S(2)}, u32[]{:S(2)}) collective-permute-start(bf16[5,32,2048]{2,1,0:T(8,128)(2,1)} %get-tuple-element.54), channel_id=1, source_target_pairs={{0,12},{2,6},{4,0},{6,10},{8,4},{10,14},{12,8},{14,2},{1,13},{3,7}... | collective-permute-start | bytes 1966088 | tf_op jit(solution)/shard_map/ppermute | solution.py:386
  126.3 10.2 %shard_map.78.refs_0_ = f32[768,640]{1,0:T(8,128)} custom-call(s32[10]{0:T(128)S(1)} %pad_add_fusion.1.at, bf16[768,2048]{1,0:T(8,128)(2,1)} %same_ref.1, bf16[768,2048]{1,0:T(8,128)(2,1)} %collective-permute-done.3.swapped_ref, bf16[512,640]{1,0:T(8,128)(2,1)S(1)} %constant_dynamic-slice_fusion.1.refs_0_, bf16[512,640]{1,0:T(8,128)(2,1)} %collective-permute-done.4.refs_1_, ...), custom_call_target="tpu_custom_call" | custom-call | flops 4026531840 | bytes 13500416 | tf_op jit(solution)/shard_map/pallas_call | solution.py:229
  136.5 5.1 %shard_map.79.la = f32[768,64]{1,0:T(8,128)S(1)} custom-call(s32[3,6]{1,0:T(4,128)S(1)} %pad_add_fusion.table_ref, bf16[768,2048]{1,0:T(8,128)(2,1)} %same_ref.1, bf16[8,64,2048]{2,1,0:T(8,128)(2,1)S(1)} %bitcast.25, bf16[6,32,2048]{2,1,0:T(8,128)(2,1)S(1)} %copy-done.6, bf16[6,32,2048]{2,1,0:T(8,128)(2,1)} %collective-permute-done.19.refs_1_), custom_call_target="tpu_custom_call" | custom-call | flops 201326592 | bytes 5242880 | tf_op jit(solution)/shard_map/pallas_call | solution.py:181
  141.6 5.2 %collective-permute-done.21.refs_3_ = bf16[512,384]{1,0:T(8,128)(2,1)S(1)} collective-permute-done((bf16[512,384]{1,0:T(8,128)(2,1)S(1)}, bf16[512,384]{1,0:T(8,128)(2,1)S(1)}, u32[]{:S(2)}, u32[]{:S(2)}) %collective-permute-start.21) | collective-permute-done | bytes 393248 | tf_op jit(solution)/shard_map/ppermute | solution.py:386
  150.1 7.6 %collective-permute-done.26.refs_6_ = bf16[512,384]{1,0:T(8,128)(2,1)S(1)} collective-permute-done((bf16[512,384]{1,0:T(8,128)(2,1)S(1)}, bf16[512,384]{1,0:T(8,128)(2,1)S(1)}, u32[]{:S(2)}, u32[]{:S(2)}) %collective-permute-start.26) | collective-permute-done | bytes 393248 | tf_op jit(solution)/shard_map/ppermute | solution.py:386
  161.4 6.2 %shard_map.81.partial_ref = f32[768,384]{1,0:T(8,128)S(1)} custom-call(s32[10]{0:T(128)S(1)} %pad_add_fusion.1.at, bf16[768,2048]{1,0:T(8,128)(2,1)} %collective-permute-done.12.same_ref, bf16[768,2048]{1,0:T(8,128)(2,1)} %collective-permute-done.18.swapped_ref, bf16[512,384]{1,0:T(8,128)(2,1)S(1)} %constant_dynamic-slice_fusion.2.refs_0_, ...), custom_call_target="tpu_custom_call" | custom-call | tf_op jit(solution)/shard_map/pallas_call | solution.py:229
  167.7 3.3 %shard_map.82 = bf16[768,384]{1,0:T(8,128)(2,1)S(1)} custom-call(s32[10]{0:T(128)S(1)} %pad_add_fusion.1.at, bf16[768,2048]{1,0:T(8,128)(2,1)} %collective-permute-done.12.same_ref, bf16[768,2048]{1,0:T(8,128)(2,1)} %collective-permute-done.18.swapped_ref, bf16[256,384]{1,0:T(8,128)(2,1)S(1)} %collective-permute-done.27.upper_ref.refs_7_, ...), custom_call_target="tpu_custom_call" | custom-call | flops 2415919104 | bytes 10616832 | tf_op jit(solution)/shard_map/pallas_call | solution.py:276
  172.0 6.5 %shard_map.83.refs_1_ = f32[768,384]{1,0:T(8,128)S(1)} custom-call(s32[10]{0:T(128)S(1)} %pad_add_fusion.1.at, bf16[768,2048]{1,0:T(8,128)(2,1)} %same_ref.1, bf16[768,2048]{1,0:T(8,128)(2,1)} %collective-permute-done.3.swapped_ref, bf16[512,384]{1,0:T(8,128)(2,1)S(1)} %constant_dynamic-slice_fusion.2.refs_0_, ...), custom_call_target="tpu_custom_call" | custom-call | flops 2415919104 | bytes 10616832 | tf_op jit(solution)/shard_map/pallas_call | solution.py:229
  178.5 2.7 %collective-permute-done.31.refs_6_ = bf16[6,32,2048]{2,1,0:T(8,128)(2,1)S(1)} collective-permute-done((bf16[6,32,2048]{2,1,0:T(8,128)(2,1)S(1)}, bf16[6,32,2048]{2,1,0:T(8,128)(2,1)S(1)}, u32[]{:S(2)}, u32[]{:S(2)}) %collective-permute-start.31) | collective-permute-done | bytes 786464 | tf_op jit(solution)/shard_map/ppermute | solution.py:386
  181.2 3.2 %collective-permute-done.30.refs_3_ = bf16[768,384]{1,0:T(8,128)(2,1)S(1)} collective-permute-done((bf16[768,384]{1,0:T(8,128)(2,1)S(1)}, bf16[768,384]{1,0:T(8,128)(2,1)S(1)}, u32[]{:S(2)}, u32[]{:S(2)}) %collective-permute-start.30) | collective-permute-done | bytes 589856 | tf_op jit(solution)/shard_map/ppermute | solution.py:387
  184.5 6.5 %shard_map.84 = bf16[768,2048]{1,0:T(8,128)(2,1)} custom-call(s32[3,6]{1,0:T(4,128)S(1)} %pad_add_fusion.table_ref, s32[6]{0:T(128)S(1)} %copy-done.7, s32[1]{0:T(128)} %bitcast.3.half_ref, f32[768,64]{1,0:T(8,128)S(1)} %shard_map.79.la, f32[768,64]{1,0:T(8,128)S(1)} %collective-permute-done.20.lb, f32[768,640]{1,0:T(8,128)} %shard_map.78.refs_0_, ...), custom_call_target="tpu_custom_call" | custom-call | flops 201326592 | bytes 9961472 | tf_op jit(solution)/shard_map/pallas_call | solution.py:341
  (91 shorter events, 30.4 us)
Async XLA Ops:
  0.0 25.8 %collective-permute-start.3 = (bf16[768,2048]{1,0:T(8,128)(2,1)}, bf16[768,2048]{1,0:T(8,128)(2,1)}, u32[]{:S(2)}, u32[]{:S(2)}) collective-permute-start(bf16[768,2048]{1,0:T(8,128)(2,1)} %same_ref.1), channel_id=1, source_target_pairs={{0,1},{1,0},{2,3},{3,2},{4,5},{5,4},{6,7},{7,6},{8,9},{9,8},{10,11... | collective-permute-start | bytes 9437192 | tf_op jit(solution)/shard_map/ppermute | solution.py:388
  0.5 71.6 %collective-permute-start.12 = (bf16[768,2048]{1,0:T(8,128)(2,1)}, bf16[768,2048]{1,0:T(8,128)(2,1)}, u32[]{:S(2)}, u32[]{:S(2)}) collective-permute-start(bf16[768,2048]{1,0:T(8,128)(2,1)} %same_ref.1), channel_id=1, source_target_pairs={{0,16},{16,0},{1,17},{17,1},{2,18},{18,2},{3,19},{19,3},{4,20},{20... | collective-permute-start | bytes 9437192 | tf_op jit(solution)/shard_map/ppermute | solution.py:387
  3.0 6.7 %collective-permute-start.1 = (s32[6]{0:T(128)}, s32[6]{0:T(128)S(1)}, u32[]{:S(2)}, u32[]{:S(2)}) collective-permute-start(s32[6]{0:T(128)} %param.11), channel_id=1, source_target_pairs={{0,14},{2,4},{4,2},{6,8},{8,6},{10,12},{12,10},{14,0},{1,15},{3,5}... | collective-permute-start | bytes 80 | tf_op jit(solution)/shard_map/ppermute | solution.py:386
  7.6 9.5 %collective-permute-start = (s32[6]{0:T(128)}, s32[6]{0:T(128)S(1)}, u32[]{:S(2)}, u32[]{:S(2)}) collective-permute-start(s32[6]{0:T(128)} %param.11), channel_id=1, source_target_pairs={{0,2},{2,0},{4,6},{6,4},{8,10},{10,8},{12,14},{14,12},{1,3},{3,1},... | collective-permute-start | bytes 80 | tf_op jit(solution)/shard_map/ppermute | solution.py:386
  7.7 17.8 %collective-permute-start.5 = (bf16[512,640]{1,0:T(8,128)(2,1)S(1)}, bf16[512,640]{1,0:T(8,128)(2,1)}, u32[]{:S(2)}, u32[]{:S(2)}) collective-permute-start(bf16[512,640]{1,0:T(8,128)(2,1)S(1)} %constant_dynamic-slice_fusion.1.refs_0_), channel_id=1, source_target_pairs={{4,0},{8,4},{12,8},{14,12},{10,14},{6,10},{2,6},{0,2},{5,1},{9,5},... | collective-permute-start | bytes 1966088 | tf_op jit(solution)/shard_map/ppermute | solution.py:386
  9.7 16.1 %collective-permute-start.4 = (bf16[512,640]{1,0:T(8,128)(2,1)S(1)}, bf16[512,640]{1,0:T(8,128)(2,1)}, u32[]{:S(2)}, u32[]{:S(2)}) collective-permute-start(bf16[512,640]{1,0:T(8,128)(2,1)S(1)} %constant_dynamic-slice_fusion.1.refs_0_), channel_id=1, source_target_pairs={{0,4},{4,8},{8,12},{12,14},{14,10},{10,6},{6,2},{2,0},{1,5},{5,9},... | collective-permute-start | bytes 1966088 | tf_op jit(solution)/shard_map/ppermute | solution.py:386
  17.1 22.3 %collective-permute-start.2 = (bf16[5,32,2048]{2,1,0:T(8,128)(2,1)}, bf16[5,32,2048]{2,1,0:T(8,128)(2,1)S(1)}, u32[]{:S(2)}, u32[]{:S(2)}) collective-permute-start(bf16[5,32,2048]{2,1,0:T(8,128)(2,1)} %get-tuple-element.33), channel_id=1, source_target_pairs={{0,12},{2,6},{4,0},{6,10},{8,4},{10,14},{12,8},{14,2},{1,13},{3,7}... | collective-permute-start | bytes 1966088 | tf_op jit(solution)/shard_map/ppermute | solution.py:386
  25.8 27.7 %collective-permute-start.8 = (bf16[512,640]{1,0:T(8,128)(2,1)}, bf16[512,640]{1,0:T(8,128)(2,1)}, u32[]{:S(2)}, u32[]{:S(2)}) collective-permute-start(bf16[512,640]{1,0:T(8,128)(2,1)} %collective-permute-done.4.refs_1_), channel_id=1, source_target_pairs={{0,4},{4,8},{8,12},{12,14},{14,10},{10,6},{6,2},{2,0},{1,5},{5,9},... | collective-permute-start | bytes 1966088 | tf_op jit(solution)/shard_map/ppermute | solution.py:386
  27.5 26.0 %collective-permute-start.10 = (bf16[512,640]{1,0:T(8,128)(2,1)}, bf16[512,640]{1,0:T(8,128)(2,1)}, u32[]{:S(2)}, u32[]{:S(2)}) collective-permute-start(bf16[512,640]{1,0:T(8,128)(2,1)} %collective-permute-done.5.refs_2_), channel_id=1, source_target_pairs={{4,0},{8,4},{12,8},{14,12},{10,14},{6,10},{2,6},{0,2},{5,1},{9,5},... | collective-permute-start | bytes 1966088 | tf_op jit(solution)/shard_map/ppermute | solution.py:386
  41.7 25.7 %collective-permute-start.6 = (bf16[6,32,2048]{2,1,0:T(8,128)(2,1)S(1)}, bf16[6,32,2048]{2,1,0:T(8,128)(2,1)S(1)}, u32[]{:S(2)}, u32[]{:S(2)}) collective-permute-start(bf16[6,32,2048]{2,1,0:T(8,128)(2,1)S(1)} %shard_map.74), channel_id=1, source_target_pairs={{0,2},{2,0},{4,6},{6,4},{8,10},{10,8},{12,14},{14,12},{1,3},{3,1},... | collective-permute-start | bytes 2359304 | tf_op jit(solution)/shard_map/ppermute | solution.py:386
  46.7 20.8 %collective-permute-start.7 = (bf16[5,32,2048]{2,1,0:T(8,128)(2,1)S(1)}, bf16[5,32,2048]{2,1,0:T(8,128)(2,1)S(1)}, u32[]{:S(2)}, u32[]{:S(2)}) collective-permute-start(bf16[5,32,2048]{2,1,0:T(8,128)(2,1)S(1)} %copy-done.10), channel_id=1, source_target_pairs={{0,12},{2,6},{4,0},{6,10},{8,4},{10,14},{12,8},{14,2},{1,13},{3,7}... | collective-permute-start | bytes 1966088 | tf_op jit(solution)/shard_map/ppermute | solution.py:386
  53.5 26.4 %collective-permute-start.9 = (bf16[512,640]{1,0:T(8,128)(2,1)}, bf16[512,640]{1,0:T(8,128)(2,1)}, u32[]{:S(2)}, u32[]{:S(2)}) collective-permute-start(bf16[512,640]{1,0:T(8,128)(2,1)} %collective-permute-done.8.refs_3_), channel_id=1, source_target_pairs={{0,4},{4,8},{8,12},{12,14},{14,10},{10,6},{6,2},{2,0},{1,5},{5,9},... | collective-permute-start | bytes 1966088 | tf_op jit(solution)/shard_map/ppermute | solution.py:386
  55.6 24.9 %collective-permute-start.11 = (bf16[512,640]{1,0:T(8,128)(2,1)}, bf16[512,640]{1,0:T(8,128)(2,1)}, u32[]{:S(2)}, u32[]{:S(2)}) collective-permute-start(bf16[512,640]{1,0:T(8,128)(2,1)} %collective-permute-done.10.refs_4_), channel_id=1, source_target_pairs={{4,0},{8,4},{12,8},{14,12},{10,14},{6,10},{2,6},{0,2},{5,1},{9,5},... | collective-permute-start | bytes 1966088 | tf_op jit(solution)/shard_map/ppermute | solution.py:386
  80.5 18.7 %collective-permute-start.18 = (bf16[768,2048]{1,0:T(8,128)(2,1)}, bf16[768,2048]{1,0:T(8,128)(2,1)}, u32[]{:S(2)}, u32[]{:S(2)}) collective-permute-start(bf16[768,2048]{1,0:T(8,128)(2,1)} %collective-permute-done.12.same_ref), channel_id=1, source_target_pairs={{0,1},{1,0},{2,3},{3,2},{4,5},{5,4},{6,7},{7,6},{8,9},{9,8},{10,11... | collective-permute-start | bytes 9437192 | tf_op jit(solution)/shard_map/ppermute | solution.py:388
  84.0 12.5 %collective-permute-start.16 = (bf16[256,640]{1,0:T(8,128)(2,1)}, bf16[256,640]{1,0:T(8,128)(2,1)}, u32[]{:S(2)}, u32[]{:S(2)}) collective-permute-start(bf16[256,640]{1,0:T(8,128)(2,1)} %slice.16), channel_id=1, source_target_pairs={{0,4},{4,8},{8,12},{12,14},{14,10},{10,6},{6,2},{2,0},{1,5},{5,9},... | collective-permute-start | bytes 983048 | tf_op jit(solution)/shard_map/ppermute | solution.py:386
  85.9 10.9 %collective-permute-start.17 = (bf16[256,640]{1,0:T(8,128)(2,1)}, bf16[256,640]{1,0:T(8,128)(2,1)}, u32[]{:S(2)}, u32[]{:S(2)}) collective-permute-start(bf16[256,640]{1,0:T(8,128)(2,1)} %slice.17), channel_id=1, source_target_pairs={{4,0},{8,4},{12,8},{14,12},{10,14},{6,10},{2,6},{0,2},{5,1},{9,5},... | collective-permute-start | bytes 983048 | tf_op jit(solution)/shard_map/ppermute | solution.py:386
  87.6 23.1 %collective-permute-start.15 = (bf16[5,32,2048]{2,1,0:T(8,128)(2,1)}, bf16[5,32,2048]{2,1,0:T(8,128)(2,1)}, u32[]{:S(2)}, u32[]{:S(2)}) collective-permute-start(bf16[5,32,2048]{2,1,0:T(8,128)(2,1)} %copy-done.8), channel_id=1, source_target_pairs={{0,12},{2,6},{4,0},{6,10},{8,4},{10,14},{12,8},{14,2},{1,13},{3,7}... | collective-permute-start | bytes 1966088 | tf_op jit(solution)/shard_map/ppermute | solution.py:386
  91.0 45.5 %collective-permute-start.19 = (bf16[6,32,2048]{2,1,0:T(8,128)(2,1)S(1)}, bf16[6,32,2048]{2,1,0:T(8,128)(2,1)}, u32[]{:S(2)}, u32[]{:S(2)}) collective-permute-start(bf16[6,32,2048]{2,1,0:T(8,128)(2,1)S(1)} %shard_map.75), channel_id=1, source_target_pairs={{0,2},{2,0},{4,6},{6,4},{8,10},{10,8},{12,14},{14,12},{1,3},{3,1},... | collective-permute-start | bytes 2359304 | tf_op jit(solution)/shard_map/ppermute | solution.py:386
  96.5 25.2 %collective-permute-start.14 = (bf16[512,384]{1,0:T(8,128)(2,1)S(1)}, bf16[512,384]{1,0:T(8,128)(2,1)S(1)}, u32[]{:S(2)}, u32[]{:S(2)}) collective-permute-start(bf16[512,384]{1,0:T(8,128)(2,1)S(1)} %constant_dynamic-slice_fusion.2.refs_0_), channel_id=1, source_target_pairs={{0,4},{4,8},{8,12},{12,14},{14,10},{10,6},{6,2},{2,0},{1,5},{5,9},... | collective-permute-start | bytes 1179656 | tf_op jit(solution)/shard_map/ppermute | solution.py:386
  96.7 25.0 %collective-permute-start.13 = (bf16[512,384]{1,0:T(8,128)(2,1)S(1)}, bf16[512,384]{1,0:T(8,128)(2,1)S(1)}, u32[]{:S(2)}, u32[]{:S(2)}) collective-permute-start(bf16[512,384]{1,0:T(8,128)(2,1)S(1)} %constant_dynamic-slice_fusion.2.refs_0_), channel_id=1, source_target_pairs={{4,0},{8,4},{12,8},{14,12},{10,14},{6,10},{2,6},{0,2},{5,1},{9,5},... | collective-permute-start | bytes 1179656 | tf_op jit(solution)/shard_map/ppermute | solution.py:386
  115.1 43.9 %collective-permute-start.24 = (bf16[6,32,2048]{2,1,0:T(8,128)(2,1)}, bf16[6,32,2048]{2,1,0:T(8,128)(2,1)}, u32[]{:S(2)}, u32[]{:S(2)}) collective-permute-start(bf16[6,32,2048]{2,1,0:T(8,128)(2,1)} %shard_map.77), channel_id=1, source_target_pairs={{0,2},{2,0},{4,6},{6,4},{8,10},{10,8},{12,14},{14,12},{1,3},{3,1},... | collective-permute-start | bytes 2359304 | tf_op jit(solution)/shard_map/ppermute | solution.py:386
  121.7 25.1 %collective-permute-start.21 = (bf16[512,384]{1,0:T(8,128)(2,1)S(1)}, bf16[512,384]{1,0:T(8,128)(2,1)S(1)}, u32[]{:S(2)}, u32[]{:S(2)}) collective-permute-start(bf16[512,384]{1,0:T(8,128)(2,1)S(1)} %collective-permute-done.14.refs_1_), channel_id=1, source_target_pairs={{0,4},{4,8},{8,12},{12,14},{14,10},{10,6},{6,2},{2,0},{1,5},{5,9},... | collective-permute-start | bytes 1179656 | tf_op jit(solution)/shard_map/ppermute | solution.py:386
  121.7 25.0 %collective-permute-start.25 = (bf16[512,384]{1,0:T(8,128)(2,1)S(1)}, bf16[512,384]{1,0:T(8,128)(2,1)S(1)}, u32[]{:S(2)}, u32[]{:S(2)}) collective-permute-start(bf16[512,384]{1,0:T(8,128)(2,1)S(1)} %collective-permute-done.13.refs_2_), channel_id=1, source_target_pairs={{4,0},{8,4},{12,8},{14,12},{10,14},{6,10},{2,6},{0,2},{5,1},{9,5},... | collective-permute-start | bytes 1179656 | tf_op jit(solution)/shard_map/ppermute | solution.py:386
  123.8 25.6 %collective-permute-start.23 = (bf16[5,32,2048]{2,1,0:T(8,128)(2,1)}, bf16[5,32,2048]{2,1,0:T(8,128)(2,1)S(1)}, u32[]{:S(2)}, u32[]{:S(2)}) collective-permute-start(bf16[5,32,2048]{2,1,0:T(8,128)(2,1)} %get-tuple-element.54), channel_id=1, source_target_pairs={{0,12},{2,6},{4,0},{6,10},{8,4},{10,14},{12,8},{14,2},{1,13},{3,7}... | collective-permute-start | bytes 1966088 | tf_op jit(solution)/shard_map/ppermute | solution.py:386
  146.8 10.9 %collective-permute-start.26 = (bf16[512,384]{1,0:T(8,128)(2,1)S(1)}, bf16[512,384]{1,0:T(8,128)(2,1)S(1)}, u32[]{:S(2)}, u32[]{:S(2)}) collective-permute-start(bf16[512,384]{1,0:T(8,128)(2,1)S(1)} %collective-permute-done.25.refs_4_), channel_id=1, source_target_pairs={{4,0},{8,4},{12,8},{14,12},{10,14},{6,10},{2,6},{0,2},{5,1},{9,5},... | collective-permute-start | bytes 1179656 | tf_op jit(solution)/shard_map/ppermute | solution.py:386
  148.5 10.5 %collective-permute-start.22 = (bf16[512,384]{1,0:T(8,128)(2,1)S(1)}, bf16[512,384]{1,0:T(8,128)(2,1)S(1)}, u32[]{:S(2)}, u32[]{:S(2)}) collective-permute-start(bf16[512,384]{1,0:T(8,128)(2,1)S(1)} %collective-permute-done.21.refs_3_), channel_id=1, source_target_pairs={{0,4},{4,8},{8,12},{12,14},{14,10},{10,6},{6,2},{2,0},{1,5},{5,9},... | collective-permute-start | bytes 1179656 | tf_op jit(solution)/shard_map/ppermute | solution.py:386
  148.8 23.2 %collective-permute-start.29 = (bf16[768,640]{1,0:T(8,128)(2,1)S(1)}, bf16[768,640]{1,0:T(8,128)(2,1)S(1)}, u32[]{:S(2)}, u32[]{:S(2)}) collective-permute-start(bf16[768,640]{1,0:T(8,128)(2,1)S(1)} %copy-done.12), channel_id=1, source_target_pairs={{0,16},{16,0},{1,17},{17,1},{2,18},{18,2},{3,19},{19,3},{4,20},{20... | collective-permute-start | bytes 2949128 | tf_op jit(solution)/shard_map/ppermute | solution.py:387
  159.0 8.6 %collective-permute-start.27 = (bf16[256,384]{1,0:T(8,128)(2,1)S(1)}, bf16[256,384]{1,0:T(8,128)(2,1)S(1)}, u32[]{:S(2)}, u32[]{:S(2)}) collective-permute-start(bf16[256,384]{1,0:T(8,128)(2,1)S(1)} %slice.18), channel_id=1, source_target_pairs={{0,4},{4,8},{8,12},{12,14},{14,10},{10,6},{6,2},{2,0},{1,5},{5,9},... | collective-permute-start | bytes 589832 | tf_op jit(solution)/shard_map/ppermute | solution.py:386
  159.5 8.1 %collective-permute-start.28 = (bf16[256,384]{1,0:T(8,128)(2,1)S(1)}, bf16[256,384]{1,0:T(8,128)(2,1)S(1)}, u32[]{:S(2)}, u32[]{:S(2)}) collective-permute-start(bf16[256,384]{1,0:T(8,128)(2,1)S(1)} %slice.19), channel_id=1, source_target_pairs={{4,0},{8,4},{12,8},{14,12},{10,14},{6,10},{2,6},{0,2},{5,1},{9,5},... | collective-permute-start | bytes 589832 | tf_op jit(solution)/shard_map/ppermute | solution.py:386
  161.1 20.2 %collective-permute-start.31 = (bf16[6,32,2048]{2,1,0:T(8,128)(2,1)S(1)}, bf16[6,32,2048]{2,1,0:T(8,128)(2,1)S(1)}, u32[]{:S(2)}, u32[]{:S(2)}) collective-permute-start(bf16[6,32,2048]{2,1,0:T(8,128)(2,1)S(1)} %shard_map.80), channel_id=1, source_target_pairs={{0,2},{2,0},{4,6},{6,4},{8,10},{10,8},{12,14},{14,12},{1,3},{3,1},... | collective-permute-start | bytes 2359304 | tf_op jit(solution)/shard_map/ppermute | solution.py:386
  171.0 13.5 %collective-permute-start.30 = (bf16[768,384]{1,0:T(8,128)(2,1)S(1)}, bf16[768,384]{1,0:T(8,128)(2,1)S(1)}, u32[]{:S(2)}, u32[]{:S(2)}) collective-permute-start(bf16[768,384]{1,0:T(8,128)(2,1)S(1)} %shard_map.82), channel_id=1, source_target_pairs={{0,16},{16,0},{1,17},{17,1},{2,18},{18,2},{3,19},{19,3},{4,20},{20... | collective-permute-start | bytes 1769480 | tf_op jit(solution)/shard_map/ppermute | solution.py:387
  171.6 6.9 %collective-permute-start.20 = (f32[768,64]{1,0:T(8,128)S(1)}, f32[768,64]{1,0:T(8,128)S(1)}, u32[]{:S(2)}, u32[]{:S(2)}) collective-permute-start(f32[768,64]{1,0:T(8,128)S(1)} %shard_map.79.la), channel_id=1, source_target_pairs={{0,1},{1,0},{2,3},{3,2},{4,5},{5,4},{6,7},{7,6},{8,9},{9,8},{10,11... | collective-permute-start | bytes 589832 | tf_op jit(solution)/shard_map/ppermute | solution.py:388
  (13 other events, 124.9 us)
